TPU v7x, 256 devices: a whole 4x4x8 slice. The times are simulated.
256 devices in a mesh: pipe: 4 (over y), row: 16 (over z, core), col: 4 (over x).
Axes of the slice: x: 4, y: 4, z: 8, core: 2. Of those that a mesh axis runs over, the one named last changes fastest.
Arguments:
- activations: bfloat16 [4, 128, 64, 512], P('pipe', 'row', 'col'), may hold values from -6 to 6
- qkv_weight: bfloat16 [4, 512, 1536], P('pipe'), may hold values from -9 to 9
- out_weight: bfloat16 [4, 512, 512], P('pipe'), may hold values from -0.25 to 0.25
- cotangent: float32 [128, 64, 512], P('row', 'col'), may hold values from -6 to 6
Outputs:
- input_grads: float32 [4, 128, 64, 512], P('pipe', 'row', 'col')
- qkv_grads: float32 [4, 512, 1536], P('pipe', ('row', 'col'))
- out_grads: float32 [4, 512, 512], P('pipe', ('row', 'col'))
All inputs are finite; a program needn't handle non-finite values.
Results may differ from a plain program's by a relative error of at most 0.015.
Values may be sent and summed in bfloat16 or wider, within the bound.
No kernel may reach another device: no remote copies, remote signals or barrier semaphores. Data moves between devices by JAX's collectives and lax.ppermute only.
A program may use at most 128 MiB of HBM per device.

v0:
```python
import jax
import jax.numpy as jnp
from jax import lax
from jax.sharding import PartitionSpec as P

H = 8


def padded_2(block, sides, width):
    for axis, dim in sides:
        count = lax.axis_size(axis)
        forward = [(i, i + 1) for i in range(count - 1)]
        backward = [(target, source) for source, target in forward]
        low = lax.ppermute(
            lax.slice_in_dim(block, block.shape[dim] - width, None, axis=dim), axis, forward
        )
        high = lax.ppermute(lax.slice_in_dim(block, 0, width, axis=dim), axis, backward)
        block = jnp.concatenate([low, block, high], axis=dim)
    return block


def shifted(block, axis, distance):
    devices = range(lax.axis_size(axis))
    route = [(i - distance, i) for i in devices if i - distance in devices]
    return lax.ppermute(block, axis, route)


def product(form, left, right):
    return jnp.einsum(form, left, right, preferred_element_type=jnp.float32)


def split_tiles(source, head_count):
    height, breadth, features = source.shape
    head_size = features // head_count
    shaped = source.reshape(height // 8, 8, breadth // 16, 16, head_count, head_size)
    return shaped.transpose(0, 2, 4, 1, 3, 5).reshape(
        height // 8, breadth // 16, head_count, 128, head_size
    )


def join_tiles(tiled_array, height, breadth):
    head_count = tiled_array.shape[2]
    head_size = tiled_array.shape[4]
    shaped = tiled_array.reshape(height // 8, breadth // 16, head_count, 8, 16, head_size)
    return shaped.transpose(0, 3, 1, 4, 2, 5).reshape(height, breadth, head_count * head_size)


def split_stats(stats):
    height, breadth, head_count = stats.shape
    shaped = stats.reshape(height // 8, 8, breadth // 16, 16, head_count)
    return shaped.transpose(0, 2, 4, 1, 3).reshape(height // 8, breadth // 16, head_count, 128)


def join_stats(tiled_array, height, breadth):
    head_count = tiled_array.shape[2]
    shaped = tiled_array.reshape(height // 8, breadth // 16, head_count, 8, 16)
    return shaped.transpose(0, 3, 1, 4, 2).reshape(height, breadth, head_count)


def regions(padded):
    height, breadth, features = padded.shape
    row_tiles = (height - 16) // 8
    col_tiles = (breadth - 16) // 16
    blocks = padded.reshape(row_tiles + 2, 8, breadth, features)
    stacked = jnp.concatenate([blocks[:row_tiles], blocks[1 : row_tiles + 1], blocks[2:]], axis=1)
    strips = stacked.reshape(row_tiles, 24, col_tiles + 1, 16, features)
    spread = jnp.concatenate([strips[:, :, :col_tiles], strips[:, :, 1:]], axis=3)
    return spread.transpose(0, 2, 1, 3, 4).reshape(row_tiles, col_tiles, 768, features)


def window_mask(row_tiles, col_tiles, row_start, col_start, row_total, col_total, keys_inside):
    inside = jnp.arange(128, dtype=jnp.int32)
    region_pos = jnp.arange(768, dtype=jnp.int32)
    tile_row = inside // 16
    tile_col = inside % 16
    region_row = region_pos // 32 - 8
    region_col = region_pos % 32 - 8
    if keys_inside:
        step_row = tile_row[:, None] - region_row[None, :]
        step_col = tile_col[:, None] - region_col[None, :]
    else:
        step_row = region_row[None, :] - tile_row[:, None]
        step_col = region_col[None, :] - tile_col[:, None]
    within = (step_row >= -8) & (step_row <= 7) & (step_col >= -8) & (step_col <= 7)
    base_row = row_start + 8 * jnp.arange(row_tiles, dtype=jnp.int32)
    base_col = col_start + 16 * jnp.arange(col_tiles, dtype=jnp.int32)
    grid_row = base_row[:, None] + region_row[None, :]
    grid_col = base_col[:, None] + region_col[None, :]
    row_valid = (grid_row >= 0) & (grid_row < row_total)
    col_valid = (grid_col >= 0) & (grid_col < col_total)
    return (
        within[None, None, None]
        & row_valid[:, None, None, None, :]
        & col_valid[None, :, None, None, :]
    )


def attend(queries, key_value_rim, query_mask, head_count):
    height, breadth, features = queries.shape
    head_size = features // head_count
    scaling = head_size ** (-0.5)
    tile_query = split_tiles(queries, head_count)
    row_tiles, col_tiles = (tile_query.shape[0], tile_query.shape[1])
    region_all = regions(key_value_rim)
    key_part = region_all[..., :features].reshape(row_tiles, col_tiles, 768, head_count, head_size)
    value_part = region_all[..., features:].reshape(
        row_tiles, col_tiles, 768, head_count, head_size
    )
    scores = product("abhqe,abkhe->abhqk", tile_query, key_part) * scaling
    scores = jnp.where(query_mask, scores, -1e30)
    highest = jnp.max(scores, axis=-1, keepdims=True)
    summed = jnp.sum(jnp.where(query_mask, jnp.exp(scores - highest), 0.0), axis=-1, keepdims=True)
    log_total = highest + jnp.log(summed)
    full_weights = jnp.where(query_mask, jnp.exp(scores - log_total), 0.0)
    mixed = product("abhqk,abkhe->abhqe", full_weights.astype(jnp.bfloat16), value_part).astype(
        jnp.bfloat16
    )
    return (
        join_tiles(mixed, height, breadth),
        join_stats(log_total[..., 0], height, breadth),
        full_weights,
        key_part,
        value_part,
    )


def body(activations, qkv_weight, out_weight, cotangent):
    source = activations[0]
    weight_in = qkv_weight[0]
    weight_back = out_weight[0]
    height, breadth, features = source.shape
    head_count = H
    head_size = features // head_count
    scaling_head = head_size ** (-0.5)
    row_tiles, col_tiles = (height // 8, breadth // 16)
    row_total = height * lax.axis_size("row")
    col_total = breadth * lax.axis_size("col")
    row_start = lax.axis_index("row") * height
    col_start = lax.axis_index("col") * breadth
    query_mask = window_mask(
        row_tiles, col_tiles, row_start, col_start, row_total, col_total, False
    )
    key_mask = window_mask(row_tiles, col_tiles, row_start, col_start, row_total, col_total, True)
    floated = source.astype(jnp.float32)
    inverse = lax.rsqrt(jnp.mean(floated * floated, axis=-1, keepdims=True) + 1e-06)
    normed = floated * inverse
    normed_low = normed.astype(jnp.bfloat16)
    normed_rows = normed_low.reshape(-1, features)
    projected = (
        jnp.dot(normed_rows, weight_in, preferred_element_type=jnp.float32)
        .astype(jnp.bfloat16)
        .reshape(height, breadth, 3 * features)
    )
    padded = padded_2(projected, (("row", 0), ("col", 1)), 8)
    mixed, log_total, query_weights, key_region, value_region = attend(
        projected[:, :, :features], padded[:, :, features:], query_mask, head_count
    )
    mixed_rows = mixed.reshape(-1, features)
    tile_key = split_tiles(projected[:, :, features : 2 * features], head_count)
    tile_value = split_tiles(projected[:, :, 2 * features :], head_count)
    reach_query = regions(padded[:, :, :features]).reshape(
        row_tiles, col_tiles, 768, head_count, head_size
    )
    key_scores = product("abhke,abqhe->abhkq", tile_key, reach_query) * scaling_head
    segment_now = lax.axis_index("pipe")
    segment_total = lax.axis_size("pipe")
    gradient = cotangent
    input_sum = jnp.zeros((height, breadth, features), jnp.float32)
    qkv_sum = jnp.zeros((features, 3 * features), jnp.float32)
    out_sum = jnp.zeros((features, features), jnp.float32)
    d_input = input_sum
    for turn_index in range(segment_total):
        if turn_index > 0:
            gradient = shifted(d_input.astype(jnp.bfloat16), "pipe", -1).astype(d_input.dtype)
        grad_low = gradient.astype(jnp.bfloat16)
        d_mixed = (
            jnp.dot(
                grad_low.reshape(-1, features), weight_back.T, preferred_element_type=jnp.float32
            )
            .astype(jnp.bfloat16)
            .reshape(height, breadth, features)
        )
        row_delta = jnp.sum(
            (d_mixed.astype(jnp.float32) * mixed.astype(jnp.float32)).reshape(
                height, breadth, head_count, -1
            ),
            axis=-1,
        )
        grad_rim = padded_2(d_mixed, (("row", 0), ("col", 1)), 8)
        stat_rim = padded_2(
            jnp.concatenate([log_total, row_delta], axis=-1), (("row", 0), ("col", 1)), 8
        )
        active = segment_now == segment_total - 1 - turn_index

        def working(operand):
            tile_grad = split_tiles(d_mixed, head_count)
            query_pressure = product("abhqe,abkhe->abhqk", tile_grad, value_region)
            query_slopes = (
                query_weights * (query_pressure - split_stats(row_delta)[..., None])
            ).astype(jnp.bfloat16)
            d_query = join_tiles(
                scaling_head * product("abhqk,abkhe->abhqe", query_slopes, key_region),
                height,
                breadth,
            )
            reach_grad = regions(grad_rim).reshape(row_tiles, col_tiles, 768, head_count, head_size)
            reach_stats = regions(stat_rim).transpose(0, 1, 3, 2)
            reach_total = reach_stats[:, :, :head_count][:, :, :, None, :]
            reach_delta = reach_stats[:, :, head_count:][:, :, :, None, :]
            key_weights = jnp.where(key_mask, jnp.exp(key_scores - reach_total), 0.0)
            key_pressure = product("abhke,abqhe->abhkq", tile_value, reach_grad)
            key_slopes = (key_weights * (key_pressure - reach_delta)).astype(jnp.bfloat16)
            d_value = join_tiles(
                product("abhkq,abqhe->abhke", key_weights.astype(jnp.bfloat16), reach_grad),
                height,
                breadth,
            )
            d_key = join_tiles(
                scaling_head * product("abhkq,abqhe->abhke", key_slopes, reach_query),
                height,
                breadth,
            )
            d_projected = jnp.concatenate([d_query, d_key, d_value], axis=-1).astype(jnp.bfloat16)
            d_normed = jnp.dot(
                d_projected.reshape(-1, 3 * features),
                weight_in.T,
                preferred_element_type=jnp.float32,
            ).reshape(height, breadth, features)
            inner = jnp.mean(d_normed * normed, axis=-1, keepdims=True)
            new_input = gradient + inverse * (d_normed - normed * inner)
            qkv_part = jnp.dot(
                normed_rows.T,
                d_projected.reshape(-1, 3 * features),
                preferred_element_type=jnp.float32,
            )
            out_part = jnp.dot(
                mixed_rows.T, grad_low.reshape(-1, features), preferred_element_type=jnp.float32
            )
            return (new_input, qkv_part, out_part)

        def resting(operand):
            return (jnp.zeros_like(input_sum), jnp.zeros_like(qkv_sum), jnp.zeros_like(out_sum))

        results = lax.cond(active, working, resting, 0)
        d_input = results[0]
        input_sum = input_sum + d_input
        qkv_sum = qkv_sum + results[1]
        out_sum = out_sum + results[2]
    qkv_part, out_part = (
        lax.psum_scatter(qkv_sum, ("row", "col"), scatter_dimension=0, tiled=True),
        lax.psum_scatter(out_sum, ("row", "col"), scatter_dimension=0, tiled=True),
    )
    scaling = (row_total * col_total) ** (-0.5)
    return (input_sum[None], (qkv_part * scaling)[None], (out_part * scaling)[None])


def solution(mesh):
    return jax.shard_map(
        body,
        mesh=mesh,
        in_specs=(
            P("pipe", "row", "col", None),
            P("pipe", None, None),
            P("pipe", None, None),
            P("row", "col", None),
        ),
        out_specs=(
            P("pipe", "row", "col", None),
            P("pipe", ("row", "col"), None),
            P("pipe", ("row", "col"), None),
        ),
        check_vma=False,
    )
```

profile of v0, /device:TPU:6, one launch (start us, length us, event | category | flops | bytes accessed | tf_op | source)
XLA Modules:
  0.0 840.2 jit_solution(3185187428599817433)
XLA Ops:
  18.1 4.1 collective-permute-start
  30.3 4.6 collective-permute-start.3
  36.3 4.6 collective-permute-start.11
  41.1 9.5 %collective-permute-done.10 = bf16[24,8,512]{2,1,0:T(8,128)(2,1)S(1)} collective-permute-done((bf16[24,8,512]{2,1,0:T(8,128)(2,1)S(1)}, bf16[24,8,512]{2,1,0:T(8,128)(2,1)S(1)}, u32[]{:S(2)}, u32[]{:S(2)}) %collective-permute-start.10) | collective-permute-done | bytes 196640 | tf_op jit(solution)/shard_map/ppermute | solution.py:14
  62.0 4.2 fusion.208
  85.5 5.7 collective-permute-start.7
  102.0 4.1 conditional.4
  108.4 6.9 collective-permute-done.12
  134.5 5.2 collective-permute-start.20
  141.8 5.2 collective-permute-start.16
  155.8 13.3 %conditional.5 = (f32[8,16,512]{2,1,0:T(8,128)}, f32[512,512]{1,0:T(8,128)}, f32[512,1536]{1,0:T(8,128)}) conditional(s32[]{:T(128)} %convert_element_type.190, () %tuple.42, (f32[8,16,1]{1,0,2:T(8,128)S(1)}, bf16[128,512]{1,0:T(8,128)(2,1)}, bf16[1,1,768,8,64]{2,4,3,1,0:T(8,128)(2,1)}, f32[8,16,8]{1,0,2:T(8,128)S(1)}, ...), branch_computations={%region_8.9_spmd, %region_9.11_spmd} | conditional | flops 987181056 | bytes 53549732 | solution.py:244
  171.4 6.4 collective-permute-done.21
  196.8 5.7 collective-permute-start.29
  204.6 5.2 collective-permute-start.25
  218.3 4.2 conditional.6
  224.8 215.8 %collective-permute-done.30 = bf16[8,16,512]{2,1,0:T(8,128)(2,1)S(1)} collective-permute-done((bf16[8,16,512]{2,1,0:T(8,128)(2,1)S(1)}, bf16[8,16,512]{2,1,0:T(8,128)(2,1)S(1)}, u32[]{:S(2)}, u32[]{:S(2)}) %collective-permute-start.30) | collective-permute-done | bytes 131104 | tf_op jit(solution)/shard_map/ppermute | solution.py:25
  459.8 5.7 collective-permute-start.38
  467.6 5.2 collective-permute-start.34
  481.4 52.6 %conditional.7 = (f32[8,16,512]{2,1,0:T(8,128)S(1)}, f32[512,512]{1,0:T(8,128)S(1)}, f32[512,1536]{1,0:T(8,128)}) conditional(s32[]{:T(128)} %convert_element_type.202, () %tuple.46, (f32[8,16,1]{1,0,2:T(8,128)S(1)}, bf16[128,512]{1,0:T(8,128)(2,1)}, bf16[1,1,768,8,64]{2,4,3,1,0:T(8,128)(2,1)}, f32[8,16,8]{1,0,2:T(8,128)S(1)}, ...), branch_computations={%region_16.17_spmd, %region_17.19_spmd} | conditional | flops 987181056 | bytes 74308456 | solution.py:244
  510.7 4.0 copy.286
  514.7 4.9 fusion.177
  537.4 7.7 add_add_fusion
  547.0 140.0 %reduce-scatter.5.cloned.1.call-done = f32[8,512]{1,0:T(8,128)} async-done(((f32[512,512]{1,0:T(8,128)}), f32[8,512]{1,0:T(8,128)}) %reduce-scatter.5.cloned.1.call-update) | async-done | bytes 16400 | tf_op jit(solution)/shard_map/reduce_scatter | solution.py:251
  688.4 143.4 %reduce-scatter.3.cloned.1.call-done = f32[8,1536]{1,0:T(8,128)} async-done(((f32[512,1536]{1,0:T(8,128)}), f32[8,1536]{1,0:T(8,128)}) %reduce-scatter.3.cloned.1.call-update) | async-done | bytes 49168 | tf_op jit(solution)/shard_map/reduce_scatter | solution.py:250
  (276 shorter events, 221.0 us)
Async XLA Ops:
  7.2 679.8 %reduce-scatter.5.cloned.1.call-start = ((), (), s32[]{:S(2)}) async-start(), calls=%async_computation.3 | async-start | bytes 1064960 | tf_op jit(solution)/shard_map/reduce_scatter | solution.py:251
  8.6 19.5 %collective-permute-start.9 = (bf16[8,16,512]{2,1,0:T(8,128)(2,1)S(1)}, bf16[8,16,512]{2,1,0:T(8,128)(2,1)S(1)}, u32[]{:S(2)}, u32[]{:S(2)}) collective-permute-start(bf16[8,16,512]{2,1,0:T(8,128)(2,1)S(1)} %bitcast.688), channel_id=1, source_target_pairs={{4,0},{8,4},{12,8},{16,12},{20,16},{24,20},{28,24},{32,28},{36,32}... | collective-permute-start | bytes 393224 | tf_op jit(solution)/shard_map/ppermute | solution.py:17
  9.9 18.2 %collective-permute-start.8 = (bf16[8,16,512]{2,1,0:T(8,128)(2,1)S(1)}, bf16[8,16,512]{2,1,0:T(8,128)(2,1)S(1)}, u32[]{:S(2)}, u32[]{:S(2)}) collective-permute-start(bf16[8,16,512]{2,1,0:T(8,128)(2,1)S(1)} %bitcast.689), channel_id=1, source_target_pairs={{0,4},{4,8},{8,12},{12,16},{16,20},{20,24},{24,28},{28,32},{32,36}... | collective-permute-start | bytes 393224 | tf_op jit(solution)/shard_map/ppermute | solution.py:14
  16.8 11.5 %collective-permute-start.1 = (bf16[8,16,1536]{2,1,0:T(8,128)(2,1)S(1)}, bf16[8,16,1536]{2,1,0:T(8,128)(2,1)S(1)}, u32[]{:S(2)}, u32[]{:S(2)}) collective-permute-start(bf16[8,16,1536]{2,1,0:T(8,128)(2,1)S(1)} %bitcast.664), channel_id=1, source_target_pairs={{4,0},{8,4},{12,8},{16,12},{20,16},{24,20},{28,24},{32,28},{36,32}... | collective-permute-start | bytes 1179656 | tf_op jit(solution)/shard_map/ppermute | solution.py:17
  29.0 24.4 %collective-permute-start.2 = (bf16[24,8,1536]{2,1,0:T(8,128)(2,1)S(1)}, bf16[24,8,1536]{2,1,0:T(8,128)(2,1)S(1)}, u32[]{:S(2)}, u32[]{:S(2)}) collective-permute-start(bf16[24,8,1536]{2,1,0:T(8,128)(2,1)S(1)} %get-tuple-element.529), channel_id=1, source_target_pairs={{0,1},{1,2},{2,3},{4,5},{5,6},{6,7},{8,9},{9,10},{10,11},{12,13},{... | collective-permute-start | bytes 1769480 | tf_op jit(solution)/shard_map/ppermute | solution.py:14
  30.3 23.1 %collective-permute-start.3 = (bf16[24,8,1536]{2,1,0:T(8,128)(2,1)S(1)}, bf16[24,8,1536]{2,1,0:T(8,128)(2,1)S(1)}, u32[]{:S(2)}, u32[]{:S(2)}) collective-permute-start(bf16[24,8,1536]{2,1,0:T(8,128)(2,1)S(1)} %get-tuple-element.530), channel_id=1, source_target_pairs={{1,0},{2,1},{3,2},{5,4},{6,5},{7,6},{9,8},{10,9},{11,10},{13,12},{... | collective-permute-start | bytes 1769480 | tf_op jit(solution)/shard_map/ppermute | solution.py:17
  35.0 15.7 %collective-permute-start.10 = (bf16[24,8,512]{2,1,0:T(8,128)(2,1)S(1)}, bf16[24,8,512]{2,1,0:T(8,128)(2,1)S(1)}, u32[]{:S(2)}, u32[]{:S(2)}) collective-permute-start(bf16[24,8,512]{2,1,0:T(8,128)(2,1)S(1)} %get-tuple-element.542), channel_id=1, source_target_pairs={{0,1},{1,2},{2,3},{4,5},{5,6},{6,7},{8,9},{9,10},{10,11},{12,13},{... | collective-permute-start | bytes 589832 | tf_op jit(solution)/shard_map/ppermute | solution.py:14
  36.3 16.2 %collective-permute-start.11 = (bf16[24,8,512]{2,1,0:T(8,128)(2,1)S(1)}, bf16[24,8,512]{2,1,0:T(8,128)(2,1)S(1)}, u32[]{:S(2)}, u32[]{:S(2)}) collective-permute-start(bf16[24,8,512]{2,1,0:T(8,128)(2,1)S(1)} %get-tuple-element.543), channel_id=1, source_target_pairs={{1,0},{2,1},{3,2},{5,4},{6,5},{7,6},{9,8},{10,9},{11,10},{13,12},{... | collective-permute-start | bytes 589832 | tf_op jit(solution)/shard_map/ppermute | solution.py:17
  84.3 15.9 %collective-permute-start.6 = (f32[24,8,16]{1,0,2:T(8,128)}, f32[24,8,16]{1,0,2:T(8,128)}, u32[]{:S(2)}, u32[]{:S(2)}) collective-permute-start(f32[24,8,16]{1,0,2:T(8,128)} %get-tuple-element.550), channel_id=1, source_target_pairs={{0,1},{1,2},{2,3},{4,5},{5,6},{6,7},{8,9},{9,10},{10,11},{12,13},{... | collective-permute-start | bytes 36872 | tf_op jit(solution)/shard_map/ppermute | solution.py:14
  85.5 14.6 %collective-permute-start.7 = (f32[24,8,16]{1,0,2:T(8,128)}, f32[24,8,16]{1,0,2:T(8,128)}, u32[]{:S(2)}, u32[]{:S(2)}) collective-permute-start(f32[24,8,16]{1,0,2:T(8,128)} %get-tuple-element.551), channel_id=1, source_target_pairs={{1,0},{2,1},{3,2},{5,4},{6,5},{7,6},{9,8},{10,9},{11,10},{13,12},{... | collective-permute-start | bytes 36872 | tf_op jit(solution)/shard_map/ppermute | solution.py:17
  117.0 13.7 %collective-permute-start.18 = (bf16[8,16,512]{2,1,0:T(8,128)(2,1)}, bf16[8,16,512]{2,1,0:T(8,128)(2,1)}, u32[]{:S(2)}, u32[]{:S(2)}) collective-permute-start(bf16[8,16,512]{2,1,0:T(8,128)(2,1)} %bitcast.173), channel_id=1, source_target_pairs={{4,0},{8,4},{12,8},{16,12},{20,16},{24,20},{28,24},{32,28},{36,32}... | collective-permute-start | bytes 393224 | tf_op jit(solution)/shard_map/ppermute | solution.py:17
  118.3 13.0 %collective-permute-start.17 = (bf16[8,16,512]{2,1,0:T(8,128)(2,1)}, bf16[8,16,512]{2,1,0:T(8,128)(2,1)}, u32[]{:S(2)}, u32[]{:S(2)}) collective-permute-start(bf16[8,16,512]{2,1,0:T(8,128)(2,1)} %bitcast.173), channel_id=1, source_target_pairs={{0,4},{4,8},{8,12},{12,16},{16,20},{20,24},{24,28},{28,32},{32,36}... | collective-permute-start | bytes 393224 | tf_op jit(solution)/shard_map/ppermute | solution.py:14
  133.2 20.4 %collective-permute-start.19 = (bf16[24,8,512]{2,1,0:T(8,128)(2,1)}, bf16[24,8,512]{2,1,0:T(8,128)(2,1)}, u32[]{:S(2)}, u32[]{:S(2)}) collective-permute-start(bf16[24,8,512]{2,1,0:T(8,128)(2,1)} %get-tuple-element.537), channel_id=1, source_target_pairs={{0,1},{1,2},{2,3},{4,5},{5,6},{6,7},{8,9},{9,10},{10,11},{12,13},{... | collective-permute-start | bytes 589832 | tf_op jit(solution)/shard_map/ppermute | solution.py:14
  134.5 19.1 %collective-permute-start.20 = (bf16[24,8,512]{2,1,0:T(8,128)(2,1)}, bf16[24,8,512]{2,1,0:T(8,128)(2,1)}, u32[]{:S(2)}, u32[]{:S(2)}) collective-permute-start(bf16[24,8,512]{2,1,0:T(8,128)(2,1)} %get-tuple-element.538), channel_id=1, source_target_pairs={{1,0},{2,1},{3,2},{5,4},{6,5},{7,6},{9,8},{10,9},{11,10},{13,12},{... | collective-permute-start | bytes 589832 | tf_op jit(solution)/shard_map/ppermute | solution.py:17
  179.4 13.6 %collective-permute-start.27 = (bf16[8,16,512]{2,1,0:T(8,128)(2,1)}, bf16[8,16,512]{2,1,0:T(8,128)(2,1)}, u32[]{:S(2)}, u32[]{:S(2)}) collective-permute-start(bf16[8,16,512]{2,1,0:T(8,128)(2,1)} %bitcast.176), channel_id=1, source_target_pairs={{4,0},{8,4},{12,8},{16,12},{20,16},{24,20},{28,24},{32,28},{36,32}... | collective-permute-start | bytes 393224 | tf_op jit(solution)/shard_map/ppermute | solution.py:17
  180.7 12.9 %collective-permute-start.26 = (bf16[8,16,512]{2,1,0:T(8,128)(2,1)}, bf16[8,16,512]{2,1,0:T(8,128)(2,1)}, u32[]{:S(2)}, u32[]{:S(2)}) collective-permute-start(bf16[8,16,512]{2,1,0:T(8,128)(2,1)} %bitcast.176), channel_id=1, source_target_pairs={{0,4},{4,8},{8,12},{12,16},{16,20},{20,24},{24,28},{28,32},{32,36}... | collective-permute-start | bytes 393224 | tf_op jit(solution)/shard_map/ppermute | solution.py:14
  195.5 20.6 %collective-permute-start.28 = (bf16[24,8,512]{2,1,0:T(8,128)(2,1)}, bf16[24,8,512]{2,1,0:T(8,128)(2,1)}, u32[]{:S(2)}, u32[]{:S(2)}) collective-permute-start(bf16[24,8,512]{2,1,0:T(8,128)(2,1)} %get-tuple-element.535), channel_id=1, source_target_pairs={{0,1},{1,2},{2,3},{4,5},{5,6},{6,7},{8,9},{9,10},{10,11},{12,13},{... | collective-permute-start | bytes 589832 | tf_op jit(solution)/shard_map/ppermute | solution.py:14
  196.8 19.3 %collective-permute-start.29 = (bf16[24,8,512]{2,1,0:T(8,128)(2,1)}, bf16[24,8,512]{2,1,0:T(8,128)(2,1)}, u32[]{:S(2)}, u32[]{:S(2)}) collective-permute-start(bf16[24,8,512]{2,1,0:T(8,128)(2,1)} %get-tuple-element.536), channel_id=1, source_target_pairs={{1,0},{2,1},{3,2},{5,4},{6,5},{7,6},{9,8},{10,9},{11,10},{13,12},{... | collective-permute-start | bytes 589832 | tf_op jit(solution)/shard_map/ppermute | solution.py:17
  223.5 217.1 %collective-permute-start.30 = (bf16[8,16,512]{2,1,0:T(8,128)(2,1)S(1)}, bf16[8,16,512]{2,1,0:T(8,128)(2,1)S(1)}, u32[]{:S(2)}, u32[]{:S(2)}) collective-permute-start(bf16[8,16,512]{2,1,0:T(8,128)(2,1)S(1)} %convert_element_type.203), channel_id=1, source_target_pairs={{64,0},{128,64},{192,128},{65,1},{129,65},{193,129},{66,2},{130,66... | collective-permute-start | bytes 393224 | tf_op jit(solution)/shard_map/ppermute | solution.py:25
  442.3 13.8 %collective-permute-start.36 = (bf16[8,16,512]{2,1,0:T(8,128)(2,1)}, bf16[8,16,512]{2,1,0:T(8,128)(2,1)}, u32[]{:S(2)}, u32[]{:S(2)}) collective-permute-start(bf16[8,16,512]{2,1,0:T(8,128)(2,1)} %bitcast.178), channel_id=1, source_target_pairs={{4,0},{8,4},{12,8},{16,12},{20,16},{24,20},{28,24},{32,28},{36,32}... | collective-permute-start | bytes 393224 | tf_op jit(solution)/shard_map/ppermute | solution.py:17
  443.5 13.1 %collective-permute-start.35 = (bf16[8,16,512]{2,1,0:T(8,128)(2,1)}, bf16[8,16,512]{2,1,0:T(8,128)(2,1)}, u32[]{:S(2)}, u32[]{:S(2)}) collective-permute-start(bf16[8,16,512]{2,1,0:T(8,128)(2,1)} %bitcast.178), channel_id=1, source_target_pairs={{0,4},{4,8},{8,12},{12,16},{16,20},{20,24},{24,28},{28,32},{32,36}... | collective-permute-start | bytes 393224 | tf_op jit(solution)/shard_map/ppermute | solution.py:14
  458.5 20.6 %collective-permute-start.37 = (bf16[24,8,512]{2,1,0:T(8,128)(2,1)}, bf16[24,8,512]{2,1,0:T(8,128)(2,1)}, u32[]{:S(2)}, u32[]{:S(2)}) collective-permute-start(bf16[24,8,512]{2,1,0:T(8,128)(2,1)} %get-tuple-element.533), channel_id=1, source_target_pairs={{0,1},{1,2},{2,3},{4,5},{5,6},{6,7},{8,9},{9,10},{10,11},{12,13},{... | collective-permute-start | bytes 589832 | tf_op jit(solution)/shard_map/ppermute | solution.py:14
  459.8 19.3 %collective-permute-start.38 = (bf16[24,8,512]{2,1,0:T(8,128)(2,1)}, bf16[24,8,512]{2,1,0:T(8,128)(2,1)}, u32[]{:S(2)}, u32[]{:S(2)}) collective-permute-start(bf16[24,8,512]{2,1,0:T(8,128)(2,1)} %get-tuple-element.534), channel_id=1, source_target_pairs={{1,0},{2,1},{3,2},{5,4},{6,5},{7,6},{9,8},{10,9},{11,10},{13,12},{... | collective-permute-start | bytes 589832 | tf_op jit(solution)/shard_map/ppermute | solution.py:17
  537.3 294.4 %reduce-scatter.3.cloned.1.call-start = ((), (), s32[]{:S(2)}) async-start(), calls=%async_computation.2 | async-start | bytes 3194880 | tf_op jit(solution)/shard_map/reduce_scatter | solution.py:250
  (49 other events, 399.6 us)
Sparse Core Ops, SparseCore 0:
  537.4 149.5 reduce-scatter.4
  691.1 140.5 reduce-scatter.2
where the time goes:
time: 848 us; the launch traced here: 840 us
  waiting for transfers between devices  535 us (63%)
  starting transfers between devices  106 us (12%)
  local copies, waits for them, and re-layouts  80.1 us (9%)
  other arithmetic  62.1 us (7%)
  matrix products  31.7 us (4%)
  between operations  14.9 us (2%)
  loops' own time  10.1 us (1%)
    ppermute x3, waiting for transfers between devices, shifted(): return lax.ppermute(block, axis, route)  229 us
    reduce_scatter x1, waiting for transfers between devices, body(): lax.psum_scatter(qkv_sum, ('row', 'col'), scatter_dimension=0, tiled=True)  143 us
    reduce_scatter x1, waiting for transfers between devices, body(): lax.psum_scatter(out_sum, ('row', 'col'), scatter_dimension=0, tiled=True)  140 us
    ppermute x18, starting transfers between devices, padded_2(): lax.ppermute(lax.slice_in_dim(block, 0, width, axis=dim), axis, backward)  58.9 us
    ppermute x18, starting transfers between devices, padded_2(): lax.ppermute(lax.slice_in_dim(block, block.shape[dim] - width, None, axis...  43.5 us
    another operation x21, local copies, waits for them, and re-layouts  27.3 us
    dot_general x6, matrix products, product(): return jnp.einsum(form, left, right, preferred_element_type=jnp.float32)  21.4 us
    concatenate x18, other arithmetic, padded_2(): block = jnp.concatenate([low, block, high], axis=dim)  19.8 us
  transfers between devices with their start and end apart: 41, of which 16 were waited for; matrix products, arithmetic and copies ran while one was open for 7% of the time, Pallas kernels for 0%

commit v1 on v0

v1 whole, which is shorter than its diff:
```python
import functools

import jax
import jax.numpy as jnp
import numpy as np
from jax import lax
from jax.experimental import pallas as pl
from jax.experimental.pallas import tpu as pltpu
from jax.sharding import Mesh
from jax.sharding import PartitionSpec as P

F32 = jnp.float32
BF16 = jnp.bfloat16
AXES = ("pipe", "z", "core", "col")
D = 512
PAIRS = 4
TOK = 128
OWN = 256
REGION = 768
VMEM_LIMIT = 40 * 1024 * 1024


def nn(a, b):
    return lax.dot_general(a, b, (((1,), (0,)), ((), ())), preferred_element_type=F32)


def nt(a, b):
    return lax.dot_general(a, b, (((1,), (1,)), ((), ())), preferred_element_type=F32)


def tn(a, b):
    return lax.dot_general(a, b, (((0,), (0,)), ((), ())), preferred_element_type=F32)


def two_heads(block):
    lane = lax.broadcasted_iota(jnp.int32, block.shape, 1)
    zero = jnp.zeros_like(block)
    return jnp.concatenate(
        [jnp.where(lane < 64, block, zero), jnp.where(lane < 64, zero, block)], axis=0
    )


def one_block(stacked):
    half = stacked.shape[0] // 2
    lane = lax.broadcasted_iota(jnp.int32, (half, 128), 1)
    return jnp.where(lane < 64, stacked[:half], stacked[half:])


def place(index, core):
    piece = index >> 8
    inner = index & 255
    side = inner - 128
    is_centre = inner < 128
    row = jnp.where(is_centre, inner >> 4, (side & 63) >> 3)
    col = jnp.where(is_centre, inner & 15, jnp.where(side < 64, (side & 7) - 8, (side & 7) + 16))
    mate = jnp.where(core == 0, 8, -8)
    row = row + jnp.where(piece == 1, mate, jnp.where(piece == 2, -mate, 0))
    return row, col


def window(where_ref, keys_own):
    row0, col0, core, rows, cols = (where_ref[i] for i in range(5))
    own = lax.broadcasted_iota(jnp.int32, (TOK, REGION), 0)
    reach_row, reach_col = place(lax.broadcasted_iota(jnp.int32, (TOK, REGION), 1), core)
    step_row, step_col = reach_row - (own >> 4), reach_col - (own & 15)
    if keys_own:
        step_row, step_col = -step_row, -step_col
    ok = (step_row >= -8) & (step_row <= 7) & (step_col >= -8) & (step_col <= 7)
    grid_row, grid_col = row0 + reach_row, col0 + reach_col
    return ok & (grid_row >= 0) & (grid_row < rows) & (grid_col >= 0) & (grid_col < cols)


def forward_kernel(where_ref, x0, x1, x2, w_ref, proj_ref, prob_ref, pack_ref, nlow_ref):
    for piece, x_ref in enumerate((x0, x1, x2)):
        x = x_ref[...].astype(F32)
        inverse = lax.rsqrt(jnp.mean(x * x, axis=-1, keepdims=True) + 1e-06)
        low = (x * inverse).astype(BF16)
        if piece < 2:
            nlow_ref[piece * TOK : (piece + 1) * TOK] = low[:TOK]
        proj_ref[piece * OWN : (piece + 1) * OWN] = nn(low, w_ref[...]).astype(BF16)
    ok = window(where_ref, False)
    ok2 = jnp.concatenate([ok, ok], axis=0)
    lane = lax.broadcasted_iota(jnp.int32, (TOK, 128), 1)
    stats = jnp.zeros((TOK, 128), F32)
    for pair in range(PAIRS):
        at = slice(128 * pair, 128 * pair + 128)
        query = two_heads(proj_ref[:TOK, at])
        scores = nt(query, proj_ref[:, D + 128 * pair : D + 128 * pair + 128]) * 0.125
        scores = jnp.where(ok2, scores, -1e30)
        highest = jnp.max(scores, axis=-1, keepdims=True)
        grown = jnp.exp(scores - highest)
        total = jnp.sum(grown, axis=-1, keepdims=True)
        probs = (grown * (1.0 / total)).astype(BF16)
        prob_ref[pair] = probs
        value = proj_ref[:, 2 * D + 128 * pair : 2 * D + 128 * pair + 128]
        pack_ref[:, at] = one_block(nn(probs, value)).astype(BF16)
        log_total = highest + jnp.log(total)
        rest = log_total
        for part in range(3):
            piece = rest.astype(BF16).astype(F32)
            rest = rest - piece
            for head in range(2):
                chosen = lane == 8 * part + 2 * pair + head
                stats = jnp.where(chosen, piece[TOK * head : TOK * head + TOK], stats)
    pack_ref[:, D:] = stats.astype(BF16)


def key_probs_kernel(where_ref, p0, p1, p2, proj_ref, prob_ref):
    head = lax.broadcasted_iota(jnp.int32, (8, 128), 0)
    lane = lax.broadcasted_iota(jnp.int32, (8, 128), 1)
    chosen = ((lane & 7) == head) & (lane < 24)
    pick = jnp.where(chosen, 1.0, 0.0).astype(BF16)
    stats = jnp.concatenate([p[:, D:] for p in (p0, p1, p2)], axis=0)
    log_total = nt(pick, stats)
    ok = window(where_ref, True)
    for pair in range(PAIRS):
        key = two_heads(proj_ref[:TOK, D + 128 * pair : D + 128 * pair + 128])
        scores = nt(key, proj_ref[:, 128 * pair : 128 * pair + 128]) * 0.125
        for side in range(2):
            at = 2 * pair + side
            part = scores[TOK * side : TOK * side + TOK] - log_total[at : at + 1]
            probs = jnp.exp(jnp.where(ok, part, -1e30))
            prob_ref[pair, TOK * side : TOK * side + TOK] = probs.astype(BF16)


def query_kernel(where_ref, g_ref, w_ref, pack_ref, proj_ref, prob_ref, dq_ref, *, turn):
    @pl.when(where_ref[5] == turn)
    def _():
        d_mixed = nt(g_ref[...].astype(BF16), w_ref[...]).astype(BF16)
        lane = lax.broadcasted_iota(jnp.int32, (TOK, 128), 1)
        for pair in range(PAIRS):
            at = slice(128 * pair, 128 * pair + 128)
            grad = d_mixed[:, at]
            prod = grad.astype(F32) * pack_ref[:, at].astype(F32)
            delta = jnp.concatenate(
                [
                    jnp.sum(jnp.where(lane < 64, prod, 0.0), axis=-1, keepdims=True),
                    jnp.sum(jnp.where(lane < 64, 0.0, prod), axis=-1, keepdims=True),
                ],
                axis=0,
            )
            value = proj_ref[:, 2 * D + 128 * pair : 2 * D + 128 * pair + 128]
            pressure = nt(two_heads(grad), value)
            slopes = (prob_ref[pair].astype(F32) * (pressure - delta)).astype(BF16)
            key = proj_ref[:, D + 128 * pair : D + 128 * pair + 128]
            dq_ref[:, at] = (one_block(nn(slopes, key)) * 0.125).astype(BF16)


def key_kernel(
    where_ref, g_ref, g0, g1, g2, wo_ref, p0, p1, p2, proj_ref, prob_ref, dq_ref, wq_ref, x_ref,
    in_prev, dp_prev, gl_prev,
    left_ref, right_ref, low_ref, in_ref, dp_ref, gl_ref, dm_ref, *, turn,
):
    active = where_ref[5] == turn

    @pl.when(jnp.logical_not(active))
    def _():
        in_ref[...] = in_prev[...]
        dp_ref[...] = dp_prev[...]
        gl_ref[...] = gl_prev[...]

    @pl.when(active)
    def _():
        head = lax.broadcasted_iota(jnp.int32, (8, D), 0)
        lane = lax.broadcasted_iota(jnp.int32, (8, D), 1)
        pick = jnp.where((lane >> 6) == head, 1.0, 0.0).astype(BF16)
        deltas = []
        for piece, (g, p) in enumerate(((g0, p0), (g1, p1), (g2, p2))):
            d_mixed = nt(g[...], wo_ref[...]).astype(BF16)
            dm_ref[piece * OWN : (piece + 1) * OWN] = d_mixed
            prod = d_mixed.astype(F32) * p[:, :D].astype(F32)
            high = prod.astype(BF16)
            rest = (prod - high.astype(F32)).astype(BF16)
            deltas.append(nt(pick, high) + nt(pick, rest))
        delta = jnp.concatenate(deltas, axis=1)
        dp_ref[:, :D] = dq_ref[...]
        for pair in range(PAIRS):
            at = slice(128 * pair, 128 * pair + 128)
            value = two_heads(proj_ref[:TOK, 2 * D + 128 * pair : 2 * D + 128 * pair + 128])
            grad = dm_ref[:, at]
            pressure = nt(value, grad)
            probs = prob_ref[pair]
            d_value = nn(probs, grad)
            slopes = []
            for side in range(2):
                h = 2 * pair + side
                rows = slice(TOK * side, TOK * side + TOK)
                slopes.append(
                    (probs[rows].astype(F32) * (pressure[rows] - delta[h : h + 1])).astype(BF16)
                )
            d_key = nn(jnp.concatenate(slopes, axis=0), proj_ref[:, at])
            dp_ref[:, D + 128 * pair : D + 128 * pair + 128] = (one_block(d_key) * 0.125).astype(BF16)
            dp_ref[:, 2 * D + 128 * pair : 2 * D + 128 * pair + 128] = one_block(d_value).astype(BF16)
        d_normed = nt(dp_ref[...], wq_ref[...])
        x = x_ref[...].astype(F32)
        inverse = lax.rsqrt(jnp.mean(x * x, axis=-1, keepdims=True) + 1e-06)
        normed = x * inverse
        inner = jnp.mean(d_normed * normed, axis=-1, keepdims=True)
        gradient = g_ref[...].astype(F32)
        out = gradient + inverse * (d_normed - normed * inner)
        in_ref[...] = out
        gl_ref[...] = g_ref[...].astype(BF16)
        low_ref[...] = out.astype(BF16)
        sides = out.reshape(8, 2, 8, D)
        left_ref[...] = sides[:, 0].reshape(64, D).astype(BF16)
        right_ref[...] = sides[:, 1].reshape(64, D).astype(BF16)


def weight_kernel(where_ref, n_ref, d0, d1, m0, m1, g0, g1, out_ref, full_ref):
    core = where_ref[2]
    full_ref[:, : 3 * D] = tn(n_ref[:TOK], d0[...]) + tn(n_ref[TOK:], d1[...])
    full_ref[:, 3 * D :] = tn(m0[...], g0[...]) + tn(m1[...], g1[...])
    chips, cols = out_ref.shape[1] // 8, out_ref.shape[0]
    for col in range(cols):
        rows = [
            full_ref[pl.ds(pl.multiple_of((2 * chip + core) * (8 * cols) + 8 * col, 8), 8)]
            for chip in range(chips)
        ]
        out_ref[col] = jnp.concatenate(rows, axis=0).astype(BF16)


def call(kernel, outs, *args, scratch=(), flops=0):
    vmem = pl.BlockSpec(memory_space=pltpu.VMEM)
    return pl.pallas_call(
        kernel,
        out_shape=[jax.ShapeDtypeStruct(s, t) for s, t in outs],
        in_specs=[pl.BlockSpec(memory_space=pltpu.SMEM)] + [vmem] * (len(args) - 1),
        out_specs=[vmem] * len(outs),
        scratch_shapes=list(scratch),
        compiler_params=pltpu.CompilerParams(vmem_limit_bytes=VMEM_LIMIT),
        cost_estimate=pl.CostEstimate(flops=flops, bytes_accessed=4 << 20, transcendentals=0),
    )(*args)


def body(sizes, activations, qkv_weight, out_weight, cotangent):
    pipes, chips, cols = sizes

    def routed(block, step, plane=None):
        pairs = []
        for p in range(pipes):
            for z in range(chips):
                for k in range(2):
                    for c in range(cols):
                        if plane is not None and p != plane:
                            continue
                        p2, r2, c2 = step(p, 2 * z + k, c)
                        if 0 <= p2 < pipes and 0 <= r2 < 2 * chips and 0 <= c2 < cols:
                            source = (p * 2 * chips + 2 * z + k) * cols + c
                            pairs.append((source, (p2 * 2 * chips + r2) * cols + c2))
        return lax.ppermute(block, AXES, pairs)

    def halves(block):
        shaped = block.reshape(8, 2, 8, block.shape[-1])
        return shaped[:, 0].reshape(64, -1), shaped[:, 1].reshape(64, -1)

    def col_rims(left_half, right_half, down=0, plane=None):
        left = routed(right_half, lambda p, r, c: (p - down, r, c + 1), plane)
        right = routed(left_half, lambda p, r, c: (p - down, r, c - 1), plane)
        return left, right

    def row_rims(own, plane=None):
        mate = routed(own, lambda p, r, c: (p, r ^ 1, c), plane)
        beyond = routed(own, lambda p, r, c: (p, r - 1 + 2 * (r & 1), c), plane)
        return own, mate, beyond

    def spread(block, plane=None):
        left, right = col_rims(*halves(block), plane=plane)
        return row_rims(jnp.concatenate([block, left, right], axis=0), plane)

    pipe, z, core, col = (lax.axis_index(axis) for axis in AXES)
    x = activations.reshape(TOK, D)
    w_qkv, w_out = qkv_weight[0], out_weight[0]
    cot = cotangent.reshape(TOK, D)
    row_total, col_total = 16 * chips, 16 * cols
    where = jnp.stack(
        [8 * (2 * z + core), 16 * col, core, row_total, col_total, pipes - 1 - pipe]
    ).astype(jnp.int32)

    xs = spread(x)
    gs = spread(cot.astype(BF16), pipes - 1)
    proj, q_probs, pack, nlow = call(
        forward_kernel,
        [((REGION, 3 * D), BF16), ((PAIRS, OWN, REGION), BF16), ((TOK, D + 128), BF16), ((OWN, D), BF16)],
        where, *xs, w_qkv, flops=2 << 30,
    )
    packs = spread(pack)
    (k_probs,) = call(
        key_probs_kernel, [((PAIRS, OWN, REGION), BF16)], where, *packs, proj, flops=1 << 28
    )
    d_in = jnp.zeros((TOK, D), F32)
    d_proj = jnp.zeros((TOK, 3 * D), BF16)
    g_low = jnp.zeros((TOK, D), BF16)
    gradient = cot
    for turn in range(pipes):
        plane = pipes - 1 - turn
        if turn > 0:
            centre = routed(low, lambda p, r, c: (p - 1, r, c), plane + 1)
            left, right = col_rims(left_half, right_half, 1, plane + 1)
            gs = row_rims(jnp.concatenate([centre, left, right], axis=0), plane)
            gradient = centre
        (d_query,) = call(
            functools.partial(query_kernel, turn=turn), [((TOK, D), BF16)],
            where, gradient, w_out, pack, proj, q_probs, flops=1 << 29,
        )
        left_half, right_half, low, d_in, d_proj, g_low = call(
            functools.partial(key_kernel, turn=turn),
            [((64, D), BF16), ((64, D), BF16), ((TOK, D), BF16), ((TOK, D), F32),
             ((TOK, 3 * D), BF16), ((TOK, D), BF16)],
            where, gradient, *gs, w_out, *packs, proj, k_probs, d_query, w_qkv, x,
            d_in, d_proj, g_low,
            scratch=[pltpu.VMEM((REGION, D), BF16)], flops=1 << 30,
        )
    swap = lambda p, r, c: (p, r ^ 1, c)
    (part,) = call(
        weight_kernel, [((cols, 8 * chips, 4 * D), BF16)],
        where, nlow, d_proj, routed(d_proj, swap), pack[:, :D], packs[1][:TOK, :D],
        g_low, routed(g_low, swap),
        scratch=[pltpu.VMEM((D, 4 * D), F32)], flops=1 << 30,
    )
    part = lax.all_to_all(part, "col", 0, 0, tiled=True)
    part = jnp.sum(part.astype(F32), axis=0).astype(BF16).reshape(chips, 8, 4 * D)
    part = lax.all_to_all(part, "z", 0, 0, tiled=True)
    part = jnp.sum(part.astype(F32), axis=0) * (row_total * col_total) ** (-0.5)
    return d_in.reshape(1, 8, 16, D), part[None, :, : 3 * D], part[None, :, 3 * D :]


def solution(mesh):
    pipes, rows, cols = (mesh.shape[axis] for axis in ("pipe", "row", "col"))
    fine = Mesh(np.asarray(mesh.devices).reshape(pipes, rows // 2, 2, cols), AXES)
    row = ("z", "core")
    return jax.shard_map(
        functools.partial(body, (pipes, rows // 2, cols)),
        mesh=fine,
        in_specs=(
            P("pipe", row, "col", None),
            P("pipe", None, None),
            P("pipe", None, None),
            P(row, "col", None),
        ),
        out_specs=(
            P("pipe", row, "col", None),
            P("pipe", ("z", "core", "col"), None),
            P("pipe", ("z", "core", "col"), None),
        ),
        check_vma=False,
    )
```

time: 848 us -> 167 us (0.20)
  waiting for transfers between devices: 535 us -> 53.9 us
  local copies, waits for them, and re-layouts: 80.1 us -> 2.56 us
  other arithmetic: 62.1 us -> 2.29 us
  starting transfers between devices: 106 us -> 46.7 us
  blocking collectives: 0 us -> 40.2 us
  matrix products: 31.7 us -> 0 us
  Pallas kernels: 0 us -> 18.3 us
  between operations: 14.9 us -> 1.29 us
  loops' own time: 10.1 us -> 0 us
    reduce_scatter x2 -> x0, waiting for transfers between devices: 283 us -> none  [the longest x1 143 us: body(): lax.psum_scatter(qkv_sum, ('row', 'col'), scatter_dimension=0, tiled=True)]
    ppermute x39 -> x29, waiting for transfers between devices: 251 us -> 53.9 us  [routed(): return lax.ppermute(block, AXES, pairs)]
    ppermute x39 -> x29, starting transfers between devices: 106 us -> 46.7 us  [routed(): return lax.ppermute(block, AXES, pairs)]
    all_to_all x0 -> x2, blocking collectives: none -> 40.2 us  [the longest x1 20.7 us: body(): part = lax.all_to_all(part, 'col', 0, 0, tiled=True)]
    another operation x24 -> x4, local copies, waits for them, and re-layouts: 33.4 us -> 1.11 us  [the longest x3 1.03 us: halves(): return (shaped[:, 0].reshape(64, -1), shaped[:, 1].reshape(64, -1))]
    dot_general x14 -> x0, matrix products: 31.7 us -> none  [the longest x6 21.4 us: product(): return jnp.einsum(form, left, right, preferred_element_type=jnp.float32)]
    concatenate x29 -> x2, other arithmetic: 21.6 us -> 0.94 us  [spread(): return row_rims(jnp.concatenate([block, left, right], axis=0), plane)]
    pallas_call x0 -> x11, Pallas kernels: none -> 18.3 us  [call(): pl.pallas_call(kernel, out_shape=[jax.ShapeDtypeStruct(s, t) for s, t in...]
  transfers between devices with their start and end apart: 41 -> 29, of which waited for: 16 -> 7; matrix products, arithmetic and copies ran while one was open for 7% -> 1% of each run, Pallas kernels for 0% -> 6%
where the time goes in v1:
time: 167 us; the launch traced here: 165 us
  waiting for transfers between devices  53.9 us (32%)
  starting transfers between devices  46.7 us (28%)
  blocking collectives  40.2 us (24%)
  Pallas kernels  18.3 us (11%)
  local copies, waits for them, and re-layouts  2.56 us (2%)
  other arithmetic  2.29 us (1%)
    ppermute x29, waiting for transfers between devices, routed(): return lax.ppermute(block, AXES, pairs)  53.9 us
    ppermute x29, starting transfers between devices, routed(): return lax.ppermute(block, AXES, pairs)  46.7 us
    all_to_all x1, blocking collectives, body(): part = lax.all_to_all(part, 'col', 0, 0, tiled=True)  20.7 us
    all_to_all x1, blocking collectives, body(): part = lax.all_to_all(part, 'z', 0, 0, tiled=True)  19.5 us
    pallas_call x11, Pallas kernels, call(): pl.pallas_call(kernel, out_shape=[jax.ShapeDtypeStruct(s, t) for s, t in...  18.3 us
  transfers between devices with their start and end apart: 29, of which 7 were waited for; matrix products, arithmetic and copies ran while one was open for 1% of the time, Pallas kernels for 6%

profile of v1, /device:TPU:6, one launch (start us, length us, event | category | flops | bytes accessed | tf_op | source)
XLA Modules:
  0.0 165.2 jit_solution(4821079613122359272)
XLA Ops:
  0.6 1.0 slice_bitcast_fusion.3
  1.6 1.3 collective-permute-start.4
  2.9 4.5 %collective-permute-start.5 = (bf16[64,512]{1,0:T(8,128)(2,1)S(1)}, bf16[64,512]{1,0:T(8,128)(2,1)S(1)}, u32[]{:S(2)}, u32[]{:S(2)}) collective-permute-start(bf16[64,512]{1,0:T(8,128)(2,1)S(1)} %get-tuple-element.58), channel_id=1, source_target_pairs={{1,0},{2,1},{3,2},{5,4},{6,5},{7,6},{9,8},{10,9},{11,10},{13,12},{... | collective-permute-start | bytes 196616 | tf_op jit(solution)/shard_map/ppermute | solution.py:250
  7.8 1.6 collective-permute-done.5
  9.4 0.9 pad_maximum_fusion.1.x0
  11.1 1.1 bitcast_convert_fusion
  13.7 4.6 %shard_map.67 = (bf16[768,1536]{1,0:T(8,128)(2,1)S(1)}, bf16[4,256,768]{2,1,0:T(8,128)(2,1)S(1)}, bf16[128,640]{1,0:T(8,128)(2,1)S(1)}, bf16[256,512]{1,0:T(8,128)(2,1)S(1)}) custom-call(s32[6]{0:T(128)S(1)} %stack.19.where_ref, bf16[256,512]{1,0:T(8,128)(2,1)S(1)} %pad_maximum_fusion.1.x0, bf16[256,512]{1,0:T(8,128)(2,1)S(1)} %collective-permute-done.6.x1, ...), custom_call_target="tpu_custom_call" | custom-call | flops 2147483648 | bytes 4194304 | tf_op jit(solution)/shard_map/pallas_call | solution.py:224
  18.3 1.4 collective-permute-start.8
  19.8 4.9 %collective-permute-start.9 = (bf16[64,640]{1,0:T(8,128)(2,1)S(1)}, bf16[64,640]{1,0:T(8,128)(2,1)S(1)}, u32[]{:S(2)}, u32[]{:S(2)}) collective-permute-start(bf16[64,640]{1,0:T(8,128)(2,1)S(1)} %get-tuple-element.55), channel_id=1, source_target_pairs={{1,0},{2,1},{3,2},{5,4},{6,5},{7,6},{9,8},{10,9},{11,10},{13,12},{... | collective-permute-start | bytes 245768 | tf_op jit(solution)/shard_map/ppermute | solution.py:250
  25.1 1.5 collective-permute-done.9
  26.7 4.2 %collective-permute-start.10 = (bf16[256,640]{1,0:T(8,128)(2,1)S(1)}, bf16[256,640]{1,0:T(8,128)(2,1)S(1)}, u32[]{:S(2)}, u32[]{:S(2)}) collective-permute-start(bf16[256,640]{1,0:T(8,128)(2,1)S(1)} %constant_dynamic-update-slice_fusion.p0), channel_id=1, source_target_pairs={{0,4},{1,5},{2,6},{3,7},{4,0},{5,1},{6,2},{7,3},{8,12},{9,13},{10,... | collective-permute-start | bytes 983048 | tf_op jit(solution)/shard_map/ppermute | solution.py:250
  33.6 1.6 shard_map.68.prob_ref
  45.5 1.3 collective-permute-start.22
  46.8 1.3 collective-permute-start.23
  48.7 46.3 %collective-permute-done.22.g_ref = bf16[128,512]{1,0:T(8,128)(2,1)S(1)} collective-permute-done((bf16[128,512]{1,0:T(8,128)(2,1)S(1)}, bf16[128,512]{1,0:T(8,128)(2,1)S(1)}, u32[]{:S(2)}, u32[]{:S(2)}) %collective-permute-start.22) | collective-permute-done | bytes 131104 | tf_op jit(solution)/shard_map/ppermute | solution.py:250
  95.0 2.2 %collective-permute-done.23 = bf16[64,512]{1,0:T(8,128)(2,1)S(1)} collective-permute-done((bf16[64,512]{1,0:T(8,128)(2,1)S(1)}, bf16[64,512]{1,0:T(8,128)(2,1)S(1)}, u32[]{:S(2)}, u32[]{:S(2)}) %collective-permute-start.23) | collective-permute-done | bytes 65568 | tf_op jit(solution)/shard_map/ppermute | solution.py:250
  97.2 9.0 %collective-permute-start.25 = (bf16[256,512]{1,0:T(8,128)(2,1)S(1)}, bf16[256,512]{1,0:T(8,128)(2,1)S(1)}, u32[]{:S(2)}, u32[]{:S(2)}) collective-permute-start(bf16[256,512]{1,0:T(8,128)(2,1)S(1)} %constant_dynamic-update-slice_fusion.9.g0), channel_id=1, source_target_pairs={{0,4},{1,5},{2,6},{3,7},{4,0},{5,1},{6,2},{7,3},{8,12},{9,13},{10,... | collective-permute-start | bytes 786440 | tf_op jit(solution)/shard_map/ppermute | solution.py:250
  106.9 2.0 %shard_map.75.dq_ref = bf16[128,512]{1,0:T(8,128)(2,1)S(1)} custom-call(s32[6]{0:T(128)S(1)} %stack.19.where_ref, bf16[128,512]{1,0:T(8,128)(2,1)S(1)} %collective-permute-done.22.g_ref, bf16[512,512]{1,0:T(8,128)(2,1)S(1)} %bitcast.49, bf16[128,640]{1,0:T(8,128)(2,1)S(1)} %get-tuple-element.28.pack_ref, bf16[768,1536]{1,0:T(8,128)(2,1)S(1)} %get-tuple-element.29.proj_ref, ...), custom_call_target="tpu_custom_call" | custom-call | flops 536870912 | bytes 4194304 | tf_op jit(solution)/shard_map/pallas_call | solution.py:224
  108.9 4.5 %shard_map.76 = (bf16[64,512]{1,0:T(8,128)(2,1)}, bf16[64,512]{1,0:T(8,128)(2,1)}, bf16[128,512]{1,0:T(8,128)(2,1)}, f32[128,512]{1,0:T(8,128)}, bf16[128,1536]{...) custom-call(s32[6]{0:T(128)S(1)} %stack.19.where_ref, bf16[128,512]{1,0:T(8,128)(2,1)S(1)} %collective-permute-done.22.g_ref, ...), custom_call_target="tpu_custom_call" | custom-call | flops 1073741824 | bytes 4194304 | tf_op jit(solution)/shard_map/pallas_call | solution.py:224
  113.5 6.6 %collective-permute-start.27 = (bf16[128,1536]{1,0:T(8,128)(2,1)S(1)}, bf16[128,1536]{1,0:T(8,128)(2,1)S(1)}, u32[]{:S(2)}, u32[]{:S(2)}) collective-permute-start(bf16[128,1536]{1,0:T(8,128)(2,1)S(1)} %get-tuple-element.51.d0), channel_id=1, source_target_pairs={{0,4},{1,5},{2,6},{3,7},{4,0},{5,1},{6,2},{7,3},{8,12},{9,13},{10,... | collective-permute-start | bytes 1179656 | tf_op jit(solution)/shard_map/ppermute | solution.py:250
  120.1 1.5 collective-permute-done.28.g1
  121.6 1.9 %shard_map.77 = bf16[4,64,2048]{2,1,0:T(8,128)(2,1)S(1)} custom-call(s32[6]{0:T(128)S(1)} %stack.19.where_ref, bf16[256,512]{1,0:T(8,128)(2,1)S(1)} %get-tuple-element.50.n_ref, bf16[128,1536]{1,0:T(8,128)(2,1)S(1)} %get-tuple-element.51.d0, bf16[128,1536]{1,0:T(8,128)(2,1)S(1)} %collective-permute-done.27.d1, bf16[128,512]{1,0:T(8,128)(2,1)S(1)} %slice.36.m0, ...), custom_call_target="tpu_custom_call" | custom-call | flops 1073741824 | bytes 4194304 | tf_op jit(solution)/shard_map/pallas_call | solution.py:224
  123.5 20.7 %all_to_all.10 = bf16[4,64,2048]{2,1,0:T(8,128)(2,1)S(1)} all-to-all(bf16[4,64,2048]{2,1,0:T(8,128)(2,1)S(1)} %shard_map.77), channel_id=1, replica_groups=mesh['pipe'=4,'z'=8,'core'=2,'col'=4] {'col'}, dimensions={0} | all-to-all | bytes 2097152 | tf_op jit(solution)/shard_map/all_to_all | solution.py:320
  144.4 19.5 %all_to_all.11 = bf16[8,8,2048]{2,1,0:T(8,128)(2,1)S(1)} all-to-all(bf16[8,8,2048]{2,1,0:T(8,128)(2,1)S(1)} %bitcast.65), channel_id=1, replica_groups=mesh['pipe'=4,'z'=8,'core'=2,'col'=4] {'z'}, dimensions={0} | all-to-all | bytes 524288 | tf_op jit(solution)/shard_map/all_to_all | solution.py:322
  (84 shorter events, 18.5 us)
Async XLA Ops:
  1.6 6.2 %collective-permute-start.4 = (bf16[64,512]{1,0:T(8,128)(2,1)S(1)}, bf16[64,512]{1,0:T(8,128)(2,1)S(1)}, u32[]{:S(2)}, u32[]{:S(2)}) collective-permute-start(bf16[64,512]{1,0:T(8,128)(2,1)S(1)} %get-tuple-element.57), channel_id=1, source_target_pairs={{0,1},{1,2},{2,3},{4,5},{5,6},{6,7},{8,9},{9,10},{10,11},{12,13},{... | collective-permute-start | bytes 196616 | tf_op jit(solution)/shard_map/ppermute | solution.py:250
  2.9 6.4 %collective-permute-start.5 = (bf16[64,512]{1,0:T(8,128)(2,1)S(1)}, bf16[64,512]{1,0:T(8,128)(2,1)S(1)}, u32[]{:S(2)}, u32[]{:S(2)}) collective-permute-start(bf16[64,512]{1,0:T(8,128)(2,1)S(1)} %get-tuple-element.58), channel_id=1, source_target_pairs={{1,0},{2,1},{3,2},{5,4},{6,5},{7,6},{9,8},{10,9},{11,10},{13,12},{... | collective-permute-start | bytes 196616 | tf_op jit(solution)/shard_map/ppermute | solution.py:250
  10.3 3.3 %collective-permute-start.6 = (bf16[256,512]{1,0:T(8,128)(2,1)S(1)}, bf16[256,512]{1,0:T(8,128)(2,1)S(1)}, u32[]{:S(2)}, u32[]{:S(2)}) collective-permute-start(bf16[256,512]{1,0:T(8,128)(2,1)S(1)} %pad_maximum_fusion.1.x0), channel_id=1, source_target_pairs={{0,4},{1,5},{2,6},{3,7},{4,0},{5,1},{6,2},{7,3},{8,12},{9,13},{10,... | collective-permute-start | bytes 786440 | tf_op jit(solution)/shard_map/ppermute | solution.py:250
  10.4 3.2 %collective-permute-start.7 = (bf16[256,512]{1,0:T(8,128)(2,1)S(1)}, bf16[256,512]{1,0:T(8,128)(2,1)S(1)}, u32[]{:S(2)}, u32[]{:S(2)}) collective-permute-start(bf16[256,512]{1,0:T(8,128)(2,1)S(1)} %pad_maximum_fusion.1.x0), channel_id=1, source_target_pairs={{4,8},{5,9},{6,10},{7,11},{8,4},{9,5},{10,6},{11,7},{12,16},{13,17... | collective-permute-start | bytes 786440 | tf_op jit(solution)/shard_map/ppermute | solution.py:250
  12.2 19.3 %collective-permute-start = (bf16[64,512]{1,0:T(8,128)(2,1)S(1)}, bf16[64,512]{1,0:T(8,128)(2,1)S(1)}, u32[]{:S(2)}, u32[]{:S(2)}) collective-permute-start(bf16[64,512]{1,0:T(8,128)(2,1)S(1)} %get-tuple-element.59), channel_id=1, source_target_pairs={{192,193},{193,194},{194,195},{196,197},{197,198},{198,199},{200,2... | collective-permute-start | bytes 196616 | tf_op jit(solution)/shard_map/ppermute | solution.py:250
  12.9 18.7 %collective-permute-start.1 = (bf16[64,512]{1,0:T(8,128)(2,1)S(1)}, bf16[64,512]{1,0:T(8,128)(2,1)S(1)}, u32[]{:S(2)}, u32[]{:S(2)}) collective-permute-start(bf16[64,512]{1,0:T(8,128)(2,1)S(1)} %get-tuple-element.60), channel_id=1, source_target_pairs={{193,192},{194,193},{195,194},{197,196},{198,197},{199,198},{201,2... | collective-permute-start | bytes 196616 | tf_op jit(solution)/shard_map/ppermute | solution.py:250
  18.3 6.8 %collective-permute-start.8 = (bf16[64,640]{1,0:T(8,128)(2,1)S(1)}, bf16[64,640]{1,0:T(8,128)(2,1)S(1)}, u32[]{:S(2)}, u32[]{:S(2)}) collective-permute-start(bf16[64,640]{1,0:T(8,128)(2,1)S(1)} %get-tuple-element.56), channel_id=1, source_target_pairs={{0,1},{1,2},{2,3},{4,5},{5,6},{6,7},{8,9},{9,10},{10,11},{12,13},{... | collective-permute-start | bytes 245768 | tf_op jit(solution)/shard_map/ppermute | solution.py:250
  19.8 6.9 %collective-permute-start.9 = (bf16[64,640]{1,0:T(8,128)(2,1)S(1)}, bf16[64,640]{1,0:T(8,128)(2,1)S(1)}, u32[]{:S(2)}, u32[]{:S(2)}) collective-permute-start(bf16[64,640]{1,0:T(8,128)(2,1)S(1)} %get-tuple-element.55), channel_id=1, source_target_pairs={{1,0},{2,1},{3,2},{5,4},{6,5},{7,6},{9,8},{10,9},{11,10},{13,12},{... | collective-permute-start | bytes 245768 | tf_op jit(solution)/shard_map/ppermute | solution.py:250
  26.7 6.8 %collective-permute-start.10 = (bf16[256,640]{1,0:T(8,128)(2,1)S(1)}, bf16[256,640]{1,0:T(8,128)(2,1)S(1)}, u32[]{:S(2)}, u32[]{:S(2)}) collective-permute-start(bf16[256,640]{1,0:T(8,128)(2,1)S(1)} %constant_dynamic-update-slice_fusion.p0), channel_id=1, source_target_pairs={{0,4},{1,5},{2,6},{3,7},{4,0},{5,1},{6,2},{7,3},{8,12},{9,13},{10,... | collective-permute-start | bytes 983048 | tf_op jit(solution)/shard_map/ppermute | solution.py:250
  30.9 2.7 %collective-permute-start.11 = (bf16[256,640]{1,0:T(8,128)(2,1)S(1)}, bf16[256,640]{1,0:T(8,128)(2,1)S(1)}, u32[]{:S(2)}, u32[]{:S(2)}) collective-permute-start(bf16[256,640]{1,0:T(8,128)(2,1)S(1)} %constant_dynamic-update-slice_fusion.p0), channel_id=1, source_target_pairs={{4,8},{5,9},{6,10},{7,11},{8,4},{9,5},{10,6},{11,7},{12,16},{13,17... | collective-permute-start | bytes 983048 | tf_op jit(solution)/shard_map/ppermute | solution.py:250
  31.6 3.6 %collective-permute-start.2 = (bf16[256,512]{1,0:T(8,128)(2,1)S(1)}, bf16[256,512]{1,0:T(8,128)(2,1)S(1)}, u32[]{:S(2)}, u32[]{:S(2)}) collective-permute-start(bf16[256,512]{1,0:T(8,128)(2,1)S(1)} %pad_maximum_fusion.g0), channel_id=1, source_target_pairs={{192,196},{193,197},{194,198},{195,199},{196,192},{197,193},{198,1... | collective-permute-start | bytes 786440 | tf_op jit(solution)/shard_map/ppermute | solution.py:250
  32.3 3.0 %collective-permute-start.3 = (bf16[256,512]{1,0:T(8,128)(2,1)S(1)}, bf16[256,512]{1,0:T(8,128)(2,1)S(1)}, u32[]{:S(2)}, u32[]{:S(2)}) collective-permute-start(bf16[256,512]{1,0:T(8,128)(2,1)S(1)} %pad_maximum_fusion.g0), channel_id=1, source_target_pairs={{196,200},{197,201},{198,202},{199,203},{200,196},{201,197},{202,1... | collective-permute-start | bytes 786440 | tf_op jit(solution)/shard_map/ppermute | solution.py:250
  35.9 2.0 %collective-permute-start.12 = (bf16[128,512]{1,0:T(8,128)(2,1)S(1)}, bf16[128,512]{1,0:T(8,128)(2,1)S(1)}, u32[]{:S(2)}, u32[]{:S(2)}) collective-permute-start(bf16[128,512]{1,0:T(8,128)(2,1)S(1)} %get-tuple-element.31), channel_id=1, source_target_pairs={{192,128},{193,129},{194,130},{195,131},{196,132},{197,133},{198,1... | collective-permute-start | bytes 393224 | tf_op jit(solution)/shard_map/ppermute | solution.py:250
  38.0 2.1 %collective-permute-start.15 = (bf16[256,512]{1,0:T(8,128)(2,1)S(1)}, bf16[256,512]{1,0:T(8,128)(2,1)S(1)}, u32[]{:S(2)}, u32[]{:S(2)}) collective-permute-start(bf16[256,512]{1,0:T(8,128)(2,1)S(1)} %constant_dynamic-update-slice_fusion.3.g0), channel_id=1, source_target_pairs={{128,132},{129,133},{130,134},{131,135},{132,128},{133,129},{134,1... | collective-permute-start | bytes 786440 | tf_op jit(solution)/shard_map/ppermute | solution.py:250
  38.7 1.4 collective-permute-start.16
  40.8 2.0 %collective-permute-start.17 = (bf16[128,512]{1,0:T(8,128)(2,1)S(1)}, bf16[128,512]{1,0:T(8,128)(2,1)S(1)}, u32[]{:S(2)}, u32[]{:S(2)}) collective-permute-start(bf16[128,512]{1,0:T(8,128)(2,1)S(1)} %get-tuple-element.37), channel_id=1, source_target_pairs={{128,64},{129,65},{130,66},{131,67},{132,68},{133,69},{134,70},{13... | collective-permute-start | bytes 393224 | tf_op jit(solution)/shard_map/ppermute | solution.py:250
  42.9 1.9 %collective-permute-start.20 = (bf16[256,512]{1,0:T(8,128)(2,1)S(1)}, bf16[256,512]{1,0:T(8,128)(2,1)S(1)}, u32[]{:S(2)}, u32[]{:S(2)}) collective-permute-start(bf16[256,512]{1,0:T(8,128)(2,1)S(1)} %constant_dynamic-update-slice_fusion.6.g0), channel_id=1, source_target_pairs={{64,68},{65,69},{66,70},{67,71},{68,64},{69,65},{70,66},{71,67},{7... | collective-permute-start | bytes 786440 | tf_op jit(solution)/shard_map/ppermute | solution.py:250
  45.5 49.5 %collective-permute-start.22 = (bf16[128,512]{1,0:T(8,128)(2,1)S(1)}, bf16[128,512]{1,0:T(8,128)(2,1)S(1)}, u32[]{:S(2)}, u32[]{:S(2)}) collective-permute-start(bf16[128,512]{1,0:T(8,128)(2,1)S(1)} %get-tuple-element.43), channel_id=1, source_target_pairs={{64,0},{65,1},{66,2},{67,3},{68,4},{69,5},{70,6},{71,7},{72,8},{73... | collective-permute-start | bytes 393224 | tf_op jit(solution)/shard_map/ppermute | solution.py:250
  46.8 50.4 %collective-permute-start.23 = (bf16[64,512]{1,0:T(8,128)(2,1)S(1)}, bf16[64,512]{1,0:T(8,128)(2,1)S(1)}, u32[]{:S(2)}, u32[]{:S(2)}) collective-permute-start(bf16[64,512]{1,0:T(8,128)(2,1)S(1)} %get-tuple-element.44), channel_id=1, source_target_pairs={{64,1},{65,2},{66,3},{68,5},{69,6},{70,7},{72,9},{73,10},{74,11},{... | collective-permute-start | bytes 196616 | tf_op jit(solution)/shard_map/ppermute | solution.py:250
  48.1 49.1 %collective-permute-start.24 = (bf16[64,512]{1,0:T(8,128)(2,1)S(1)}, bf16[64,512]{1,0:T(8,128)(2,1)S(1)}, u32[]{:S(2)}, u32[]{:S(2)}) collective-permute-start(bf16[64,512]{1,0:T(8,128)(2,1)S(1)} %get-tuple-element.45), channel_id=1, source_target_pairs={{65,0},{66,1},{67,2},{69,4},{70,5},{71,6},{73,8},{74,9},{75,10},{7... | collective-permute-start | bytes 196616 | tf_op jit(solution)/shard_map/ppermute | solution.py:250
  97.2 11.7 %collective-permute-start.25 = (bf16[256,512]{1,0:T(8,128)(2,1)S(1)}, bf16[256,512]{1,0:T(8,128)(2,1)S(1)}, u32[]{:S(2)}, u32[]{:S(2)}) collective-permute-start(bf16[256,512]{1,0:T(8,128)(2,1)S(1)} %constant_dynamic-update-slice_fusion.9.g0), channel_id=1, source_target_pairs={{0,4},{1,5},{2,6},{3,7},{4,0},{5,1},{6,2},{7,3},{8,12},{9,13},{10,... | collective-permute-start | bytes 786440 | tf_op jit(solution)/shard_map/ppermute | solution.py:250
  106.2 2.7 %collective-permute-start.26 = (bf16[256,512]{1,0:T(8,128)(2,1)S(1)}, bf16[256,512]{1,0:T(8,128)(2,1)S(1)}, u32[]{:S(2)}, u32[]{:S(2)}) collective-permute-start(bf16[256,512]{1,0:T(8,128)(2,1)S(1)} %constant_dynamic-update-slice_fusion.9.g0), channel_id=1, source_target_pairs={{4,8},{5,9},{6,10},{7,11},{8,4},{9,5},{10,6},{11,7},{12,16},{13,17... | collective-permute-start | bytes 786440 | tf_op jit(solution)/shard_map/ppermute | solution.py:250
  113.5 8.2 %collective-permute-start.27 = (bf16[128,1536]{1,0:T(8,128)(2,1)S(1)}, bf16[128,1536]{1,0:T(8,128)(2,1)S(1)}, u32[]{:S(2)}, u32[]{:S(2)}) collective-permute-start(bf16[128,1536]{1,0:T(8,128)(2,1)S(1)} %get-tuple-element.51.d0), channel_id=1, source_target_pairs={{0,4},{1,5},{2,6},{3,7},{4,0},{5,1},{6,2},{7,3},{8,12},{9,13},{10,... | collective-permute-start | bytes 1179656 | tf_op jit(solution)/shard_map/ppermute | solution.py:250
  120.1 1.5 collective-permute-start.28
  (9 other events, 49.7 us)

commit v2 on v1

--- a/solution.py
+++ b/solution.py
@@ -70,9 +70,14 @@
     return ok & (grid_row >= 0) & (grid_row < rows) & (grid_col >= 0) & (grid_col < cols)
 
 
-def forward_kernel(where_ref, x0, x1, x2, w_ref, proj_ref, prob_ref, pack_ref, nlow_ref):
-    for piece, x_ref in enumerate((x0, x1, x2)):
-        x = x_ref[...].astype(F32)
+def rows_of(refs, at):
+    return jnp.concatenate([ref[:, at] for ref in refs], axis=0)
+
+
+def forward_kernel(where_ref, *refs):
+    pieces, (w_ref, proj_ref, prob_ref, pack_ref, nlow_ref) = refs[:9], refs[9:]
+    for piece in range(3):
+        x = rows_of(pieces[3 * piece : 3 * piece + 3], slice(0, D)).astype(F32)
         inverse = lax.rsqrt(jnp.mean(x * x, axis=-1, keepdims=True) + 1e-06)
         low = (x * inverse).astype(BF16)
         if piece < 2:
@@ -105,13 +110,13 @@
     pack_ref[:, D:] = stats.astype(BF16)
 
 
-def key_probs_kernel(where_ref, p0, p1, p2, proj_ref, prob_ref):
+def key_probs_kernel(where_ref, *refs):
+    pieces, (proj_ref, prob_ref) = refs[:9], refs[9:]
     head = lax.broadcasted_iota(jnp.int32, (8, 128), 0)
     lane = lax.broadcasted_iota(jnp.int32, (8, 128), 1)
     chosen = ((lane & 7) == head) & (lane < 24)
     pick = jnp.where(chosen, 1.0, 0.0).astype(BF16)
-    stats = jnp.concatenate([p[:, D:] for p in (p0, p1, p2)], axis=0)
-    log_total = nt(pick, stats)
+    log_total = nt(pick, rows_of(pieces, slice(D, D + 128)))
     ok = window(where_ref, True)
     for pair in range(PAIRS):
         key = two_heads(proj_ref[:TOK, D + 128 * pair : D + 128 * pair + 128])
@@ -146,11 +151,50 @@
             dq_ref[:, at] = (one_block(nn(slopes, key)) * 0.125).astype(BF16)
 
 
-def key_kernel(
-    where_ref, g_ref, g0, g1, g2, wo_ref, p0, p1, p2, proj_ref, prob_ref, dq_ref, wq_ref, x_ref,
-    in_prev, dp_prev, gl_prev,
-    left_ref, right_ref, low_ref, in_ref, dp_ref, gl_ref, dm_ref, *, turn,
-):
+def key_side(first, grads, mixes, wo_ref, proj_ref, prob_ref):
+    d_mixed = nt(rows_of(grads, slice(-D, None)), wo_ref[...]).astype(BF16)
+    count = d_mixed.shape[0]
+    head = lax.broadcasted_iota(jnp.int32, (8, D), 0)
+    lane = lax.broadcasted_iota(jnp.int32, (8, D), 1)
+    pick = jnp.where((lane >> 6) == head, 1.0, 0.0).astype(BF16)
+    prod = d_mixed.astype(F32) * rows_of(mixes, slice(0, D)).astype(F32)
+    high = prod.astype(BF16)
+    rest = (prod - high.astype(F32)).astype(BF16)
+    delta = nt(pick, high) + nt(pick, rest)
+    terms = []
+    for pair in range(PAIRS):
+        at = slice(128 * pair, 128 * pair + 128)
+        value = two_heads(proj_ref[:TOK, 2 * D + 128 * pair : 2 * D + 128 * pair + 128])
+        grad = d_mixed[:, at]
+        pressure = nt(value, grad)
+        probs = prob_ref[pair, :, first : first + count]
+        slopes = []
+        for side in range(2):
+            h = 2 * pair + side
+            rows = slice(TOK * side, TOK * side + TOK)
+            slopes.append(
+                (probs[rows].astype(F32) * (pressure[rows] - delta[h : h + 1])).astype(BF16)
+            )
+        d_key = nn(jnp.concatenate(slopes, axis=0), proj_ref[first : first + count, at])
+        terms.append((one_block(d_key), one_block(nn(probs, grad))))
+    return terms
+
+
+def near_kernel(where_ref, *refs, turn):
+    grads, mixes, (wo_ref, proj_ref, prob_ref, sum_ref) = refs[:3], refs[3:6], refs[6:]
+
+    @pl.when(where_ref[5] == turn)
+    def _():
+        terms = key_side(0, grads, mixes, wo_ref, proj_ref, prob_ref)
+        for pair, (d_key, d_value) in enumerate(terms):
+            sum_ref[:, 128 * pair : 128 * pair + 128] = d_key
+            sum_ref[:, D + 128 * pair : D + 128 * pair + 128] = d_value
+
+
+def far_kernel(where_ref, *refs, turn, last):
+    grads, mixes, refs = refs[:6], refs[6:12], refs[12:]
+    (wo_ref, proj_ref, prob_ref, sum_ref, g_ref, dq_ref, wq_ref, x_ref), refs = refs[:8], refs[8:]
+    (in_prev, dp_prev, gl_prev), (in_ref, dp_ref, gl_ref, *sends) = refs[:3], refs[3:]
     active = where_ref[5] == turn
 
     @pl.when(jnp.logical_not(active))
@@ -161,62 +205,44 @@
 
     @pl.when(active)
     def _():
-        head = lax.broadcasted_iota(jnp.int32, (8, D), 0)
-        lane = lax.broadcasted_iota(jnp.int32, (8, D), 1)
-        pick = jnp.where((lane >> 6) == head, 1.0, 0.0).astype(BF16)
-        deltas = []
-        for piece, (g, p) in enumerate(((g0, p0), (g1, p1), (g2, p2))):
-            d_mixed = nt(g[...], wo_ref[...]).astype(BF16)
-            dm_ref[piece * OWN : (piece + 1) * OWN] = d_mixed
-            prod = d_mixed.astype(F32) * p[:, :D].astype(F32)
-            high = prod.astype(BF16)
-            rest = (prod - high.astype(F32)).astype(BF16)
-            deltas.append(nt(pick, high) + nt(pick, rest))
-        delta = jnp.concatenate(deltas, axis=1)
         dp_ref[:, :D] = dq_ref[...]
-        for pair in range(PAIRS):
-            at = slice(128 * pair, 128 * pair + 128)
-            value = two_heads(proj_ref[:TOK, 2 * D + 128 * pair : 2 * D + 128 * pair + 128])
-            grad = dm_ref[:, at]
-            pressure = nt(value, grad)
-            probs = prob_ref[pair]
-            d_value = nn(probs, grad)
-            slopes = []
-            for side in range(2):
-                h = 2 * pair + side
-                rows = slice(TOK * side, TOK * side + TOK)
-                slopes.append(
-                    (probs[rows].astype(F32) * (pressure[rows] - delta[h : h + 1])).astype(BF16)
-                )
-            d_key = nn(jnp.concatenate(slopes, axis=0), proj_ref[:, at])
-            dp_ref[:, D + 128 * pair : D + 128 * pair + 128] = (one_block(d_key) * 0.125).astype(BF16)
-            dp_ref[:, 2 * D + 128 * pair : 2 * D + 128 * pair + 128] = one_block(d_value).astype(BF16)
+        terms = key_side(OWN, grads, mixes, wo_ref, proj_ref, prob_ref)
+        for pair, (d_key, d_value) in enumerate(terms):
+            low, high = 128 * pair, 128 * pair + 128
+            d_key = (d_key + sum_ref[:, low:high]) * 0.125
+            dp_ref[:, D + low : D + high] = d_key.astype(BF16)
+            d_value = d_value + sum_ref[:, D + low : D + high]
+            dp_ref[:, 2 * D + low : 2 * D + high] = d_value.astype(BF16)
         d_normed = nt(dp_ref[...], wq_ref[...])
         x = x_ref[...].astype(F32)
         inverse = lax.rsqrt(jnp.mean(x * x, axis=-1, keepdims=True) + 1e-06)
         normed = x * inverse
         inner = jnp.mean(d_normed * normed, axis=-1, keepdims=True)
-        gradient = g_ref[...].astype(F32)
-        out = gradient + inverse * (d_normed - normed * inner)
+        out = g_ref[...].astype(F32) + inverse * (d_normed - normed * inner)
         in_ref[...] = out
-        gl_ref[...] = g_ref[...].astype(BF16)
-        low_ref[...] = out.astype(BF16)
-        sides = out.reshape(8, 2, 8, D)
-        left_ref[...] = sides[:, 0].reshape(64, D).astype(BF16)
-        right_ref[...] = sides[:, 1].reshape(64, D).astype(BF16)
-
-
-def weight_kernel(where_ref, n_ref, d0, d1, m0, m1, g0, g1, out_ref, full_ref):
-    core = where_ref[2]
+        gl_ref[:TOK] = g_ref[...].astype(BF16)
+        gl_ref[TOK:] = grads[0][:, -D:]
+        if not last:
+            low_ref, left_ref, right_ref = sends
+            low_ref[...] = out.astype(BF16)
+            sides = out.reshape(8, 2, 8, D)
+            left_ref[...] = sides[:, 0].reshape(64, D).astype(BF16)
+            right_ref[...] = sides[:, 1].reshape(64, D).astype(BF16)
+
+
+def weight_kernel(where_ref, n_ref, d0, d1, m0, m1, g_ref, *refs):
+    outs, full_ref = refs[:-1], refs[-1]
+    core, here = where_ref[2], where_ref[6]
     full_ref[:, : 3 * D] = tn(n_ref[:TOK], d0[...]) + tn(n_ref[TOK:], d1[...])
-    full_ref[:, 3 * D :] = tn(m0[...], g0[...]) + tn(m1[...], g1[...])
-    chips, cols = out_ref.shape[1] // 8, out_ref.shape[0]
-    for col in range(cols):
+    full_ref[:, 3 * D :] = tn(m0[:, :D], g_ref[:TOK]) + tn(m1[:, :D], g_ref[TOK:])
+    cols = len(outs)
+    for distance, out_ref in enumerate(outs):
+        col = lax.rem(here + distance, cols)
         rows = [
             full_ref[pl.ds(pl.multiple_of((2 * chip + core) * (8 * cols) + 8 * col, 8), 8)]
-            for chip in range(chips)
+            for chip in range(out_ref.shape[0] // 8)
         ]
-        out_ref[col] = jnp.concatenate(rows, axis=0).astype(BF16)
+        out_ref[...] = jnp.concatenate(rows, axis=0).astype(BF16)
 
 
 def call(kernel, outs, *args, scratch=(), flops=0):
@@ -249,23 +275,24 @@
                             pairs.append((source, (p2 * 2 * chips + r2) * cols + c2))
         return lax.ppermute(block, AXES, pairs)
 
-    def halves(block):
-        shaped = block.reshape(8, 2, 8, block.shape[-1])
-        return shaped[:, 0].reshape(64, -1), shaped[:, 1].reshape(64, -1)
-
-    def col_rims(left_half, right_half, down=0, plane=None):
-        left = routed(right_half, lambda p, r, c: (p - down, r, c + 1), plane)
-        right = routed(left_half, lambda p, r, c: (p - down, r, c - 1), plane)
-        return left, right
-
-    def row_rims(own, plane=None):
-        mate = routed(own, lambda p, r, c: (p, r ^ 1, c), plane)
-        beyond = routed(own, lambda p, r, c: (p, r - 1 + 2 * (r & 1), c), plane)
-        return own, mate, beyond
-
-    def spread(block, plane=None):
-        left, right = col_rims(*halves(block), plane=plane)
-        return row_rims(jnp.concatenate([block, left, right], axis=0), plane)
+    def side(block, at):
+        return block.reshape(8, 2, 8, -1)[:, at].reshape(64, -1)
+
+    def beyond(p, r, c):
+        return p, r - 1 + 2 * (r & 1), c
+
+    def mate(p, r, c):
+        return p, r ^ 1, c
+
+    def spread(block):
+        low, high = side(block, 0), side(block, 1)
+        left = routed(high, lambda p, r, c: (p, r, c + 1))
+        right = routed(low, lambda p, r, c: (p, r, c - 1))
+        far_left = routed(high, lambda p, r, c: beyond(p, r, c + 1))
+        far_right = routed(low, lambda p, r, c: beyond(p, r, c - 1))
+        far = routed(block, beyond)
+        near = [routed(piece, mate) for piece in (block, left, right)]
+        return [block, left, right, *near, far, far_left, far_right]
 
     pipe, z, core, col = (lax.axis_index(axis) for axis in AXES)
     x = activations.reshape(TOK, D)
@@ -273,15 +300,14 @@
     cot = cotangent.reshape(TOK, D)
     row_total, col_total = 16 * chips, 16 * cols
     where = jnp.stack(
-        [8 * (2 * z + core), 16 * col, core, row_total, col_total, pipes - 1 - pipe]
+        [8 * (2 * z + core), 16 * col, core, row_total, col_total, pipes - 1 - pipe, col]
     ).astype(jnp.int32)
 
-    xs = spread(x)
-    gs = spread(cot.astype(BF16), pipes - 1)
+    both = spread(jnp.concatenate([x, cot.astype(BF16)], axis=1))
     proj, q_probs, pack, nlow = call(
         forward_kernel,
         [((REGION, 3 * D), BF16), ((PAIRS, OWN, REGION), BF16), ((TOK, D + 128), BF16), ((OWN, D), BF16)],
-        where, *xs, w_qkv, flops=2 << 30,
+        where, *both, w_qkv, flops=2 << 30,
     )
     packs = spread(pack)
     (k_probs,) = call(
@@ -289,37 +315,49 @@
     )
     d_in = jnp.zeros((TOK, D), F32)
     d_proj = jnp.zeros((TOK, 3 * D), BF16)
-    g_low = jnp.zeros((TOK, D), BF16)
+    g_low = jnp.zeros((OWN, D), BF16)
     gradient = cot
+    grads = both
     for turn in range(pipes):
-        plane = pipes - 1 - turn
+        plane, last = pipes - 1 - turn, turn == pipes - 1
         if turn > 0:
-            centre = routed(low, lambda p, r, c: (p - 1, r, c), plane + 1)
-            left, right = col_rims(left_half, right_half, 1, plane + 1)
-            gs = row_rims(jnp.concatenate([centre, left, right], axis=0), plane)
-            gradient = centre
+            low, low_side, high_side = sends
+            gradient = routed(low, lambda p, r, c: (p - 1, r, c), plane + 1)
+            left = routed(high_side, lambda p, r, c: (p - 1, r, c + 1), plane + 1)
+            right = routed(low_side, lambda p, r, c: (p - 1, r, c - 1), plane + 1)
+            own = [gradient, left, right]
+            grads = own + [None] * 6
+            for at, piece in enumerate(own):
+                grads[6 + at] = routed(piece, beyond, plane)
+                grads[3 + at] = routed(piece, mate, plane)
         (d_query,) = call(
             functools.partial(query_kernel, turn=turn), [((TOK, D), BF16)],
             where, gradient, w_out, pack, proj, q_probs, flops=1 << 29,
         )
-        left_half, right_half, low, d_in, d_proj, g_low = call(
-            functools.partial(key_kernel, turn=turn),
-            [((64, D), BF16), ((64, D), BF16), ((TOK, D), BF16), ((TOK, D), F32),
-             ((TOK, 3 * D), BF16), ((TOK, D), BF16)],
-            where, gradient, *gs, w_out, *packs, proj, k_probs, d_query, w_qkv, x,
-            d_in, d_proj, g_low,
-            scratch=[pltpu.VMEM((REGION, D), BF16)], flops=1 << 30,
+        (sums,) = call(
+            functools.partial(near_kernel, turn=turn), [((TOK, 2 * D), F32)],
+            where, *grads[:3], *packs[:3], w_out, proj, k_probs, flops=1 << 29,
         )
-    swap = lambda p, r, c: (p, r ^ 1, c)
-    (part,) = call(
-        weight_kernel, [((cols, 8 * chips, 4 * D), BF16)],
-        where, nlow, d_proj, routed(d_proj, swap), pack[:, :D], packs[1][:TOK, :D],
-        g_low, routed(g_low, swap),
+        halves = [((64, D), BF16), ((64, D), BF16)]
+        d_in, d_proj, g_low, *sends = call(
+            functools.partial(far_kernel, turn=turn, last=last),
+            [((TOK, D), F32), ((TOK, 3 * D), BF16), ((OWN, D), BF16)]
+            + ([] if last else [((TOK, D), BF16)] + halves),
+            where, *grads[3:], *packs[3:], w_out, proj, k_probs, sums, gradient, d_query,
+            w_qkv, x, d_in, d_proj, g_low, flops=1 << 30,
+        )
+    parts = call(
+        weight_kernel, [((8 * chips, 4 * D), BF16)] * cols,
+        where, nlow, d_proj, routed(d_proj, mate), pack, packs[3], g_low,
         scratch=[pltpu.VMEM((D, 4 * D), F32)], flops=1 << 30,
     )
-    part = lax.all_to_all(part, "col", 0, 0, tiled=True)
-    part = jnp.sum(part.astype(F32), axis=0).astype(BF16).reshape(chips, 8, 4 * D)
-    part = lax.all_to_all(part, "z", 0, 0, tiled=True)
+    total = parts[0].astype(F32)
+    for distance in range(1, cols):
+        moved = lax.ppermute(
+            parts[distance], "col", [(c, (c + distance) % cols) for c in range(cols)]
+        )
+        total = total + moved.astype(F32)
+    part = lax.all_to_all(total.astype(BF16).reshape(chips, 8, 4 * D), "z", 0, 0, tiled=True)
     part = jnp.sum(part.astype(F32), axis=0) * (row_total * col_total) ** (-0.5)
     return d_in.reshape(1, 8, 16, D), part[None, :, : 3 * D], part[None, :, 3 * D :]
 

time: 167 us -> 214 us (1.28)
  starting transfers between devices: 46.7 us -> 93.7 us
  blocking collectives: 40.2 us -> 19.3 us
  waiting for transfers between devices: 53.9 us -> 71.5 us
  Pallas kernels: 18.3 us -> 21.4 us
    ppermute x0 -> x3, starting transfers between devices: none -> 31.6 us  [body(): lax.ppermute(parts[distance], 'col', [(c, (c + distance) % cols) for c in...]
    all_to_all x2 -> x1, blocking collectives: 40.2 us -> 19.3 us  [body(): lax.all_to_all(total.astype(BF16).reshape(chips, 8, 4 * D), 'z', 0, 0, ti...]
    ppermute x29 -> x44, starting transfers between devices: 46.7 us -> 62 us  [routed(): return lax.ppermute(block, AXES, pairs)]
    ppermute x29 -> x44, waiting for transfers between devices: 53.9 us -> 64.5 us  [routed(): return lax.ppermute(block, AXES, pairs)]
    ppermute x0 -> x3, waiting for transfers between devices: none -> 6.97 us  [body(): lax.ppermute(parts[distance], 'col', [(c, (c + distance) % cols) for c in...]
    pallas_call x11 -> x15, Pallas kernels: 18.3 us -> 21.4 us  [call(): pl.pallas_call(kernel, out_shape=[jax.ShapeDtypeStruct(s, t) for s, t in...]
  transfers between devices with their start and end apart: 29 -> 47, of which waited for: 7 -> 7; matrix products, arithmetic and copies ran while one was open for 1% -> 0% of each run, Pallas kernels for 6% -> 3%
where the time goes in v2:
time: 214 us; the launch traced here: 212 us
  starting transfers between devices  93.7 us (44%)
  waiting for transfers between devices  71.5 us (33%)
  Pallas kernels  21.4 us (10%)
  blocking collectives  19.3 us (9%)
  other arithmetic  3.18 us (1%)
    ppermute x44, waiting for transfers between devices, routed(): return lax.ppermute(block, AXES, pairs)  64.5 us
    ppermute x44, starting transfers between devices, routed(): return lax.ppermute(block, AXES, pairs)  62 us
    ppermute x3, starting transfers between devices, body(): lax.ppermute(parts[distance], 'col', [(c, (c + distance) % cols) for c in...  31.6 us
    pallas_call x15, Pallas kernels, call(): pl.pallas_call(kernel, out_shape=[jax.ShapeDtypeStruct(s, t) for s, t in...  21.4 us
    all_to_all x1, blocking collectives, body(): lax.all_to_all(total.astype(BF16).reshape(chips, 8, 4 * D), 'z', 0, 0, ti...  19.3 us
    ppermute x3, waiting for transfers between devices, body(): lax.ppermute(parts[distance], 'col', [(c, (c + distance) % cols) for c in...  6.97 us
  transfers between devices with their start and end apart: 47, of which 7 were waited for; matrix products, arithmetic and copies ran while one was open for 0% of the time, Pallas kernels for 3%

profile of v2, /device:TPU:6, one launch (start us, length us, event | category | flops | bytes accessed | tf_op | source)
XLA Modules:
  0.0 212.0 jit_solution(14156076005234808136)
XLA Ops:
  3.4 2.7 %collective-permute-start.3 = (bf16[64,1024]{1,0:T(8,128)(2,1)S(1)}, bf16[64,1024]{1,0:T(8,128)(2,1)S(1)}, u32[]{:S(2)}, u32[]{:S(2)}) collective-permute-start(bf16[64,1024]{1,0:T(8,128)(2,1)S(1)} %get-tuple-element.61), channel_id=1, source_target_pairs={{1,0},{2,1},{3,2},{5,4},{6,5},{7,6},{9,8},{10,9},{11,10},{13,12},{... | collective-permute-start | bytes 393224 | tf_op jit(solution)/shard_map/ppermute | solution.py:276
  6.1 1.3 collective-permute-start.1
  9.1 4.6 %collective-permute-start = (bf16[128,1024]{1,0:T(8,128)(2,1)S(1)}, bf16[128,1024]{1,0:T(8,128)(2,1)S(1)}, u32[]{:S(2)}, u32[]{:S(2)}) collective-permute-start(bf16[128,1024]{1,0:T(8,128)(2,1)S(1)} %pad_maximum_fusion.refs_0_), channel_id=1, source_target_pairs={{0,4},{1,5},{2,6},{3,7},{4,0},{5,1},{6,2},{7,3},{8,12},{9,13},{10,... | collective-permute-start | bytes 786440 | tf_op jit(solution)/shard_map/ppermute | solution.py:276
  16.5 4.6 %shard_map.67 = (bf16[768,1536]{1,0:T(8,128)(2,1)S(1)}, bf16[4,256,768]{2,1,0:T(8,128)(2,1)S(1)}, bf16[128,640]{1,0:T(8,128)(2,1)S(1)}, bf16[256,512]{1,0:T(8,128)(2,1)S(1)}) custom-call(s32[7]{0:T(128)S(1)} %stack.23.where_ref, bf16[128,1024]{1,0:T(8,128)(2,1)S(1)} %pad_maximum_fusion.refs_0_, bf16[64,1024]{1,0:T(8,128)(2,1)S(1)} %collective-permute-done.1.refs_1_, ...), custom_call_target="tpu_custom_call" | custom-call | flops 2147483648 | bytes 4194304 | tf_op jit(solution)/shard_map/pallas_call | solution.py:250
  21.8 6.0 %collective-permute-start.11 = (bf16[64,640]{1,0:T(8,128)(2,1)S(1)}, bf16[64,640]{1,0:T(8,128)(2,1)S(1)}, u32[]{:S(2)}, u32[]{:S(2)}) collective-permute-start(bf16[64,640]{1,0:T(8,128)(2,1)S(1)} %get-tuple-element.65), channel_id=1, source_target_pairs={{1,0},{2,1},{3,2},{5,4},{6,5},{7,6},{9,8},{10,9},{11,10},{13,12},{... | collective-permute-start | bytes 245768 | tf_op jit(solution)/shard_map/ppermute | solution.py:276
  27.8 1.3 collective-permute-start.9
  29.8 8.8 %collective-permute-start.8 = (bf16[128,640]{1,0:T(8,128)(2,1)S(1)}, bf16[128,640]{1,0:T(8,128)(2,1)S(1)}, u32[]{:S(2)}, u32[]{:S(2)}) collective-permute-start(bf16[128,640]{1,0:T(8,128)(2,1)S(1)} %get-tuple-element.32.refs_0_.refs_3_.pack_ref.m0), channel_id=1, source_target_pairs={{0,4},{1,5},{2,6},{3,7},{4,0},{5,1},{6,2},{7,3},{8,12},{9,13},{10,... | collective-permute-start | bytes 491528 | tf_op jit(solution)/shard_map/ppermute | solution.py:276
  41.3 1.6 shard_map.68.refs_8_.refs_14_
  60.5 1.3 collective-permute-start.34
  61.8 1.5 collective-permute-start.36
  64.0 61.0 %collective-permute-done.36.refs_1_ = bf16[64,512]{1,0:T(8,128)(2,1)S(1)} collective-permute-done((bf16[64,512]{1,0:T(8,128)(2,1)S(1)}, bf16[64,512]{1,0:T(8,128)(2,1)S(1)}, u32[]{:S(2)}, u32[]{:S(2)}) %collective-permute-start.36) | collective-permute-done | bytes 65568 | tf_op jit(solution)/shard_map/ppermute | solution.py:276
  126.3 6.8 %collective-permute-start.35 = (bf16[128,512]{1,0:T(8,128)(2,1)S(1)}, bf16[128,512]{1,0:T(8,128)(2,1)S(1)}, u32[]{:S(2)}, u32[]{:S(2)}) collective-permute-start(bf16[128,512]{1,0:T(8,128)(2,1)S(1)} %collective-permute-done.34.refs_0_.g_ref.refs_16_), channel_id=1, source_target_pairs={{0,4},{1,5},{2,6},{3,7},{4,0},{5,1},{6,2},{7,3},{8,12},{9,13},{10,... | collective-permute-start | bytes 393224 | tf_op jit(solution)/shard_map/ppermute | solution.py:276
  133.2 1.9 collective-permute-start.37
  135.8 5.4 %collective-permute-start.39 = (bf16[64,512]{1,0:T(8,128)(2,1)S(1)}, bf16[64,512]{1,0:T(8,128)(2,1)S(1)}, u32[]{:S(2)}, u32[]{:S(2)}) collective-permute-start(bf16[64,512]{1,0:T(8,128)(2,1)S(1)} %collective-permute-done.38.refs_2_), channel_id=1, source_target_pairs={{0,4},{1,5},{2,6},{3,7},{4,0},{5,1},{6,2},{7,3},{8,12},{9,13},{10,... | collective-permute-start | bytes 196616 | tf_op jit(solution)/shard_map/ppermute | solution.py:276
  141.2 2.0 shard_map.79.refs_17_
  143.2 2.1 shard_map.78.refs_15_
  145.3 3.8 %shard_map.80 = (f32[128,512]{1,0:T(8,128)}, bf16[128,1536]{1,0:T(8,128)(2,1)S(1)}, bf16[256,512]{1,0:T(8,128)(2,1)S(1)}) custom-call(s32[7]{0:T(128)S(1)} %stack.23.where_ref, bf16[128,512]{1,0:T(8,128)(2,1)S(1)} %collective-permute-done.35.refs_0_, bf16[64,512]{1,0:T(8,128)(2,1)S(1)} %collective-permute-done.37.refs_1_, ...), custom_call_target="tpu_custom_call" | custom-call | flops 1073741824 | bytes 4194304 | tf_op jit(solution)/shard_map/pallas_call | solution.py:250
  149.1 1.7 collective-permute-done.43.d1
  150.8 1.9 shard_map.81
  152.7 8.0 %collective-permute-start.44 = (bf16[64,2048]{1,0:T(8,128)(2,1)S(1)}, bf16[64,2048]{1,0:T(8,128)(2,1)S(1)}, u32[]{:S(2)}, u32[]{:S(2)}) collective-permute-start(bf16[64,2048]{1,0:T(8,128)(2,1)S(1)} %get-tuple-element.58), channel_id=1, source_target_pairs={{0,1},{1,2},{2,3},{3,0},{4,5},{5,6},{6,7},{7,4},{8,9},{9,10},{10,1... | collective-permute-start | bytes 786440 | tf_op jit(solution)/shard_map/ppermute | solution.py:356
  160.7 11.8 %collective-permute-start.45 = (bf16[64,2048]{1,0:T(8,128)(2,1)S(1)}, bf16[64,2048]{1,0:T(8,128)(2,1)S(1)}, u32[]{:S(2)}, u32[]{:S(2)}) collective-permute-start(bf16[64,2048]{1,0:T(8,128)(2,1)S(1)} %get-tuple-element.59), channel_id=1, source_target_pairs={{0,2},{1,3},{2,0},{3,1},{4,6},{5,7},{6,4},{7,5},{8,10},{9,11},{10,... | collective-permute-start | bytes 786440 | tf_op jit(solution)/shard_map/ppermute | solution.py:356
  172.5 11.8 %collective-permute-start.46 = (bf16[64,2048]{1,0:T(8,128)(2,1)S(1)}, bf16[64,2048]{1,0:T(8,128)(2,1)S(1)}, u32[]{:S(2)}, u32[]{:S(2)}) collective-permute-start(bf16[64,2048]{1,0:T(8,128)(2,1)S(1)} %get-tuple-element.60), channel_id=1, source_target_pairs={{0,3},{1,0},{2,1},{3,2},{4,7},{5,4},{6,5},{7,6},{8,11},{9,8},{10,9... | collective-permute-start | bytes 786440 | tf_op jit(solution)/shard_map/ppermute | solution.py:356
  184.4 7.0 %collective-permute-done.46 = bf16[64,2048]{1,0:T(8,128)(2,1)S(1)} collective-permute-done((bf16[64,2048]{1,0:T(8,128)(2,1)S(1)}, bf16[64,2048]{1,0:T(8,128)(2,1)S(1)}, u32[]{:S(2)}, u32[]{:S(2)}) %collective-permute-start.46) | collective-permute-done | bytes 262176 | tf_op jit(solution)/shard_map/ppermute | solution.py:356
  191.5 19.3 %all_to_all.5 = bf16[8,8,2048]{2,1,0:T(8,128)(2,1)S(1)} all-to-all(bf16[8,8,2048]{2,1,0:T(8,128)(2,1)S(1)} %fusion), channel_id=1, replica_groups=mesh['pipe'=4,'z'=8,'core'=2,'col'=4] {'z'}, dimensions={0} | all-to-all | bytes 524288 | tf_op jit(solution)/shard_map/all_to_all | solution.py:360
  (107 shorter events, 32.4 us)
Async XLA Ops:
  2.7 10.9 %collective-permute-start.7 = (bf16[64,1024]{1,0:T(8,128)(2,1)S(1)}, bf16[64,1024]{1,0:T(8,128)(2,1)S(1)}, u32[]{:S(2)}, u32[]{:S(2)}) collective-permute-start(bf16[64,1024]{1,0:T(8,128)(2,1)S(1)} %get-tuple-element.61), channel_id=1, source_target_pairs={{5,8},{6,9},{7,10},{9,4},{10,5},{11,6},{13,16},{14,17},{15,18},{17... | collective-permute-start | bytes 393224 | tf_op jit(solution)/shard_map/ppermute | solution.py:276
  3.4 10.9 %collective-permute-start.3 = (bf16[64,1024]{1,0:T(8,128)(2,1)S(1)}, bf16[64,1024]{1,0:T(8,128)(2,1)S(1)}, u32[]{:S(2)}, u32[]{:S(2)}) collective-permute-start(bf16[64,1024]{1,0:T(8,128)(2,1)S(1)} %get-tuple-element.61), channel_id=1, source_target_pairs={{1,0},{2,1},{3,2},{5,4},{6,5},{7,6},{9,8},{10,9},{11,10},{13,12},{... | collective-permute-start | bytes 393224 | tf_op jit(solution)/shard_map/ppermute | solution.py:276
  6.1 8.9 %collective-permute-start.1 = (bf16[64,1024]{1,0:T(8,128)(2,1)S(1)}, bf16[64,1024]{1,0:T(8,128)(2,1)S(1)}, u32[]{:S(2)}, u32[]{:S(2)}) collective-permute-start(bf16[64,1024]{1,0:T(8,128)(2,1)S(1)} %get-tuple-element.62), channel_id=1, source_target_pairs={{0,1},{1,2},{2,3},{4,5},{5,6},{6,7},{8,9},{9,10},{10,11},{12,13},{... | collective-permute-start | bytes 393224 | tf_op jit(solution)/shard_map/ppermute | solution.py:276
  8.4 8.1 %collective-permute-start.5 = (bf16[128,1024]{1,0:T(8,128)(2,1)S(1)}, bf16[128,1024]{1,0:T(8,128)(2,1)S(1)}, u32[]{:S(2)}, u32[]{:S(2)}) collective-permute-start(bf16[128,1024]{1,0:T(8,128)(2,1)S(1)} %pad_maximum_fusion.refs_0_), channel_id=1, source_target_pairs={{4,8},{5,9},{6,10},{7,11},{8,4},{9,5},{10,6},{11,7},{12,16},{13,17... | collective-permute-start | bytes 786440 | tf_op jit(solution)/shard_map/ppermute | solution.py:276
  9.1 7.4 %collective-permute-start = (bf16[128,1024]{1,0:T(8,128)(2,1)S(1)}, bf16[128,1024]{1,0:T(8,128)(2,1)S(1)}, u32[]{:S(2)}, u32[]{:S(2)}) collective-permute-start(bf16[128,1024]{1,0:T(8,128)(2,1)S(1)} %pad_maximum_fusion.refs_0_), channel_id=1, source_target_pairs={{0,4},{1,5},{2,6},{3,7},{4,0},{5,1},{6,2},{7,3},{8,12},{9,13},{10,... | collective-permute-start | bytes 786440 | tf_op jit(solution)/shard_map/ppermute | solution.py:276
  21.1 17.4 %collective-permute-start.15 = (bf16[64,640]{1,0:T(8,128)(2,1)S(1)}, bf16[64,640]{1,0:T(8,128)(2,1)S(1)}, u32[]{:S(2)}, u32[]{:S(2)}) collective-permute-start(bf16[64,640]{1,0:T(8,128)(2,1)S(1)} %get-tuple-element.65), channel_id=1, source_target_pairs={{5,8},{6,9},{7,10},{9,4},{10,5},{11,6},{13,16},{14,17},{15,18},{17... | collective-permute-start | bytes 245768 | tf_op jit(solution)/shard_map/ppermute | solution.py:276
  21.8 17.4 %collective-permute-start.11 = (bf16[64,640]{1,0:T(8,128)(2,1)S(1)}, bf16[64,640]{1,0:T(8,128)(2,1)S(1)}, u32[]{:S(2)}, u32[]{:S(2)}) collective-permute-start(bf16[64,640]{1,0:T(8,128)(2,1)S(1)} %get-tuple-element.65), channel_id=1, source_target_pairs={{1,0},{2,1},{3,2},{5,4},{6,5},{7,6},{9,8},{10,9},{11,10},{13,12},{... | collective-permute-start | bytes 245768 | tf_op jit(solution)/shard_map/ppermute | solution.py:276
  27.8 12.2 %collective-permute-start.9 = (bf16[64,640]{1,0:T(8,128)(2,1)S(1)}, bf16[64,640]{1,0:T(8,128)(2,1)S(1)}, u32[]{:S(2)}, u32[]{:S(2)}) collective-permute-start(bf16[64,640]{1,0:T(8,128)(2,1)S(1)} %get-tuple-element.66), channel_id=1, source_target_pairs={{0,1},{1,2},{2,3},{4,5},{5,6},{6,7},{8,9},{9,10},{10,11},{12,13},{... | collective-permute-start | bytes 245768 | tf_op jit(solution)/shard_map/ppermute | solution.py:276
  29.1 12.2 %collective-permute-start.13 = (bf16[128,640]{1,0:T(8,128)(2,1)S(1)}, bf16[128,640]{1,0:T(8,128)(2,1)S(1)}, u32[]{:S(2)}, u32[]{:S(2)}) collective-permute-start(bf16[128,640]{1,0:T(8,128)(2,1)S(1)} %get-tuple-element.32.refs_0_.refs_3_.pack_ref.m0), channel_id=1, source_target_pairs={{4,8},{5,9},{6,10},{7,11},{8,4},{9,5},{10,6},{11,7},{12,16},{13,17... | collective-permute-start | bytes 491528 | tf_op jit(solution)/shard_map/ppermute | solution.py:276
  29.8 11.5 %collective-permute-start.8 = (bf16[128,640]{1,0:T(8,128)(2,1)S(1)}, bf16[128,640]{1,0:T(8,128)(2,1)S(1)}, u32[]{:S(2)}, u32[]{:S(2)}) collective-permute-start(bf16[128,640]{1,0:T(8,128)(2,1)S(1)} %get-tuple-element.32.refs_0_.refs_3_.pack_ref.m0), channel_id=1, source_target_pairs={{0,4},{1,5},{2,6},{3,7},{4,0},{5,1},{6,2},{7,3},{8,12},{9,13},{10,... | collective-permute-start | bytes 491528 | tf_op jit(solution)/shard_map/ppermute | solution.py:276
  47.3 4.5 %collective-permute-start.22 = (bf16[128,512]{1,0:T(8,128)(2,1)S(1)}, bf16[128,512]{1,0:T(8,128)(2,1)S(1)}, u32[]{:S(2)}, u32[]{:S(2)}) collective-permute-start(bf16[128,512]{1,0:T(8,128)(2,1)S(1)} %collective-permute-done.16.refs_0_.g_ref.refs_16_), channel_id=1, source_target_pairs={{132,136},{133,137},{134,138},{135,139},{136,132},{137,133},{138,1... | collective-permute-start | bytes 393224 | tf_op jit(solution)/shard_map/ppermute | solution.py:276
  55.3 4.5 %collective-permute-start.31 = (bf16[128,512]{1,0:T(8,128)(2,1)S(1)}, bf16[128,512]{1,0:T(8,128)(2,1)S(1)}, u32[]{:S(2)}, u32[]{:S(2)}) collective-permute-start(bf16[128,512]{1,0:T(8,128)(2,1)S(1)} %collective-permute-done.25.refs_0_.g_ref.refs_16_), channel_id=1, source_target_pairs={{68,72},{69,73},{70,74},{71,75},{72,68},{73,69},{74,70},{75,71},{7... | collective-permute-start | bytes 393224 | tf_op jit(solution)/shard_map/ppermute | solution.py:276
  60.5 65.2 %collective-permute-start.34 = (bf16[128,512]{1,0:T(8,128)(2,1)S(1)}, bf16[128,512]{1,0:T(8,128)(2,1)S(1)}, u32[]{:S(2)}, u32[]{:S(2)}) collective-permute-start(bf16[128,512]{1,0:T(8,128)(2,1)S(1)} %get-tuple-element.47), channel_id=1, source_target_pairs={{64,0},{65,1},{66,2},{67,3},{68,4},{69,5},{70,6},{71,7},{72,8},{73... | collective-permute-start | bytes 393224 | tf_op jit(solution)/shard_map/ppermute | solution.py:276
  61.8 63.2 %collective-permute-start.36 = (bf16[64,512]{1,0:T(8,128)(2,1)S(1)}, bf16[64,512]{1,0:T(8,128)(2,1)S(1)}, u32[]{:S(2)}, u32[]{:S(2)}) collective-permute-start(bf16[64,512]{1,0:T(8,128)(2,1)S(1)} %get-tuple-element.48), channel_id=1, source_target_pairs={{64,1},{65,2},{66,3},{68,5},{69,6},{70,7},{72,9},{73,10},{74,11},{... | collective-permute-start | bytes 196616 | tf_op jit(solution)/shard_map/ppermute | solution.py:276
  63.3 71.8 %collective-permute-start.38 = (bf16[64,512]{1,0:T(8,128)(2,1)S(1)}, bf16[64,512]{1,0:T(8,128)(2,1)S(1)}, u32[]{:S(2)}, u32[]{:S(2)}) collective-permute-start(bf16[64,512]{1,0:T(8,128)(2,1)S(1)} %get-tuple-element.49), channel_id=1, source_target_pairs={{65,0},{66,1},{67,2},{69,4},{70,5},{71,6},{73,8},{74,9},{75,10},{7... | collective-permute-start | bytes 196616 | tf_op jit(solution)/shard_map/ppermute | solution.py:276
  125.0 10.8 %collective-permute-start.41 = (bf16[64,512]{1,0:T(8,128)(2,1)S(1)}, bf16[64,512]{1,0:T(8,128)(2,1)S(1)}, u32[]{:S(2)}, u32[]{:S(2)}) collective-permute-start(bf16[64,512]{1,0:T(8,128)(2,1)S(1)} %collective-permute-done.36.refs_1_), channel_id=1, source_target_pairs={{4,8},{5,9},{6,10},{7,11},{8,4},{9,5},{10,6},{11,7},{12,16},{13,17... | collective-permute-start | bytes 196616 | tf_op jit(solution)/shard_map/ppermute | solution.py:276
  125.6 19.6 %collective-permute-start.40 = (bf16[128,512]{1,0:T(8,128)(2,1)S(1)}, bf16[128,512]{1,0:T(8,128)(2,1)S(1)}, u32[]{:S(2)}, u32[]{:S(2)}) collective-permute-start(bf16[128,512]{1,0:T(8,128)(2,1)S(1)} %collective-permute-done.34.refs_0_.g_ref.refs_16_), channel_id=1, source_target_pairs={{4,8},{5,9},{6,10},{7,11},{8,4},{9,5},{10,6},{11,7},{12,16},{13,17... | collective-permute-start | bytes 393224 | tf_op jit(solution)/shard_map/ppermute | solution.py:276
  126.3 19.0 %collective-permute-start.35 = (bf16[128,512]{1,0:T(8,128)(2,1)S(1)}, bf16[128,512]{1,0:T(8,128)(2,1)S(1)}, u32[]{:S(2)}, u32[]{:S(2)}) collective-permute-start(bf16[128,512]{1,0:T(8,128)(2,1)S(1)} %collective-permute-done.34.refs_0_.g_ref.refs_16_), channel_id=1, source_target_pairs={{0,4},{1,5},{2,6},{3,7},{4,0},{5,1},{6,2},{7,3},{8,12},{9,13},{10,... | collective-permute-start | bytes 393224 | tf_op jit(solution)/shard_map/ppermute | solution.py:276
  133.2 12.1 %collective-permute-start.37 = (bf16[64,512]{1,0:T(8,128)(2,1)S(1)}, bf16[64,512]{1,0:T(8,128)(2,1)S(1)}, u32[]{:S(2)}, u32[]{:S(2)}) collective-permute-start(bf16[64,512]{1,0:T(8,128)(2,1)S(1)} %collective-permute-done.36.refs_1_), channel_id=1, source_target_pairs={{0,4},{1,5},{2,6},{3,7},{4,0},{5,1},{6,2},{7,3},{8,12},{9,13},{10,... | collective-permute-start | bytes 196616 | tf_op jit(solution)/shard_map/ppermute | solution.py:276
  135.1 10.2 %collective-permute-start.42 = (bf16[64,512]{1,0:T(8,128)(2,1)S(1)}, bf16[64,512]{1,0:T(8,128)(2,1)S(1)}, u32[]{:S(2)}, u32[]{:S(2)}) collective-permute-start(bf16[64,512]{1,0:T(8,128)(2,1)S(1)} %collective-permute-done.38.refs_2_), channel_id=1, source_target_pairs={{4,8},{5,9},{6,10},{7,11},{8,4},{9,5},{10,6},{11,7},{12,16},{13,17... | collective-permute-start | bytes 196616 | tf_op jit(solution)/shard_map/ppermute | solution.py:276
  135.8 9.5 %collective-permute-start.39 = (bf16[64,512]{1,0:T(8,128)(2,1)S(1)}, bf16[64,512]{1,0:T(8,128)(2,1)S(1)}, u32[]{:S(2)}, u32[]{:S(2)}) collective-permute-start(bf16[64,512]{1,0:T(8,128)(2,1)S(1)} %collective-permute-done.38.refs_2_), channel_id=1, source_target_pairs={{0,4},{1,5},{2,6},{3,7},{4,0},{5,1},{6,2},{7,3},{8,12},{9,13},{10,... | collective-permute-start | bytes 196616 | tf_op jit(solution)/shard_map/ppermute | solution.py:276
  152.7 31.6 %collective-permute-start.44 = (bf16[64,2048]{1,0:T(8,128)(2,1)S(1)}, bf16[64,2048]{1,0:T(8,128)(2,1)S(1)}, u32[]{:S(2)}, u32[]{:S(2)}) collective-permute-start(bf16[64,2048]{1,0:T(8,128)(2,1)S(1)} %get-tuple-element.58), channel_id=1, source_target_pairs={{0,1},{1,2},{2,3},{3,0},{4,5},{5,6},{6,7},{7,4},{8,9},{9,10},{10,1... | collective-permute-start | bytes 786440 | tf_op jit(solution)/shard_map/ppermute | solution.py:356
  160.7 23.7 %collective-permute-start.45 = (bf16[64,2048]{1,0:T(8,128)(2,1)S(1)}, bf16[64,2048]{1,0:T(8,128)(2,1)S(1)}, u32[]{:S(2)}, u32[]{:S(2)}) collective-permute-start(bf16[64,2048]{1,0:T(8,128)(2,1)S(1)} %get-tuple-element.59), channel_id=1, source_target_pairs={{0,2},{1,3},{2,0},{3,1},{4,6},{5,7},{6,4},{7,5},{8,10},{9,11},{10,... | collective-permute-start | bytes 786440 | tf_op jit(solution)/shard_map/ppermute | solution.py:356
  172.5 18.8 %collective-permute-start.46 = (bf16[64,2048]{1,0:T(8,128)(2,1)S(1)}, bf16[64,2048]{1,0:T(8,128)(2,1)S(1)}, u32[]{:S(2)}, u32[]{:S(2)}) collective-permute-start(bf16[64,2048]{1,0:T(8,128)(2,1)S(1)} %get-tuple-element.60), channel_id=1, source_target_pairs={{0,3},{1,0},{2,1},{3,2},{4,7},{5,4},{6,5},{7,6},{8,11},{9,8},{10,9... | collective-permute-start | bytes 786440 | tf_op jit(solution)/shard_map/ppermute | solution.py:356
  (27 other events, 119.9 us)

commit v3 on v1

--- a/solution.py
+++ b/solution.py
@@ -60,17 +60,27 @@
 
 def window(where_ref, keys_own):
     row0, col0, core, rows, cols = (where_ref[i] for i in range(5))
-    own = lax.broadcasted_iota(jnp.int32, (TOK, REGION), 0)
-    reach_row, reach_col = place(lax.broadcasted_iota(jnp.int32, (TOK, REGION), 1), core)
-    step_row, step_col = reach_row - (own >> 4), reach_col - (own & 15)
+    own = lax.broadcasted_iota(jnp.int32, (TOK, 1), 0)
+    reach_row, reach_col = place(lax.broadcasted_iota(jnp.int32, (1, REGION), 1), core)
+    grid_row, grid_col = row0 + reach_row, col0 + reach_col
+    inside = (grid_row >= 0) & (grid_row < rows) & (grid_col >= 0) & (grid_col < cols)
+    reach_row = jnp.where(inside, reach_row, 1 << 20)
     if keys_own:
-        step_row, step_col = -step_row, -step_col
-    ok = (step_row >= -8) & (step_row <= 7) & (step_col >= -8) & (step_col <= 7)
-    grid_row, grid_col = row0 + reach_row, col0 + reach_col
-    return ok & (grid_row >= 0) & (grid_row < rows) & (grid_col >= 0) & (grid_col < cols)
-
-
-def forward_kernel(where_ref, x0, x1, x2, w_ref, proj_ref, prob_ref, pack_ref, nlow_ref):
+        step_row, step_col = (own >> 4) - reach_row, (own & 15) - reach_col
+    else:
+        step_row, step_col = reach_row - (own >> 4), reach_col - (own & 15)
+    return (step_row >= -8) & (step_row <= 7) & (step_col >= -8) & (step_col <= 7)
+
+
+def put_sides(block, left_ref, right_ref):
+    sides = block.reshape(8, 2, 8, block.shape[-1])
+    left_ref[...] = sides[:, 0].reshape(64, -1).astype(BF16)
+    right_ref[...] = sides[:, 1].reshape(64, -1).astype(BF16)
+
+
+def forward_kernel(
+    where_ref, x0, x1, x2, w_ref, cot_ref, proj_ref, prob_ref, nlow_ref, pack_ref, left_ref, right_ref
+):
     for piece, x_ref in enumerate((x0, x1, x2)):
         x = x_ref[...].astype(F32)
         inverse = lax.rsqrt(jnp.mean(x * x, axis=-1, keepdims=True) + 1e-06)
@@ -84,8 +94,8 @@
     stats = jnp.zeros((TOK, 128), F32)
     for pair in range(PAIRS):
         at = slice(128 * pair, 128 * pair + 128)
-        query = two_heads(proj_ref[:TOK, at])
-        scores = nt(query, proj_ref[:, D + 128 * pair : D + 128 * pair + 128]) * 0.125
+        query = two_heads(proj_ref[:TOK, at] * 0.125)
+        scores = nt(query, proj_ref[:, D + 128 * pair : D + 128 * pair + 128])
         scores = jnp.where(ok2, scores, -1e30)
         highest = jnp.max(scores, axis=-1, keepdims=True)
         grown = jnp.exp(scores - highest)
@@ -102,7 +112,9 @@
             for head in range(2):
                 chosen = lane == 8 * part + 2 * pair + head
                 stats = jnp.where(chosen, piece[TOK * head : TOK * head + TOK], stats)
-    pack_ref[:, D:] = stats.astype(BF16)
+    pack_ref[:, D : D + 128] = stats.astype(BF16)
+    pack_ref[:, D + 128 :] = cot_ref[...].astype(BF16)
+    put_sides(pack_ref[...].astype(F32), left_ref, right_ref)
 
 
 def key_probs_kernel(where_ref, p0, p1, p2, proj_ref, prob_ref):
@@ -110,12 +122,12 @@
     lane = lax.broadcasted_iota(jnp.int32, (8, 128), 1)
     chosen = ((lane & 7) == head) & (lane < 24)
     pick = jnp.where(chosen, 1.0, 0.0).astype(BF16)
-    stats = jnp.concatenate([p[:, D:] for p in (p0, p1, p2)], axis=0)
+    stats = jnp.concatenate([p[:, D : D + 128] for p in (p0, p1, p2)], axis=0)
     log_total = nt(pick, stats)
     ok = window(where_ref, True)
     for pair in range(PAIRS):
-        key = two_heads(proj_ref[:TOK, D + 128 * pair : D + 128 * pair + 128])
-        scores = nt(key, proj_ref[:, 128 * pair : 128 * pair + 128]) * 0.125
+        key = two_heads(proj_ref[:TOK, D + 128 * pair : D + 128 * pair + 128] * 0.125)
+        scores = nt(key, proj_ref[:, 128 * pair : 128 * pair + 128])
         for side in range(2):
             at = 2 * pair + side
             part = scores[TOK * side : TOK * side + TOK] - log_total[at : at + 1]
@@ -149,8 +161,9 @@
 def key_kernel(
     where_ref, g_ref, g0, g1, g2, wo_ref, p0, p1, p2, proj_ref, prob_ref, dq_ref, wq_ref, x_ref,
     in_prev, dp_prev, gl_prev,
-    left_ref, right_ref, low_ref, in_ref, dp_ref, gl_ref, dm_ref, *, turn,
+    in_ref, dp_ref, gl_ref, *rest, turn,
 ):
+    sends, dm_ref = rest[:-1], rest[-1]
     active = where_ref[5] == turn
 
     @pl.when(jnp.logical_not(active))
@@ -166,7 +179,7 @@
         pick = jnp.where((lane >> 6) == head, 1.0, 0.0).astype(BF16)
         deltas = []
         for piece, (g, p) in enumerate(((g0, p0), (g1, p1), (g2, p2))):
-            d_mixed = nt(g[...], wo_ref[...]).astype(BF16)
+            d_mixed = nt(g[:, -D:], wo_ref[...]).astype(BF16)
             dm_ref[piece * OWN : (piece + 1) * OWN] = d_mixed
             prod = d_mixed.astype(F32) * p[:, :D].astype(F32)
             high = prod.astype(BF16)
@@ -199,17 +212,18 @@
         gradient = g_ref[...].astype(F32)
         out = gradient + inverse * (d_normed - normed * inner)
         in_ref[...] = out
-        gl_ref[...] = g_ref[...].astype(BF16)
-        low_ref[...] = out.astype(BF16)
-        sides = out.reshape(8, 2, 8, D)
-        left_ref[...] = sides[:, 0].reshape(64, D).astype(BF16)
-        right_ref[...] = sides[:, 1].reshape(64, D).astype(BF16)
-
-
-def weight_kernel(where_ref, n_ref, d0, d1, m0, m1, g0, g1, out_ref, full_ref):
+        gl_ref[:TOK] = g_ref[...].astype(BF16)
+        gl_ref[TOK:] = g1[:TOK, -D:]
+        if sends:
+            low_ref, left_ref, right_ref = sends
+            low_ref[...] = out.astype(BF16)
+            put_sides(out, left_ref, right_ref)
+
+
+def weight_kernel(where_ref, n_ref, d0, d1, m0, m1, g_ref, out_ref, full_ref):
     core = where_ref[2]
     full_ref[:, : 3 * D] = tn(n_ref[:TOK], d0[...]) + tn(n_ref[TOK:], d1[...])
-    full_ref[:, 3 * D :] = tn(m0[...], g0[...]) + tn(m1[...], g1[...])
+    full_ref[:, 3 * D :] = tn(m0[:, :D], g_ref[:TOK]) + tn(m1[:TOK, :D], g_ref[TOK:])
     chips, cols = out_ref.shape[1] // 8, out_ref.shape[0]
     for col in range(cols):
         rows = [
@@ -217,6 +231,14 @@
             for chip in range(chips)
         ]
         out_ref[col] = jnp.concatenate(rows, axis=0).astype(BF16)
+
+
+def total_kernel(where_ref, part_ref, qkv_ref, out_ref, *, scale):
+    total = part_ref[0].astype(F32)
+    for source in range(1, part_ref.shape[0]):
+        total = total + part_ref[source].astype(F32)
+    qkv_ref[...] = total[:, : 3 * D] * scale
+    out_ref[...] = total[:, 3 * D :] * scale
 
 
 def call(kernel, outs, *args, scratch=(), flops=0):
@@ -249,23 +271,18 @@
                             pairs.append((source, (p2 * 2 * chips + r2) * cols + c2))
         return lax.ppermute(block, AXES, pairs)
 
-    def halves(block):
-        shaped = block.reshape(8, 2, 8, block.shape[-1])
-        return shaped[:, 0].reshape(64, -1), shaped[:, 1].reshape(64, -1)
-
     def col_rims(left_half, right_half, down=0, plane=None):
         left = routed(right_half, lambda p, r, c: (p - down, r, c + 1), plane)
         right = routed(left_half, lambda p, r, c: (p - down, r, c - 1), plane)
         return left, right
 
-    def row_rims(own, plane=None):
-        mate = routed(own, lambda p, r, c: (p, r ^ 1, c), plane)
+    def mate(p, r, c):
+        return p, r ^ 1, c
+
+    def row_rims(pieces, plane=None):
+        own = jnp.concatenate(pieces, axis=0)
         beyond = routed(own, lambda p, r, c: (p, r - 1 + 2 * (r & 1), c), plane)
-        return own, mate, beyond
-
-    def spread(block, plane=None):
-        left, right = col_rims(*halves(block), plane=plane)
-        return row_rims(jnp.concatenate([block, left, right], axis=0), plane)
+        return own, routed(own, mate, plane), beyond
 
     pipe, z, core, col = (lax.axis_index(axis) for axis in AXES)
     x = activations.reshape(TOK, D)
@@ -276,52 +293,54 @@
         [8 * (2 * z + core), 16 * col, core, row_total, col_total, pipes - 1 - pipe]
     ).astype(jnp.int32)
 
-    xs = spread(x)
-    gs = spread(cot.astype(BF16), pipes - 1)
-    proj, q_probs, pack, nlow = call(
+    x_sides = x.reshape(8, 2, 8, D)
+    xs = row_rims([x, *col_rims(x_sides[:, 0].reshape(64, D), x_sides[:, 1].reshape(64, D))])
+    wide = 2 * D + 128
+    proj, q_probs, nlow, pack, low_side, high_side = call(
         forward_kernel,
-        [((REGION, 3 * D), BF16), ((PAIRS, OWN, REGION), BF16), ((TOK, D + 128), BF16), ((OWN, D), BF16)],
-        where, *xs, w_qkv, flops=2 << 30,
-    )
-    packs = spread(pack)
+        [((REGION, 3 * D), BF16), ((PAIRS, OWN, REGION), BF16), ((OWN, D), BF16),
+         ((TOK, wide), BF16), ((64, wide), BF16), ((64, wide), BF16)],
+        where, *xs, w_qkv, cot, flops=2 << 30,
+    )
+    packs = row_rims([pack, *col_rims(low_side, high_side)])
     (k_probs,) = call(
         key_probs_kernel, [((PAIRS, OWN, REGION), BF16)], where, *packs, proj, flops=1 << 28
     )
     d_in = jnp.zeros((TOK, D), F32)
     d_proj = jnp.zeros((TOK, 3 * D), BF16)
-    g_low = jnp.zeros((TOK, D), BF16)
-    gradient = cot
+    g_low = jnp.zeros((OWN, D), BF16)
+    gradient, gs = cot, packs
     for turn in range(pipes):
-        plane = pipes - 1 - turn
+        plane, last = pipes - 1 - turn, turn == pipes - 1
         if turn > 0:
-            centre = routed(low, lambda p, r, c: (p - 1, r, c), plane + 1)
-            left, right = col_rims(left_half, right_half, 1, plane + 1)
-            gs = row_rims(jnp.concatenate([centre, left, right], axis=0), plane)
-            gradient = centre
+            low, low_side, high_side = sends
+            gradient = routed(low, lambda p, r, c: (p - 1, r, c), plane + 1)
+            gs = row_rims([gradient, *col_rims(low_side, high_side, 1, plane + 1)], plane)
         (d_query,) = call(
             functools.partial(query_kernel, turn=turn), [((TOK, D), BF16)],
             where, gradient, w_out, pack, proj, q_probs, flops=1 << 29,
         )
-        left_half, right_half, low, d_in, d_proj, g_low = call(
+        halves = [((TOK, D), BF16), ((64, D), BF16), ((64, D), BF16)]
+        d_in, d_proj, g_low, *sends = call(
             functools.partial(key_kernel, turn=turn),
-            [((64, D), BF16), ((64, D), BF16), ((TOK, D), BF16), ((TOK, D), F32),
-             ((TOK, 3 * D), BF16), ((TOK, D), BF16)],
+            [((TOK, D), F32), ((TOK, 3 * D), BF16), ((OWN, D), BF16)] + ([] if last else halves),
             where, gradient, *gs, w_out, *packs, proj, k_probs, d_query, w_qkv, x,
             d_in, d_proj, g_low,
             scratch=[pltpu.VMEM((REGION, D), BF16)], flops=1 << 30,
         )
-    swap = lambda p, r, c: (p, r ^ 1, c)
     (part,) = call(
         weight_kernel, [((cols, 8 * chips, 4 * D), BF16)],
-        where, nlow, d_proj, routed(d_proj, swap), pack[:, :D], packs[1][:TOK, :D],
-        g_low, routed(g_low, swap),
+        where, nlow, d_proj, routed(d_proj, mate), pack, packs[1], g_low,
         scratch=[pltpu.VMEM((D, 4 * D), F32)], flops=1 << 30,
     )
     part = lax.all_to_all(part, "col", 0, 0, tiled=True)
     part = jnp.sum(part.astype(F32), axis=0).astype(BF16).reshape(chips, 8, 4 * D)
     part = lax.all_to_all(part, "z", 0, 0, tiled=True)
-    part = jnp.sum(part.astype(F32), axis=0) * (row_total * col_total) ** (-0.5)
-    return d_in.reshape(1, 8, 16, D), part[None, :, : 3 * D], part[None, :, 3 * D :]
+    qkv_part, out_part = call(
+        functools.partial(total_kernel, scale=(row_total * col_total) ** (-0.5)),
+        [((8, 3 * D), F32), ((8, D), F32)], where, part,
+    )
+    return d_in.reshape(1, 8, 16, D), qkv_part[None], out_part[None]
 
 
 def solution(mesh):

time: 167 us -> 160 us (0.958)
  starting transfers between devices: 46.7 us -> 39.2 us
    ppermute x29 -> x24, starting transfers between devices: 46.7 us -> 39.2 us  [routed(): return lax.ppermute(block, AXES, pairs)]
    unnamed x16 -> x20, local copies, waits for them, and re-layouts: 0.1 us -> 2.47 us
    pallas_call x11 -> x12, Pallas kernels: 18.3 us -> 19 us  [call(): pl.pallas_call(kernel, out_shape=[jax.ShapeDtypeStruct(s, t) for s, t in...]
    ppermute x29 -> x24, waiting for transfers between devices: 53.9 us -> 54.3 us  [routed(): return lax.ppermute(block, AXES, pairs)]
  transfers between devices with their start and end apart: 29 -> 24, of which waited for: 7 -> 9; matrix products, arithmetic and copies ran while one was open for 1% -> 0% of each run, Pallas kernels for 6% -> 2%
where the time goes in v3:
time: 160 us; the launch traced here: 158 us
  waiting for transfers between devices  54.3 us (34%)
  blocking collectives  40 us (25%)
  starting transfers between devices  39.2 us (25%)
  Pallas kernels  19 us (12%)
  local copies, waits for them, and re-layouts  3.54 us (2%)
    ppermute x24, waiting for transfers between devices, routed(): return lax.ppermute(block, AXES, pairs)  54.3 us
    ppermute x24, starting transfers between devices, routed(): return lax.ppermute(block, AXES, pairs)  39.2 us
    all_to_all x1, blocking collectives, body(): part = lax.all_to_all(part, 'col', 0, 0, tiled=True)  20.7 us
    all_to_all x1, blocking collectives, body(): part = lax.all_to_all(part, 'z', 0, 0, tiled=True)  19.3 us
    pallas_call x12, Pallas kernels, call(): pl.pallas_call(kernel, out_shape=[jax.ShapeDtypeStruct(s, t) for s, t in...  19 us
  transfers between devices with their start and end apart: 24, of which 9 were waited for; matrix products, arithmetic and copies ran while one was open for 0% of the time, Pallas kernels for 2%

profile of v3, /device:TPU:6, one launch (start us, length us, event | category | flops | bytes accessed | tf_op | source)
XLA Modules:
  0.0 158.2 jit_solution(11468194308709077938)
XLA Ops:
  1.5 1.3 collective-permute-start
  2.8 4.5 %collective-permute-start.1 = (bf16[64,512]{1,0:T(8,128)(2,1)S(1)}, bf16[64,512]{1,0:T(8,128)(2,1)S(1)}, u32[]{:S(2)}, u32[]{:S(2)}) collective-permute-start(bf16[64,512]{1,0:T(8,128)(2,1)S(1)} %get-tuple-element.62), channel_id=1, source_target_pairs={{1,0},{2,1},{3,2},{5,4},{6,5},{7,6},{9,8},{10,9},{11,10},{13,12},{... | collective-permute-start | bytes 196616 | tf_op jit(solution)/shard_map/ppermute | solution.py:272
  7.7 1.6 collective-permute-done.1
  10.9 3.4 %collective-permute-start.2 = (bf16[256,512]{1,0:T(8,128)(2,1)S(1)}, bf16[256,512]{1,0:T(8,128)(2,1)S(1)}, u32[]{:S(2)}, u32[]{:S(2)}) collective-permute-start(bf16[256,512]{1,0:T(8,128)(2,1)S(1)} %pad_maximum_fusion.x0), channel_id=1, source_target_pairs={{0,4},{1,5},{2,6},{3,7},{4,0},{5,1},{6,2},{7,3},{8,12},{9,13},{10,... | collective-permute-start | bytes 786440 | tf_op jit(solution)/shard_map/ppermute | solution.py:272
  15.4 1.4 copy-done.1
  17.7 4.5 %shard_map.67 = (bf16[768,1536]{1,0:T(8,128)(2,1)S(1)}, bf16[4,256,768]{2,1,0:T(8,128)(2,1)S(1)}, bf16[256,512]{1,0:T(8,128)(2,1)S(1)}, bf16[128,1152]{1,0:T(8,1...) custom-call(s32[6]{0:T(128)S(1)} %stack.19.where_ref, bf16[256,512]{1,0:T(8,128)(2,1)S(1)} %pad_maximum_fusion.x0, ...), custom_call_target="tpu_custom_call" | custom-call | flops 2147483648 | bytes 4194304 | tf_op jit(solution)/shard_map/pallas_call | solution.py:246
  22.2 1.3 collective-permute-start.4
  23.5 4.9 %collective-permute-start.5 = (bf16[64,1152]{1,0:T(8,128)(2,1)S(1)}, bf16[64,1152]{1,0:T(8,128)(2,1)S(1)}, u32[]{:S(2)}, u32[]{:S(2)}) collective-permute-start(bf16[64,1152]{1,0:T(8,128)(2,1)S(1)} %get-tuple-element.34), channel_id=1, source_target_pairs={{1,0},{2,1},{3,2},{5,4},{6,5},{7,6},{9,8},{10,9},{11,10},{13,12},{... | collective-permute-start | bytes 442376 | tf_op jit(solution)/shard_map/ppermute | solution.py:272
  28.5 1.1 collective-permute-done.4
  29.6 1.5 collective-permute-done.5
  31.8 6.7 %collective-permute-start.6 = (bf16[256,1152]{1,0:T(8,128)(2,1)S(1)}, bf16[256,1152]{1,0:T(8,128)(2,1)S(1)}, u32[]{:S(2)}, u32[]{:S(2)}) collective-permute-start(bf16[256,1152]{1,0:T(8,128)(2,1)S(1)} %constant_dynamic-update-slice_fusion.p0.g0), channel_id=1, source_target_pairs={{0,4},{1,5},{2,6},{3,7},{4,0},{5,1},{6,2},{7,3},{8,12},{9,13},{10,... | collective-permute-start | bytes 1769480 | tf_op jit(solution)/shard_map/ppermute | solution.py:272
  40.2 1.5 shard_map.68.prob_ref
  51.9 1.3 collective-permute-start.18
  53.2 1.3 collective-permute-start.19
  55.2 43.2 %collective-permute-done.18.g_ref = bf16[128,512]{1,0:T(8,128)(2,1)S(1)} collective-permute-done((bf16[128,512]{1,0:T(8,128)(2,1)S(1)}, bf16[128,512]{1,0:T(8,128)(2,1)S(1)}, u32[]{:S(2)}, u32[]{:S(2)}) %collective-permute-start.18) | collective-permute-done | bytes 131104 | tf_op jit(solution)/shard_map/ppermute | solution.py:272
  98.5 2.8 %collective-permute-done.19 = bf16[64,512]{1,0:T(8,128)(2,1)S(1)} collective-permute-done((bf16[64,512]{1,0:T(8,128)(2,1)S(1)}, bf16[64,512]{1,0:T(8,128)(2,1)S(1)}, u32[]{:S(2)}, u32[]{:S(2)}) %collective-permute-start.19) | collective-permute-done | bytes 65568 | tf_op jit(solution)/shard_map/ppermute | solution.py:272
  101.9 5.0 %collective-permute-start.21 = (bf16[256,512]{1,0:T(8,128)(2,1)S(1)}, bf16[256,512]{1,0:T(8,128)(2,1)S(1)}, u32[]{:S(2)}, u32[]{:S(2)}) collective-permute-start(bf16[256,512]{1,0:T(8,128)(2,1)S(1)} %constant_dynamic-update-slice_fusion.9.g0), channel_id=1, source_target_pairs={{0,4},{1,5},{2,6},{3,7},{4,0},{5,1},{6,2},{7,3},{8,12},{9,13},{10,... | collective-permute-start | bytes 786440 | tf_op jit(solution)/shard_map/ppermute | solution.py:272
  106.9 2.0 %shard_map.75.dq_ref = bf16[128,512]{1,0:T(8,128)(2,1)S(1)} custom-call(s32[6]{0:T(128)S(1)} %stack.19.where_ref, bf16[128,512]{1,0:T(8,128)(2,1)S(1)} %collective-permute-done.18.g_ref, bf16[512,512]{1,0:T(8,128)(2,1)S(1)} %bitcast.27, bf16[128,1152]{1,0:T(8,128)(2,1)S(1)} %get-tuple-element.32.pack_ref.m0, ...), custom_call_target="tpu_custom_call" | custom-call | flops 536870912 | bytes 4194304 | tf_op jit(solution)/shard_map/pallas_call | solution.py:246
  109.0 4.2 %shard_map.76 = (f32[128,512]{1,0:T(8,128)}, bf16[128,1536]{1,0:T(8,128)(2,1)S(1)}, bf16[256,512]{1,0:T(8,128)(2,1)S(1)}) custom-call(s32[6]{0:T(128)S(1)} %stack.19.where_ref, bf16[128,512]{1,0:T(8,128)(2,1)S(1)} %collective-permute-done.18.g_ref, bf16[256,512]{1,0:T(8,128)(2,1)S(1)} %constant_dynamic-update-slice_fusion.9.g0, ...), custom_call_target="tpu_custom_call" | custom-call | flops 1073741824 | bytes 4194304 | tf_op jit(solution)/shard_map/pallas_call | solution.py:246
  113.3 1.6 %collective-permute-done.23.d1 = bf16[128,1536]{1,0:T(8,128)(2,1)S(1)} collective-permute-done((bf16[128,1536]{1,0:T(8,128)(2,1)S(1)}, bf16[128,1536]{1,0:T(8,128)(2,1)S(1)}, u32[]{:S(2)}, u32[]{:S(2)}) %collective-permute-start.23) | collective-permute-done | bytes 393248 | tf_op jit(solution)/shard_map/ppermute | solution.py:272
  114.9 1.9 %shard_map.77 = bf16[4,64,2048]{2,1,0:T(8,128)(2,1)S(1)} custom-call(s32[6]{0:T(128)S(1)} %stack.19.where_ref, bf16[256,512]{1,0:T(8,128)(2,1)S(1)} %get-tuple-element.56.n_ref, bf16[128,1536]{1,0:T(8,128)(2,1)S(1)} %get-tuple-element.57.d0, bf16[128,1536]{1,0:T(8,128)(2,1)S(1)} %collective-permute-done.23.d1, ...), custom_call_target="tpu_custom_call" | custom-call | flops 1073741824 | bytes 4194304 | tf_op jit(solution)/shard_map/pallas_call | solution.py:246
  116.8 20.7 %all_to_all.10 = bf16[4,64,2048]{2,1,0:T(8,128)(2,1)S(1)} all-to-all(bf16[4,64,2048]{2,1,0:T(8,128)(2,1)S(1)} %shard_map.77), channel_id=1, replica_groups=mesh['pipe'=4,'z'=8,'core'=2,'col'=4] {'col'}, dimensions={0} | all-to-all | bytes 2097152 | tf_op jit(solution)/shard_map/all_to_all | solution.py:336
  137.8 19.3 %all_to_all.11.part_ref = bf16[8,8,2048]{2,1,0:T(8,128)(2,1)S(1)} all-to-all(bf16[8,8,2048]{2,1,0:T(8,128)(2,1)S(1)} %bitcast.43), channel_id=1, replica_groups=mesh['pipe'=4,'z'=8,'core'=2,'col'=4] {'z'}, dimensions={0} | all-to-all | bytes 524288 | tf_op jit(solution)/shard_map/all_to_all | solution.py:338
  157.0 1.2 shard_map.78
  (69 shorter events, 18.9 us)
Async XLA Ops:
  1.5 6.2 %collective-permute-start = (bf16[64,512]{1,0:T(8,128)(2,1)S(1)}, bf16[64,512]{1,0:T(8,128)(2,1)S(1)}, u32[]{:S(2)}, u32[]{:S(2)}) collective-permute-start(bf16[64,512]{1,0:T(8,128)(2,1)S(1)} %get-tuple-element.61), channel_id=1, source_target_pairs={{0,1},{1,2},{2,3},{4,5},{5,6},{6,7},{8,9},{9,10},{10,11},{12,13},{... | collective-permute-start | bytes 196616 | tf_op jit(solution)/shard_map/ppermute | solution.py:272
  2.8 6.4 %collective-permute-start.1 = (bf16[64,512]{1,0:T(8,128)(2,1)S(1)}, bf16[64,512]{1,0:T(8,128)(2,1)S(1)}, u32[]{:S(2)}, u32[]{:S(2)}) collective-permute-start(bf16[64,512]{1,0:T(8,128)(2,1)S(1)} %get-tuple-element.62), channel_id=1, source_target_pairs={{1,0},{2,1},{3,2},{5,4},{6,5},{7,6},{9,8},{10,9},{11,10},{13,12},{... | collective-permute-start | bytes 196616 | tf_op jit(solution)/shard_map/ppermute | solution.py:272
  10.2 4.1 %collective-permute-start.3 = (bf16[256,512]{1,0:T(8,128)(2,1)S(1)}, bf16[256,512]{1,0:T(8,128)(2,1)S(1)}, u32[]{:S(2)}, u32[]{:S(2)}) collective-permute-start(bf16[256,512]{1,0:T(8,128)(2,1)S(1)} %pad_maximum_fusion.x0), channel_id=1, source_target_pairs={{4,8},{5,9},{6,10},{7,11},{8,4},{9,5},{10,6},{11,7},{12,16},{13,17... | collective-permute-start | bytes 786440 | tf_op jit(solution)/shard_map/ppermute | solution.py:272
  10.9 4.5 %collective-permute-start.2 = (bf16[256,512]{1,0:T(8,128)(2,1)S(1)}, bf16[256,512]{1,0:T(8,128)(2,1)S(1)}, u32[]{:S(2)}, u32[]{:S(2)}) collective-permute-start(bf16[256,512]{1,0:T(8,128)(2,1)S(1)} %pad_maximum_fusion.x0), channel_id=1, source_target_pairs={{0,4},{1,5},{2,6},{3,7},{4,0},{5,1},{6,2},{7,3},{8,12},{9,13},{10,... | collective-permute-start | bytes 786440 | tf_op jit(solution)/shard_map/ppermute | solution.py:272
  22.2 7.4 %collective-permute-start.4 = (bf16[64,1152]{1,0:T(8,128)(2,1)S(1)}, bf16[64,1152]{1,0:T(8,128)(2,1)S(1)}, u32[]{:S(2)}, u32[]{:S(2)}) collective-permute-start(bf16[64,1152]{1,0:T(8,128)(2,1)S(1)} %get-tuple-element.33), channel_id=1, source_target_pairs={{0,1},{1,2},{2,3},{4,5},{5,6},{6,7},{8,9},{9,10},{10,11},{12,13},{... | collective-permute-start | bytes 442376 | tf_op jit(solution)/shard_map/ppermute | solution.py:272
  23.5 7.6 %collective-permute-start.5 = (bf16[64,1152]{1,0:T(8,128)(2,1)S(1)}, bf16[64,1152]{1,0:T(8,128)(2,1)S(1)}, u32[]{:S(2)}, u32[]{:S(2)}) collective-permute-start(bf16[64,1152]{1,0:T(8,128)(2,1)S(1)} %get-tuple-element.34), channel_id=1, source_target_pairs={{1,0},{2,1},{3,2},{5,4},{6,5},{7,6},{9,8},{10,9},{11,10},{13,12},{... | collective-permute-start | bytes 442376 | tf_op jit(solution)/shard_map/ppermute | solution.py:272
  31.1 8.0 %collective-permute-start.7 = (bf16[256,1152]{1,0:T(8,128)(2,1)S(1)}, bf16[256,1152]{1,0:T(8,128)(2,1)S(1)}, u32[]{:S(2)}, u32[]{:S(2)}) collective-permute-start(bf16[256,1152]{1,0:T(8,128)(2,1)S(1)} %constant_dynamic-update-slice_fusion.p0.g0), channel_id=1, source_target_pairs={{4,8},{5,9},{6,10},{7,11},{8,4},{9,5},{10,6},{11,7},{12,16},{13,17... | collective-permute-start | bytes 1769480 | tf_op jit(solution)/shard_map/ppermute | solution.py:272
  31.8 8.4 %collective-permute-start.6 = (bf16[256,1152]{1,0:T(8,128)(2,1)S(1)}, bf16[256,1152]{1,0:T(8,128)(2,1)S(1)}, u32[]{:S(2)}, u32[]{:S(2)}) collective-permute-start(bf16[256,1152]{1,0:T(8,128)(2,1)S(1)} %constant_dynamic-update-slice_fusion.p0.g0), channel_id=1, source_target_pairs={{0,4},{1,5},{2,6},{3,7},{4,0},{5,1},{6,2},{7,3},{8,12},{9,13},{10,... | collective-permute-start | bytes 1769480 | tf_op jit(solution)/shard_map/ppermute | solution.py:272
  42.4 2.0 %collective-permute-start.8 = (bf16[128,512]{1,0:T(8,128)(2,1)S(1)}, bf16[128,512]{1,0:T(8,128)(2,1)S(1)}, u32[]{:S(2)}, u32[]{:S(2)}) collective-permute-start(bf16[128,512]{1,0:T(8,128)(2,1)S(1)} %get-tuple-element.37), channel_id=1, source_target_pairs={{192,128},{193,129},{194,130},{195,131},{196,132},{197,133},{198,1... | collective-permute-start | bytes 393224 | tf_op jit(solution)/shard_map/ppermute | solution.py:272
  43.1 1.4 collective-permute-start.9
  43.7 0.7 collective-permute-start.10
  44.5 1.9 %collective-permute-start.12 = (bf16[256,512]{1,0:T(8,128)(2,1)S(1)}, bf16[256,512]{1,0:T(8,128)(2,1)S(1)}, u32[]{:S(2)}, u32[]{:S(2)}) collective-permute-start(bf16[256,512]{1,0:T(8,128)(2,1)S(1)} %constant_dynamic-update-slice_fusion.3.g0), channel_id=1, source_target_pairs={{132,136},{133,137},{134,138},{135,139},{136,132},{137,133},{138,1... | collective-permute-start | bytes 786440 | tf_op jit(solution)/shard_map/ppermute | solution.py:272
  45.2 1.3 collective-permute-start.11
  47.2 2.0 %collective-permute-start.13 = (bf16[128,512]{1,0:T(8,128)(2,1)S(1)}, bf16[128,512]{1,0:T(8,128)(2,1)S(1)}, u32[]{:S(2)}, u32[]{:S(2)}) collective-permute-start(bf16[128,512]{1,0:T(8,128)(2,1)S(1)} %get-tuple-element.43), channel_id=1, source_target_pairs={{128,64},{129,65},{130,66},{131,67},{132,68},{133,69},{134,70},{13... | collective-permute-start | bytes 393224 | tf_op jit(solution)/shard_map/ppermute | solution.py:272
  47.9 1.4 collective-permute-start.14
  48.6 0.7 collective-permute-start.15
  49.4 1.9 %collective-permute-start.17 = (bf16[256,512]{1,0:T(8,128)(2,1)S(1)}, bf16[256,512]{1,0:T(8,128)(2,1)S(1)}, u32[]{:S(2)}, u32[]{:S(2)}) collective-permute-start(bf16[256,512]{1,0:T(8,128)(2,1)S(1)} %constant_dynamic-update-slice_fusion.6.g0), channel_id=1, source_target_pairs={{68,72},{69,73},{70,74},{71,75},{72,68},{73,69},{74,70},{75,71},{7... | collective-permute-start | bytes 786440 | tf_op jit(solution)/shard_map/ppermute | solution.py:272
  50.0 1.3 collective-permute-start.16
  51.9 46.5 %collective-permute-start.18 = (bf16[128,512]{1,0:T(8,128)(2,1)S(1)}, bf16[128,512]{1,0:T(8,128)(2,1)S(1)}, u32[]{:S(2)}, u32[]{:S(2)}) collective-permute-start(bf16[128,512]{1,0:T(8,128)(2,1)S(1)} %get-tuple-element.49), channel_id=1, source_target_pairs={{64,0},{65,1},{66,2},{67,3},{68,4},{69,5},{70,6},{71,7},{72,8},{73... | collective-permute-start | bytes 393224 | tf_op jit(solution)/shard_map/ppermute | solution.py:272
  53.2 48.0 %collective-permute-start.19 = (bf16[64,512]{1,0:T(8,128)(2,1)S(1)}, bf16[64,512]{1,0:T(8,128)(2,1)S(1)}, u32[]{:S(2)}, u32[]{:S(2)}) collective-permute-start(bf16[64,512]{1,0:T(8,128)(2,1)S(1)} %get-tuple-element.50), channel_id=1, source_target_pairs={{64,1},{65,2},{66,3},{68,5},{69,6},{70,7},{72,9},{73,10},{74,11},{... | collective-permute-start | bytes 196616 | tf_op jit(solution)/shard_map/ppermute | solution.py:272
  54.5 46.7 %collective-permute-start.20 = (bf16[64,512]{1,0:T(8,128)(2,1)S(1)}, bf16[64,512]{1,0:T(8,128)(2,1)S(1)}, u32[]{:S(2)}, u32[]{:S(2)}) collective-permute-start(bf16[64,512]{1,0:T(8,128)(2,1)S(1)} %get-tuple-element.51), channel_id=1, source_target_pairs={{65,0},{66,1},{67,2},{69,4},{70,5},{71,6},{73,8},{74,9},{75,10},{7... | collective-permute-start | bytes 196616 | tf_op jit(solution)/shard_map/ppermute | solution.py:272
  101.3 7.7 %collective-permute-start.22 = (bf16[256,512]{1,0:T(8,128)(2,1)S(1)}, bf16[256,512]{1,0:T(8,128)(2,1)S(1)}, u32[]{:S(2)}, u32[]{:S(2)}) collective-permute-start(bf16[256,512]{1,0:T(8,128)(2,1)S(1)} %constant_dynamic-update-slice_fusion.9.g0), channel_id=1, source_target_pairs={{4,8},{5,9},{6,10},{7,11},{8,4},{9,5},{10,6},{11,7},{12,16},{13,17... | collective-permute-start | bytes 786440 | tf_op jit(solution)/shard_map/ppermute | solution.py:272
  101.9 7.0 %collective-permute-start.21 = (bf16[256,512]{1,0:T(8,128)(2,1)S(1)}, bf16[256,512]{1,0:T(8,128)(2,1)S(1)}, u32[]{:S(2)}, u32[]{:S(2)}) collective-permute-start(bf16[256,512]{1,0:T(8,128)(2,1)S(1)} %constant_dynamic-update-slice_fusion.9.g0), channel_id=1, source_target_pairs={{0,4},{1,5},{2,6},{3,7},{4,0},{5,1},{6,2},{7,3},{8,12},{9,13},{10,... | collective-permute-start | bytes 786440 | tf_op jit(solution)/shard_map/ppermute | solution.py:272
  113.2 1.7 %collective-permute-start.23 = (bf16[128,1536]{1,0:T(8,128)(2,1)S(1)}, bf16[128,1536]{1,0:T(8,128)(2,1)S(1)}, u32[]{:S(2)}, u32[]{:S(2)}) collective-permute-start(bf16[128,1536]{1,0:T(8,128)(2,1)S(1)} %get-tuple-element.57.d0), channel_id=1, source_target_pairs={{0,4},{1,5},{2,6},{3,7},{4,0},{5,1},{6,2},{7,3},{8,12},{9,13},{10,... | collective-permute-start | bytes 1179656 | tf_op jit(solution)/shard_map/ppermute | solution.py:272
  (6 other events, 30.0 us)

commit v4 on v3

--- a/solution.py
+++ b/solution.py
@@ -160,17 +160,18 @@
 
 def key_kernel(
     where_ref, g_ref, g0, g1, g2, wo_ref, p0, p1, p2, proj_ref, prob_ref, dq_ref, wq_ref, x_ref,
-    in_prev, dp_prev, gl_prev,
-    in_ref, dp_ref, gl_ref, *rest, turn,
+    *rest, turn,
 ):
-    sends, dm_ref = rest[:-1], rest[-1]
+    prev, rest = (rest[:3], rest[3:]) if turn else ((), rest)
+    (in_ref, dp_ref, gl_ref), sends, dm_ref = rest[:3], rest[3:-1], rest[-1]
     active = where_ref[5] == turn
 
-    @pl.when(jnp.logical_not(active))
-    def _():
-        in_ref[...] = in_prev[...]
-        dp_ref[...] = dp_prev[...]
-        gl_ref[...] = gl_prev[...]
+    if prev:
+
+        @pl.when(jnp.logical_not(active))
+        def _():
+            for new, old in zip((in_ref, dp_ref, gl_ref), prev):
+                new[...] = old[...]
 
     @pl.when(active)
     def _():
@@ -241,6 +242,29 @@
     out_ref[...] = total[:, 3 * D :] * scale
 
 
+def stage_kernel(*refs):
+    sources, targets, sems = refs[: len(refs) // 2], refs[len(refs) // 2 : -1], refs[-1]
+    copies = [
+        pltpu.make_async_copy(source, target, sems.at[at])
+        for at, (source, target) in enumerate(zip(sources, targets))
+    ]
+    for copy in copies:
+        copy.start()
+    for copy in copies:
+        copy.wait()
+
+
+def staged(*arrays):
+    return pl.pallas_call(
+        stage_kernel,
+        out_shape=[jax.ShapeDtypeStruct(a.shape, a.dtype) for a in arrays],
+        in_specs=[pl.BlockSpec(memory_space=pl.ANY)] * len(arrays),
+        out_specs=[pl.BlockSpec(memory_space=pltpu.VMEM)] * len(arrays),
+        scratch_shapes=[pltpu.SemaphoreType.DMA((len(arrays),))],
+        cost_estimate=pl.CostEstimate(flops=0, bytes_accessed=6 << 20, transcendentals=0),
+    )(*arrays)
+
+
 def call(kernel, outs, *args, scratch=(), flops=0):
     vmem = pl.BlockSpec(memory_space=pltpu.VMEM)
     return pl.pallas_call(
@@ -279,10 +303,13 @@
     def mate(p, r, c):
         return p, r ^ 1, c
 
-    def row_rims(pieces, plane=None):
+    def row_rims(pieces, plane=None, beside=None):
         own = jnp.concatenate(pieces, axis=0)
         beyond = routed(own, lambda p, r, c: (p, r - 1 + 2 * (r & 1), c), plane)
-        return own, routed(own, mate, plane), beyond
+        if beside is None:
+            return own, routed(own, mate, plane), beyond
+        late, done = lax.optimization_barrier((own, beside()))
+        return (own, routed(late, mate, plane), beyond), done
 
     pipe, z, core, col = (lax.axis_index(axis) for axis in AXES)
     x = activations.reshape(TOK, D)
@@ -295,6 +322,7 @@
 
     x_sides = x.reshape(8, 2, 8, D)
     xs = row_rims([x, *col_rims(x_sides[:, 0].reshape(64, D), x_sides[:, 1].reshape(64, D))])
+    x, cot, w_qkv, w_out = staged(x, cot, w_qkv, w_out)
     wide = 2 * D + 128
     proj, q_probs, nlow, pack, low_side, high_side = call(
         forward_kernel,
@@ -302,32 +330,40 @@
          ((TOK, wide), BF16), ((64, wide), BF16), ((64, wide), BF16)],
         where, *xs, w_qkv, cot, flops=2 << 30,
     )
-    packs = row_rims([pack, *col_rims(low_side, high_side)])
+
+    def query_side(turn, gradient):
+        return call(
+            functools.partial(query_kernel, turn=turn), [((TOK, D), BF16)],
+            where, gradient, w_out, pack, proj, q_probs, flops=1 << 29,
+        )[0]
+
+    gradient = cot
+    packs, d_query = row_rims(
+        [pack, *col_rims(low_side, high_side)], beside=lambda: query_side(0, cot)
+    )
+    gs = packs
     (k_probs,) = call(
         key_probs_kernel, [((PAIRS, OWN, REGION), BF16)], where, *packs, proj, flops=1 << 28
     )
-    d_in = jnp.zeros((TOK, D), F32)
-    d_proj = jnp.zeros((TOK, 3 * D), BF16)
-    g_low = jnp.zeros((OWN, D), BF16)
-    gradient, gs = cot, packs
+    state = ()
     for turn in range(pipes):
         plane, last = pipes - 1 - turn, turn == pipes - 1
         if turn > 0:
             low, low_side, high_side = sends
             gradient = routed(low, lambda p, r, c: (p - 1, r, c), plane + 1)
-            gs = row_rims([gradient, *col_rims(low_side, high_side, 1, plane + 1)], plane)
-        (d_query,) = call(
-            functools.partial(query_kernel, turn=turn), [((TOK, D), BF16)],
-            where, gradient, w_out, pack, proj, q_probs, flops=1 << 29,
-        )
+            sides = col_rims(low_side, high_side, 1, plane + 1)
+            gs, d_query = row_rims(
+                [gradient, *sides], plane, lambda: query_side(turn, gradient)
+            )
         halves = [((TOK, D), BF16), ((64, D), BF16), ((64, D), BF16)]
-        d_in, d_proj, g_low, *sends = call(
+        outs = call(
             functools.partial(key_kernel, turn=turn),
             [((TOK, D), F32), ((TOK, 3 * D), BF16), ((OWN, D), BF16)] + ([] if last else halves),
-            where, gradient, *gs, w_out, *packs, proj, k_probs, d_query, w_qkv, x,
-            d_in, d_proj, g_low,
+            where, gradient, *gs, w_out, *packs, proj, k_probs, d_query, w_qkv, x, *state,
             scratch=[pltpu.VMEM((REGION, D), BF16)], flops=1 << 30,
         )
+        state, sends = outs[:3], outs[3:]
+    d_in, d_proj, g_low = state
     (part,) = call(
         weight_kernel, [((cols, 8 * chips, 4 * D), BF16)],
         where, nlow, d_proj, routed(d_proj, mate), pack, packs[1], g_low,

time: 160 us -> 174 us (1.087)
  starting transfers between devices: 39.2 us -> 46.4 us
  Pallas kernels: 19 us -> 22 us
  waiting for transfers between devices: 54.3 us -> 56.4 us
  blocking collectives: 40 us -> 42 us
    ppermute x24, starting transfers between devices: 39.2 us -> 46.4 us  [routed(): return lax.ppermute(block, AXES, pairs)]
    pallas_call x0 -> x1, Pallas kernels: none -> 3.14 us  [staged(): pl.pallas_call(stage_kernel, out_shape=[jax.ShapeDtypeStruct(a.shape, a.d...]
    ppermute x24, waiting for transfers between devices: 54.3 us -> 56.4 us  [routed(): return lax.ppermute(block, AXES, pairs)]
    all_to_all x1, blocking collectives: 19.3 us -> 21.2 us  [body(): part = lax.all_to_all(part, 'z', 0, 0, tiled=True)]
  transfers between devices with their start and end apart: 24 -> 24, of which waited for: 9 -> 9; matrix products, arithmetic and copies ran while one was open for 0% -> 0% of each run, Pallas kernels for 2% -> 4%
where the time goes in v4:
time: 174 us; the launch traced here: 172 us
  waiting for transfers between devices  56.4 us (32%)
  starting transfers between devices  46.4 us (27%)
  blocking collectives  42 us (24%)
  Pallas kernels  22 us (13%)
  local copies, waits for them, and re-layouts  3.48 us (2%)
    ppermute x24, waiting for transfers between devices, routed(): return lax.ppermute(block, AXES, pairs)  56.4 us
    ppermute x24, starting transfers between devices, routed(): return lax.ppermute(block, AXES, pairs)  46.4 us
    all_to_all x1, blocking collectives, body(): part = lax.all_to_all(part, 'z', 0, 0, tiled=True)  21.2 us
    all_to_all x1, blocking collectives, body(): part = lax.all_to_all(part, 'col', 0, 0, tiled=True)  20.8 us
    pallas_call x12, Pallas kernels, call(): pl.pallas_call(kernel, out_shape=[jax.ShapeDtypeStruct(s, t) for s, t in...  18.9 us
  transfers between devices with their start and end apart: 24, of which 9 were waited for; matrix products, arithmetic and copies ran while one was open for 0% of the time, Pallas kernels for 4%

profile of v4, /device:TPU:6, one launch (start us, length us, event | category | flops | bytes accessed | tf_op | source)
XLA Modules:
  0.0 172.5 jit_solution(1582494965712861534)
XLA Ops:
  1.5 1.3 collective-permute-start
  2.8 4.5 %collective-permute-start.1 = (bf16[64,512]{1,0:T(8,128)(2,1)S(1)}, bf16[64,512]{1,0:T(8,128)(2,1)S(1)}, u32[]{:S(2)}, u32[]{:S(2)}) collective-permute-start(bf16[64,512]{1,0:T(8,128)(2,1)S(1)} %get-tuple-element.86), channel_id=1, source_target_pairs={{1,0},{2,1},{3,2},{5,4},{6,5},{7,6},{9,8},{10,9},{11,10},{13,12},{... | collective-permute-start | bytes 196616 | tf_op jit(solution)/shard_map/ppermute | solution.py:296
  7.7 1.6 collective-permute-done.1
  10.9 3.4 %collective-permute-start.2 = (bf16[256,512]{1,0:T(8,128)(2,1)S(1)}, bf16[256,512]{1,0:T(8,128)(2,1)S(1)}, u32[]{:S(2)}, u32[]{:S(2)}) collective-permute-start(bf16[256,512]{1,0:T(8,128)(2,1)S(1)} %pad_maximum_fusion.x0), channel_id=1, source_target_pairs={{0,4},{1,5},{2,6},{3,7},{4,0},{5,1},{6,2},{7,3},{8,12},{9,13},{10,... | collective-permute-start | bytes 786440 | tf_op jit(solution)/shard_map/ppermute | solution.py:296
  14.2 3.1 %shard_map.67 = (bf16[128,512]{1,0:T(8,128)(2,1)}, f32[128,512]{1,0:T(8,128)}, bf16[512,1536]{1,0:T(8,128)(2,1)}, bf16[512,512]{1,0:T(8,128)(2,1)}) custom-call(bf16[128,512]{1,0:T(8,128)(2,1)} %bitcast.24, f32[128,512]{1,0:T(8,128)} %bitcast.27, bf16[512,1536]{1,0:T(8,128)(2,1)} %bitcast.21, bf16[512,512]{1,0:T(8,128)(2,1)} %bitcast.26), custom_call_target="tpu_custom_call" | custom-call | bytes 6291456 | tf_op jit(solution)/shard_map/pallas_call | solution.py:258
  17.5 1.4 copy-done.1
  19.8 4.5 %shard_map.68 = (bf16[768,1536]{1,0:T(8,128)(2,1)S(1)}, bf16[4,256,768]{2,1,0:T(8,128)(2,1)S(1)}, bf16[256,512]{1,0:T(8,128)(2,1)S(1)}, bf16[128,1152]{1,0:T(8,1...) custom-call(s32[6]{0:T(128)S(1)} %stack.19.where_ref, bf16[256,512]{1,0:T(8,128)(2,1)S(1)} %pad_maximum_fusion.x0, ...), custom_call_target="tpu_custom_call" | custom-call | flops 2147483648 | bytes 4194304 | tf_op jit(solution)/shard_map/pallas_call | solution.py:270
  24.3 1.3 collective-permute-start.4
  25.6 4.9 %collective-permute-start.5 = (bf16[64,1152]{1,0:T(8,128)(2,1)S(1)}, bf16[64,1152]{1,0:T(8,128)(2,1)S(1)}, u32[]{:S(2)}, u32[]{:S(2)}) collective-permute-start(bf16[64,1152]{1,0:T(8,128)(2,1)S(1)} %get-tuple-element.48), channel_id=1, source_target_pairs={{1,0},{2,1},{3,2},{5,4},{6,5},{7,6},{9,8},{10,9},{11,10},{13,12},{... | collective-permute-start | bytes 442376 | tf_op jit(solution)/shard_map/ppermute | solution.py:296
  31.1 2.1 %collective-permute-done.4 = bf16[64,1152]{1,0:T(8,128)(2,1)S(1)} collective-permute-done((bf16[64,1152]{1,0:T(8,128)(2,1)S(1)}, bf16[64,1152]{1,0:T(8,128)(2,1)S(1)}, u32[]{:S(2)}, u32[]{:S(2)}) %collective-permute-start.4) | collective-permute-done | bytes 147488 | tf_op jit(solution)/shard_map/ppermute | solution.py:296
  33.3 1.2 collective-permute-done.5
  36.6 1.5 shard_map.70.prob_ref
  48.2 1.3 collective-permute-start.18
  49.5 1.3 collective-permute-start.19
  51.5 46.4 %collective-permute-done.18.g_ref = bf16[128,512]{1,0:T(8,128)(2,1)S(1)} collective-permute-done((bf16[128,512]{1,0:T(8,128)(2,1)S(1)}, bf16[128,512]{1,0:T(8,128)(2,1)S(1)}, u32[]{:S(2)}, u32[]{:S(2)}) %collective-permute-start.18) | collective-permute-done | bytes 131104 | tf_op jit(solution)/shard_map/ppermute | solution.py:296
  97.9 1.8 %collective-permute-done.19 = bf16[64,512]{1,0:T(8,128)(2,1)S(1)} collective-permute-done((bf16[64,512]{1,0:T(8,128)(2,1)S(1)}, bf16[64,512]{1,0:T(8,128)(2,1)S(1)}, u32[]{:S(2)}, u32[]{:S(2)}) %collective-permute-start.19) | collective-permute-done | bytes 65568 | tf_op jit(solution)/shard_map/ppermute | solution.py:296
  99.6 2.0 %shard_map.76.dq_ref = bf16[128,512]{1,0:T(8,128)(2,1)S(1)} custom-call(s32[6]{0:T(128)S(1)} %stack.19.where_ref, bf16[128,512]{1,0:T(8,128)(2,1)S(1)} %collective-permute-done.18.g_ref, bf16[512,512]{1,0:T(8,128)(2,1)S(1)} %copy-done, bf16[128,1152]{1,0:T(8,128)(2,1)S(1)} %get-tuple-element.46.pack_ref.m0, ...), custom_call_target="tpu_custom_call" | custom-call | flops 536870912 | bytes 4194304 | tf_op jit(solution)/shard_map/pallas_call | solution.py:270
  101.7 10.8 %collective-permute-start.21 = (bf16[256,512]{1,0:T(8,128)(2,1)S(1)}, bf16[256,512]{1,0:T(8,128)(2,1)S(1)}, u32[]{:S(2)}, u32[]{:S(2)}) collective-permute-start(bf16[256,512]{1,0:T(8,128)(2,1)S(1)} %constant_dynamic-update-slice_fusion.9.g0), channel_id=1, source_target_pairs={{0,4},{1,5},{2,6},{3,7},{4,0},{5,1},{6,2},{7,3},{8,12},{9,13},{10,... | collective-permute-start | bytes 786440 | tf_op jit(solution)/shard_map/ppermute | solution.py:296
  113.6 4.2 %shard_map.77 = (f32[128,512]{1,0:T(8,128)}, bf16[128,1536]{1,0:T(8,128)(2,1)S(1)}, bf16[256,512]{1,0:T(8,128)(2,1)S(1)}) custom-call(s32[6]{0:T(128)S(1)} %stack.19.where_ref, bf16[128,512]{1,0:T(8,128)(2,1)S(1)} %collective-permute-done.18.g_ref, bf16[256,512]{1,0:T(8,128)(2,1)S(1)} %constant_dynamic-update-slice_fusion.9.g0, ...), custom_call_target="tpu_custom_call" | custom-call | flops 1073741824 | bytes 4194304 | tf_op jit(solution)/shard_map/pallas_call | solution.py:270
  117.8 8.0 %collective-permute-start.23 = (bf16[128,1536]{1,0:T(8,128)(2,1)S(1)}, bf16[128,1536]{1,0:T(8,128)(2,1)S(1)}, u32[]{:S(2)}, u32[]{:S(2)}) collective-permute-start(bf16[128,1536]{1,0:T(8,128)(2,1)S(1)} %get-tuple-element.81.d0), channel_id=1, source_target_pairs={{0,4},{1,5},{2,6},{3,7},{4,0},{5,1},{6,2},{7,3},{8,12},{9,13},{10,... | collective-permute-start | bytes 1179656 | tf_op jit(solution)/shard_map/ppermute | solution.py:296
  125.8 1.3 collective-permute-done.23.d1
  127.2 1.9 %shard_map.78 = bf16[4,64,2048]{2,1,0:T(8,128)(2,1)S(1)} custom-call(s32[6]{0:T(128)S(1)} %stack.19.where_ref, bf16[256,512]{1,0:T(8,128)(2,1)S(1)} %get-tuple-element.80.n_ref, bf16[128,1536]{1,0:T(8,128)(2,1)S(1)} %get-tuple-element.81.d0, bf16[128,1536]{1,0:T(8,128)(2,1)S(1)} %collective-permute-done.23.d1, ...), custom_call_target="tpu_custom_call" | custom-call | flops 1073741824 | bytes 4194304 | tf_op jit(solution)/shard_map/pallas_call | solution.py:270
  129.1 20.8 %all_to_all.10 = bf16[4,64,2048]{2,1,0:T(8,128)(2,1)S(1)} all-to-all(bf16[4,64,2048]{2,1,0:T(8,128)(2,1)S(1)} %shard_map.78), channel_id=1, replica_groups=mesh['pipe'=4,'z'=8,'core'=2,'col'=4] {'col'}, dimensions={0} | all-to-all | bytes 2097152 | tf_op jit(solution)/shard_map/all_to_all | solution.py:372
  150.1 21.2 %all_to_all.11.part_ref = bf16[8,8,2048]{2,1,0:T(8,128)(2,1)S(1)} all-to-all(bf16[8,8,2048]{2,1,0:T(8,128)(2,1)S(1)} %bitcast.25), channel_id=1, replica_groups=mesh['pipe'=4,'z'=8,'core'=2,'col'=4] {'z'}, dimensions={0} | all-to-all | bytes 524288 | tf_op jit(solution)/shard_map/all_to_all | solution.py:374
  (67 shorter events, 19.6 us)
Async XLA Ops:
  1.5 6.2 %collective-permute-start = (bf16[64,512]{1,0:T(8,128)(2,1)S(1)}, bf16[64,512]{1,0:T(8,128)(2,1)S(1)}, u32[]{:S(2)}, u32[]{:S(2)}) collective-permute-start(bf16[64,512]{1,0:T(8,128)(2,1)S(1)} %get-tuple-element.85), channel_id=1, source_target_pairs={{0,1},{1,2},{2,3},{4,5},{5,6},{6,7},{8,9},{9,10},{10,11},{12,13},{... | collective-permute-start | bytes 196616 | tf_op jit(solution)/shard_map/ppermute | solution.py:296
  2.8 6.4 %collective-permute-start.1 = (bf16[64,512]{1,0:T(8,128)(2,1)S(1)}, bf16[64,512]{1,0:T(8,128)(2,1)S(1)}, u32[]{:S(2)}, u32[]{:S(2)}) collective-permute-start(bf16[64,512]{1,0:T(8,128)(2,1)S(1)} %get-tuple-element.86), channel_id=1, source_target_pairs={{1,0},{2,1},{3,2},{5,4},{6,5},{7,6},{9,8},{10,9},{11,10},{13,12},{... | collective-permute-start | bytes 196616 | tf_op jit(solution)/shard_map/ppermute | solution.py:296
  10.2 7.3 %collective-permute-start.3 = (bf16[256,512]{1,0:T(8,128)(2,1)S(1)}, bf16[256,512]{1,0:T(8,128)(2,1)S(1)}, u32[]{:S(2)}, u32[]{:S(2)}) collective-permute-start(bf16[256,512]{1,0:T(8,128)(2,1)S(1)} %pad_maximum_fusion.x0), channel_id=1, source_target_pairs={{4,8},{5,9},{6,10},{7,11},{8,4},{9,5},{10,6},{11,7},{12,16},{13,17... | collective-permute-start | bytes 786440 | tf_op jit(solution)/shard_map/ppermute | solution.py:296
  10.9 6.6 %collective-permute-start.2 = (bf16[256,512]{1,0:T(8,128)(2,1)S(1)}, bf16[256,512]{1,0:T(8,128)(2,1)S(1)}, u32[]{:S(2)}, u32[]{:S(2)}) collective-permute-start(bf16[256,512]{1,0:T(8,128)(2,1)S(1)} %pad_maximum_fusion.x0), channel_id=1, source_target_pairs={{0,4},{1,5},{2,6},{3,7},{4,0},{5,1},{6,2},{7,3},{8,12},{9,13},{10,... | collective-permute-start | bytes 786440 | tf_op jit(solution)/shard_map/ppermute | solution.py:296
  24.3 8.9 %collective-permute-start.4 = (bf16[64,1152]{1,0:T(8,128)(2,1)S(1)}, bf16[64,1152]{1,0:T(8,128)(2,1)S(1)}, u32[]{:S(2)}, u32[]{:S(2)}) collective-permute-start(bf16[64,1152]{1,0:T(8,128)(2,1)S(1)} %get-tuple-element.47), channel_id=1, source_target_pairs={{0,1},{1,2},{2,3},{4,5},{5,6},{6,7},{8,9},{9,10},{10,11},{12,13},{... | collective-permute-start | bytes 442376 | tf_op jit(solution)/shard_map/ppermute | solution.py:296
  25.6 8.9 %collective-permute-start.5 = (bf16[64,1152]{1,0:T(8,128)(2,1)S(1)}, bf16[64,1152]{1,0:T(8,128)(2,1)S(1)}, u32[]{:S(2)}, u32[]{:S(2)}) collective-permute-start(bf16[64,1152]{1,0:T(8,128)(2,1)S(1)} %get-tuple-element.48), channel_id=1, source_target_pairs={{1,0},{2,1},{3,2},{5,4},{6,5},{7,6},{9,8},{10,9},{11,10},{13,12},{... | collective-permute-start | bytes 442376 | tf_op jit(solution)/shard_map/ppermute | solution.py:296
  34.5 2.1 %collective-permute-start.6 = (bf16[256,1152]{1,0:T(8,128)(2,1)S(1)}, bf16[256,1152]{1,0:T(8,128)(2,1)S(1)}, u32[]{:S(2)}, u32[]{:S(2)}) collective-permute-start(bf16[256,1152]{1,0:T(8,128)(2,1)S(1)} %constant_dynamic-update-slice_fusion.p0.g0), channel_id=1, source_target_pairs={{0,4},{1,5},{2,6},{3,7},{4,0},{5,1},{6,2},{7,3},{8,12},{9,13},{10,... | collective-permute-start | bytes 1769480 | tf_op jit(solution)/shard_map/ppermute | solution.py:296
  34.6 2.0 %collective-permute-start.7 = (bf16[256,1152]{1,0:T(8,128)(2,1)S(1)}, bf16[256,1152]{1,0:T(8,128)(2,1)S(1)}, u32[]{:S(2)}, u32[]{:S(2)}) collective-permute-start(bf16[256,1152]{1,0:T(8,128)(2,1)S(1)} %constant_dynamic-update-slice_fusion.p0.g0), channel_id=1, source_target_pairs={{4,8},{5,9},{6,10},{7,11},{8,4},{9,5},{10,6},{11,7},{12,16},{13,17... | collective-permute-start | bytes 1769480 | tf_op jit(solution)/shard_map/ppermute | solution.py:296
  38.7 2.0 %collective-permute-start.8 = (bf16[128,512]{1,0:T(8,128)(2,1)S(1)}, bf16[128,512]{1,0:T(8,128)(2,1)S(1)}, u32[]{:S(2)}, u32[]{:S(2)}) collective-permute-start(bf16[128,512]{1,0:T(8,128)(2,1)S(1)} %get-tuple-element.55), channel_id=1, source_target_pairs={{192,128},{193,129},{194,130},{195,131},{196,132},{197,133},{198,1... | collective-permute-start | bytes 393224 | tf_op jit(solution)/shard_map/ppermute | solution.py:296
  39.3 1.4 collective-permute-start.9
  40.0 1.3 collective-permute-start.10
  41.3 1.4 collective-permute-start.11
  42.0 0.7 collective-permute-start.12
  43.5 2.0 %collective-permute-start.13 = (bf16[128,512]{1,0:T(8,128)(2,1)S(1)}, bf16[128,512]{1,0:T(8,128)(2,1)S(1)}, u32[]{:S(2)}, u32[]{:S(2)}) collective-permute-start(bf16[128,512]{1,0:T(8,128)(2,1)S(1)} %get-tuple-element.63), channel_id=1, source_target_pairs={{128,64},{129,65},{130,66},{131,67},{132,68},{133,69},{134,70},{13... | collective-permute-start | bytes 393224 | tf_op jit(solution)/shard_map/ppermute | solution.py:296
  44.2 1.4 collective-permute-start.14
  44.9 1.3 collective-permute-start.15
  46.2 1.4 collective-permute-start.16
  46.9 0.7 collective-permute-start.17
  48.2 49.7 %collective-permute-start.18 = (bf16[128,512]{1,0:T(8,128)(2,1)S(1)}, bf16[128,512]{1,0:T(8,128)(2,1)S(1)}, u32[]{:S(2)}, u32[]{:S(2)}) collective-permute-start(bf16[128,512]{1,0:T(8,128)(2,1)S(1)} %get-tuple-element.71), channel_id=1, source_target_pairs={{64,0},{65,1},{66,2},{67,3},{68,4},{69,5},{70,6},{71,7},{72,8},{73... | collective-permute-start | bytes 393224 | tf_op jit(solution)/shard_map/ppermute | solution.py:296
  49.5 50.1 %collective-permute-start.19 = (bf16[64,512]{1,0:T(8,128)(2,1)S(1)}, bf16[64,512]{1,0:T(8,128)(2,1)S(1)}, u32[]{:S(2)}, u32[]{:S(2)}) collective-permute-start(bf16[64,512]{1,0:T(8,128)(2,1)S(1)} %get-tuple-element.72), channel_id=1, source_target_pairs={{64,1},{65,2},{66,3},{68,5},{69,6},{70,7},{72,9},{73,10},{74,11},{... | collective-permute-start | bytes 196616 | tf_op jit(solution)/shard_map/ppermute | solution.py:296
  50.8 50.8 %collective-permute-start.20 = (bf16[64,512]{1,0:T(8,128)(2,1)S(1)}, bf16[64,512]{1,0:T(8,128)(2,1)S(1)}, u32[]{:S(2)}, u32[]{:S(2)}) collective-permute-start(bf16[64,512]{1,0:T(8,128)(2,1)S(1)} %get-tuple-element.73), channel_id=1, source_target_pairs={{65,0},{66,1},{67,2},{69,4},{70,5},{71,6},{73,8},{74,9},{75,10},{7... | collective-permute-start | bytes 196616 | tf_op jit(solution)/shard_map/ppermute | solution.py:296
  101.7 12.0 %collective-permute-start.21 = (bf16[256,512]{1,0:T(8,128)(2,1)S(1)}, bf16[256,512]{1,0:T(8,128)(2,1)S(1)}, u32[]{:S(2)}, u32[]{:S(2)}) collective-permute-start(bf16[256,512]{1,0:T(8,128)(2,1)S(1)} %constant_dynamic-update-slice_fusion.9.g0), channel_id=1, source_target_pairs={{0,4},{1,5},{2,6},{3,7},{4,0},{5,1},{6,2},{7,3},{8,12},{9,13},{10,... | collective-permute-start | bytes 786440 | tf_op jit(solution)/shard_map/ppermute | solution.py:296
  112.5 1.1 collective-permute-start.22
  117.8 9.3 %collective-permute-start.23 = (bf16[128,1536]{1,0:T(8,128)(2,1)S(1)}, bf16[128,1536]{1,0:T(8,128)(2,1)S(1)}, u32[]{:S(2)}, u32[]{:S(2)}) collective-permute-start(bf16[128,1536]{1,0:T(8,128)(2,1)S(1)} %get-tuple-element.81.d0), channel_id=1, source_target_pairs={{0,4},{1,5},{2,6},{3,7},{4,0},{5,1},{6,2},{7,3},{8,12},{9,13},{10,... | collective-permute-start | bytes 1179656 | tf_op jit(solution)/shard_map/ppermute | solution.py:296
  (6 other events, 23.8 us)

commit v5 on v3

--- a/solution.py
+++ b/solution.py
@@ -78,16 +78,36 @@
     right_ref[...] = sides[:, 1].reshape(64, -1).astype(BF16)
 
 
+def first_kernel(where_ref, x_ref, base_ref, left_ref, right_ref):
+    base_ref[:TOK] = x_ref[...]
+    base_ref[TOK:] = jnp.zeros((TOK, D), BF16)
+    put_sides(x_ref[...].astype(F32), left_ref, right_ref)
+
+
+def normed_low(x_ref):
+    x = x_ref[...].astype(F32)
+    inverse = lax.rsqrt(jnp.mean(x * x, axis=-1, keepdims=True) + 1e-06)
+    return (x * inverse).astype(BF16)
+
+
+def own_kernel(where_ref, x_ref, w_ref, cot_ref, proj_ref, nlow_ref, cot_low_ref):
+    low = normed_low(x_ref)
+    nlow_ref[...] = low[:TOK]
+    proj_ref[...] = nn(low, w_ref[...]).astype(BF16)
+    cot_low_ref[...] = cot_ref[...].astype(BF16)
+
+
 def forward_kernel(
-    where_ref, x0, x1, x2, w_ref, cot_ref, proj_ref, prob_ref, nlow_ref, pack_ref, left_ref, right_ref
+    where_ref, x1, x2, proj_ref, w_ref, cot_ref,
+    kv_ref, prob_ref, nlow_ref, far_ref, pack_ref, left_ref, right_ref,
 ):
-    for piece, x_ref in enumerate((x0, x1, x2)):
-        x = x_ref[...].astype(F32)
-        inverse = lax.rsqrt(jnp.mean(x * x, axis=-1, keepdims=True) + 1e-06)
-        low = (x * inverse).astype(BF16)
-        if piece < 2:
-            nlow_ref[piece * TOK : (piece + 1) * TOK] = low[:TOK]
-        proj_ref[piece * OWN : (piece + 1) * OWN] = nn(low, w_ref[...]).astype(BF16)
+    kv_ref[:OWN] = proj_ref[:, D:]
+    for piece, x_ref in enumerate((x1, x2)):
+        low = normed_low(x_ref)
+        far_ref[piece * OWN : (piece + 1) * OWN] = low
+        if piece == 0:
+            nlow_ref[...] = low[:TOK]
+        kv_ref[(piece + 1) * OWN : (piece + 2) * OWN] = nn(low, w_ref[:, D:]).astype(BF16)
     ok = window(where_ref, False)
     ok2 = jnp.concatenate([ok, ok], axis=0)
     lane = lax.broadcasted_iota(jnp.int32, (TOK, 128), 1)
@@ -95,14 +115,14 @@
     for pair in range(PAIRS):
         at = slice(128 * pair, 128 * pair + 128)
         query = two_heads(proj_ref[:TOK, at] * 0.125)
-        scores = nt(query, proj_ref[:, D + 128 * pair : D + 128 * pair + 128])
+        scores = nt(query, kv_ref[:, at])
         scores = jnp.where(ok2, scores, -1e30)
         highest = jnp.max(scores, axis=-1, keepdims=True)
         grown = jnp.exp(scores - highest)
         total = jnp.sum(grown, axis=-1, keepdims=True)
         probs = (grown * (1.0 / total)).astype(BF16)
         prob_ref[pair] = probs
-        value = proj_ref[:, 2 * D + 128 * pair : 2 * D + 128 * pair + 128]
+        value = kv_ref[:, D + 128 * pair : D + 128 * pair + 128]
         pack_ref[:, at] = one_block(nn(probs, value)).astype(BF16)
         log_total = highest + jnp.log(total)
         rest = log_total
@@ -113,21 +133,29 @@
                 chosen = lane == 8 * part + 2 * pair + head
                 stats = jnp.where(chosen, piece[TOK * head : TOK * head + TOK], stats)
     pack_ref[:, D : D + 128] = stats.astype(BF16)
-    pack_ref[:, D + 128 :] = cot_ref[...].astype(BF16)
+    pack_ref[:, D + 128 :] = cot_ref[...]
     put_sides(pack_ref[...].astype(F32), left_ref, right_ref)
 
 
-def key_probs_kernel(where_ref, p0, p1, p2, proj_ref, prob_ref):
+def turned_kernel(where_ref, proj_ref, far_ref, w_ref, query_ref):
+    query_ref[:, :OWN] = proj_ref[:, :D].astype(F32).T.astype(BF16)
+    far = nn(far_ref[...], w_ref[:, :D]).astype(BF16)
+    query_ref[:, OWN:] = far.astype(F32).T.astype(BF16)
+
+
+def key_probs_kernel(where_ref, p0, p1, p2, proj_ref, query_ref, prob_ref, mixed_ref):
     head = lax.broadcasted_iota(jnp.int32, (8, 128), 0)
     lane = lax.broadcasted_iota(jnp.int32, (8, 128), 1)
     chosen = ((lane & 7) == head) & (lane < 24)
     pick = jnp.where(chosen, 1.0, 0.0).astype(BF16)
     stats = jnp.concatenate([p[:, D : D + 128] for p in (p0, p1, p2)], axis=0)
     log_total = nt(pick, stats)
+    for piece, p in enumerate((p0, p1, p2)):
+        mixed_ref[:, piece * OWN : (piece + 1) * OWN] = p[:, :D].astype(F32).T.astype(BF16)
     ok = window(where_ref, True)
     for pair in range(PAIRS):
         key = two_heads(proj_ref[:TOK, D + 128 * pair : D + 128 * pair + 128] * 0.125)
-        scores = nt(key, proj_ref[:, 128 * pair : 128 * pair + 128])
+        scores = nn(key, query_ref[128 * pair : 128 * pair + 128])
         for side in range(2):
             at = 2 * pair + side
             part = scores[TOK * side : TOK * side + TOK] - log_total[at : at + 1]
@@ -135,7 +163,7 @@
             prob_ref[pair, TOK * side : TOK * side + TOK] = probs.astype(BF16)
 
 
-def query_kernel(where_ref, g_ref, w_ref, pack_ref, proj_ref, prob_ref, dq_ref, *, turn):
+def query_kernel(where_ref, g_ref, w_ref, pack_ref, kv_ref, prob_ref, dq_ref, *, turn):
     @pl.when(where_ref[5] == turn)
     def _():
         d_mixed = nt(g_ref[...].astype(BF16), w_ref[...]).astype(BF16)
@@ -151,59 +179,55 @@
                 ],
                 axis=0,
             )
-            value = proj_ref[:, 2 * D + 128 * pair : 2 * D + 128 * pair + 128]
+            value = kv_ref[:, D + 128 * pair : D + 128 * pair + 128]
             pressure = nt(two_heads(grad), value)
             slopes = (prob_ref[pair].astype(F32) * (pressure - delta)).astype(BF16)
-            key = proj_ref[:, D + 128 * pair : D + 128 * pair + 128]
-            dq_ref[:, at] = (one_block(nn(slopes, key)) * 0.125).astype(BF16)
+            dq_ref[:, at] = (one_block(nn(slopes, kv_ref[:, at])) * 0.125).astype(BF16)
+
+
+def turned_block(stacked):
+    row = lax.broadcasted_iota(jnp.int32, (128, 128), 0)
+    return jnp.where(row < 64, stacked[:, :128], stacked[:, 128:]).T
 
 
 def key_kernel(
-    where_ref, g_ref, g0, g1, g2, wo_ref, p0, p1, p2, proj_ref, prob_ref, dq_ref, wq_ref, x_ref,
-    in_prev, dp_prev, gl_prev,
-    in_ref, dp_ref, gl_ref, *rest, turn,
+    where_ref, g_ref, g0, g1, g2, wo_ref, mixed_ref, proj_ref, query_ref, prob_ref, dq_ref, wq_ref,
+    x_ref, *rest, turn,
 ):
-    sends, dm_ref = rest[:-1], rest[-1]
+    prev, rest = (rest[:3], rest[3:]) if turn else ((), rest)
+    (in_ref, dp_ref, gl_ref), sends, dm_ref = rest[:3], rest[3:-1], rest[-1]
     active = where_ref[5] == turn
 
-    @pl.when(jnp.logical_not(active))
-    def _():
-        in_ref[...] = in_prev[...]
-        dp_ref[...] = dp_prev[...]
-        gl_ref[...] = gl_prev[...]
+    if prev:
+
+        @pl.when(jnp.logical_not(active))
+        def _():
+            for new, old in zip((in_ref, dp_ref, gl_ref), prev):
+                new[...] = old[...]
 
     @pl.when(active)
     def _():
-        head = lax.broadcasted_iota(jnp.int32, (8, D), 0)
-        lane = lax.broadcasted_iota(jnp.int32, (8, D), 1)
-        pick = jnp.where((lane >> 6) == head, 1.0, 0.0).astype(BF16)
-        deltas = []
-        for piece, (g, p) in enumerate(((g0, p0), (g1, p1), (g2, p2))):
-            d_mixed = nt(g[:, -D:], wo_ref[...]).astype(BF16)
-            dm_ref[piece * OWN : (piece + 1) * OWN] = d_mixed
-            prod = d_mixed.astype(F32) * p[:, :D].astype(F32)
-            high = prod.astype(BF16)
-            rest = (prod - high.astype(F32)).astype(BF16)
-            deltas.append(nt(pick, high) + nt(pick, rest))
-        delta = jnp.concatenate(deltas, axis=1)
+        for piece, g in enumerate((g0, g1, g2)):
+            d_mixed = nt(wo_ref[...], g[:, -D:]).astype(BF16)
+            dm_ref[:, piece * OWN : (piece + 1) * OWN] = d_mixed
         dp_ref[:, :D] = dq_ref[...]
         for pair in range(PAIRS):
             at = slice(128 * pair, 128 * pair + 128)
             value = two_heads(proj_ref[:TOK, 2 * D + 128 * pair : 2 * D + 128 * pair + 128])
-            grad = dm_ref[:, at]
-            pressure = nt(value, grad)
+            grad = dm_ref[at]
+            prod = grad.astype(F32) * mixed_ref[at].astype(F32)
+            pressure = nn(value, grad)
             probs = prob_ref[pair]
-            d_value = nn(probs, grad)
+            d_value = nt(grad, probs)
             slopes = []
             for side in range(2):
-                h = 2 * pair + side
+                delta = jnp.sum(prod[64 * side : 64 * side + 64], axis=0, keepdims=True)
                 rows = slice(TOK * side, TOK * side + TOK)
-                slopes.append(
-                    (probs[rows].astype(F32) * (pressure[rows] - delta[h : h + 1])).astype(BF16)
-                )
-            d_key = nn(jnp.concatenate(slopes, axis=0), proj_ref[:, at])
-            dp_ref[:, D + 128 * pair : D + 128 * pair + 128] = (one_block(d_key) * 0.125).astype(BF16)
-            dp_ref[:, 2 * D + 128 * pair : 2 * D + 128 * pair + 128] = one_block(d_value).astype(BF16)
+                slopes.append((probs[rows].astype(F32) * (pressure[rows] - delta)).astype(BF16))
+            d_key = nt(query_ref[at], jnp.concatenate(slopes, axis=0))
+            low, high = D + 128 * pair, D + 128 * pair + 128
+            dp_ref[:, low:high] = (turned_block(d_key) * 0.125).astype(BF16)
+            dp_ref[:, D + low : D + high] = turned_block(d_value).astype(BF16)
         d_normed = nt(dp_ref[...], wq_ref[...])
         x = x_ref[...].astype(F32)
         inverse = lax.rsqrt(jnp.mean(x * x, axis=-1, keepdims=True) + 1e-06)
@@ -220,9 +244,9 @@
             put_sides(out, left_ref, right_ref)
 
 
-def weight_kernel(where_ref, n_ref, d0, d1, m0, m1, g_ref, out_ref, full_ref):
+def weight_kernel(where_ref, n0, n1, d0, d1, m0, m1, g_ref, out_ref, full_ref):
     core = where_ref[2]
-    full_ref[:, : 3 * D] = tn(n_ref[:TOK], d0[...]) + tn(n_ref[TOK:], d1[...])
+    full_ref[:, : 3 * D] = tn(n0[...], d0[...]) + tn(n1[...], d1[...])
     full_ref[:, 3 * D :] = tn(m0[:, :D], g_ref[:TOK]) + tn(m1[:TOK, :D], g_ref[TOK:])
     chips, cols = out_ref.shape[1] // 8, out_ref.shape[0]
     for col in range(cols):
@@ -293,23 +317,33 @@
         [8 * (2 * z + core), 16 * col, core, row_total, col_total, pipes - 1 - pipe]
     ).astype(jnp.int32)
 
-    x_sides = x.reshape(8, 2, 8, D)
-    xs = row_rims([x, *col_rims(x_sides[:, 0].reshape(64, D), x_sides[:, 1].reshape(64, D))])
+    base, low_side, high_side = call(
+        first_kernel, [((OWN, D), BF16), ((64, D), BF16), ((64, D), BF16)], where, x
+    )
+    left, right = col_rims(low_side, high_side)
+    own = lax.dynamic_update_slice(base, left, (TOK, 0))
+    own, near, far = row_rims([lax.dynamic_update_slice(own, right, (TOK + 64, 0))])
+    proj, nlow, cot_low = call(
+        own_kernel, [((OWN, 3 * D), BF16), ((TOK, D), BF16), ((TOK, D), BF16)],
+        where, own, w_qkv, cot, flops=1 << 29,
+    )
     wide = 2 * D + 128
-    proj, q_probs, nlow, pack, low_side, high_side = call(
+    kv, q_probs, nlow_mate, low_far, pack, low_side, high_side = call(
         forward_kernel,
-        [((REGION, 3 * D), BF16), ((PAIRS, OWN, REGION), BF16), ((OWN, D), BF16),
-         ((TOK, wide), BF16), ((64, wide), BF16), ((64, wide), BF16)],
-        where, *xs, w_qkv, cot, flops=2 << 30,
+        [((REGION, 2 * D), BF16), ((PAIRS, OWN, REGION), BF16), ((TOK, D), BF16),
+         ((2 * OWN, D), BF16), ((TOK, wide), BF16), ((64, wide), BF16), ((64, wide), BF16)],
+        where, near, far, proj, w_qkv, cot_low, flops=2 << 30,
     )
     packs = row_rims([pack, *col_rims(low_side, high_side)])
-    (k_probs,) = call(
-        key_probs_kernel, [((PAIRS, OWN, REGION), BF16)], where, *packs, proj, flops=1 << 28
-    )
-    d_in = jnp.zeros((TOK, D), F32)
-    d_proj = jnp.zeros((TOK, 3 * D), BF16)
-    g_low = jnp.zeros((OWN, D), BF16)
+    (queries,) = call(
+        turned_kernel, [((D, REGION), BF16)], where, proj, low_far, w_qkv, flops=1 << 28
+    )
+    k_probs, mixed = call(
+        key_probs_kernel, [((PAIRS, OWN, REGION), BF16), ((D, REGION), BF16)],
+        where, *packs, proj, queries, flops=1 << 28,
+    )
     gradient, gs = cot, packs
+    state = ()
     for turn in range(pipes):
         plane, last = pipes - 1 - turn, turn == pipes - 1
         if turn > 0:
@@ -318,19 +352,20 @@
             gs = row_rims([gradient, *col_rims(low_side, high_side, 1, plane + 1)], plane)
         (d_query,) = call(
             functools.partial(query_kernel, turn=turn), [((TOK, D), BF16)],
-            where, gradient, w_out, pack, proj, q_probs, flops=1 << 29,
+            where, gradient, w_out, pack, kv, q_probs, flops=1 << 29,
         )
         halves = [((TOK, D), BF16), ((64, D), BF16), ((64, D), BF16)]
-        d_in, d_proj, g_low, *sends = call(
+        outs = call(
             functools.partial(key_kernel, turn=turn),
             [((TOK, D), F32), ((TOK, 3 * D), BF16), ((OWN, D), BF16)] + ([] if last else halves),
-            where, gradient, *gs, w_out, *packs, proj, k_probs, d_query, w_qkv, x,
-            d_in, d_proj, g_low,
-            scratch=[pltpu.VMEM((REGION, D), BF16)], flops=1 << 30,
+            where, gradient, *gs, w_out, mixed, proj, queries, k_probs, d_query, w_qkv, x, *state,
+            scratch=[pltpu.VMEM((D, REGION), BF16)], flops=1 << 30,
         )
+        state, sends = outs[:3], outs[3:]
+    d_in, d_proj, g_low = state
     (part,) = call(
         weight_kernel, [((cols, 8 * chips, 4 * D), BF16)],
-        where, nlow, d_proj, routed(d_proj, mate), pack, packs[1], g_low,
+        where, nlow, nlow_mate, d_proj, routed(d_proj, mate), pack, packs[1], g_low,
         scratch=[pltpu.VMEM((D, 4 * D), F32)], flops=1 << 30,
     )
     part = lax.all_to_all(part, "col", 0, 0, tiled=True)

time: 160 us -> 156 us (0.975)
  waiting for transfers between devices: 54.3 us -> 51.9 us
  Pallas kernels: 19 us -> 20.9 us
    ppermute x24, waiting for transfers between devices: 54.3 us -> 51.9 us  [routed(): return lax.ppermute(block, AXES, pairs)]
    pallas_call x12 -> x15, Pallas kernels: 19 us -> 20.9 us  [call(): pl.pallas_call(kernel, out_shape=[jax.ShapeDtypeStruct(s, t) for s, t in...]
    unnamed x20 -> x22, local copies, waits for them, and re-layouts: 2.47 us -> 3.59 us
  transfers between devices with their start and end apart: 24 -> 24, of which waited for: 9 -> 7; matrix products, arithmetic and copies ran while one was open for 0% -> 0% of each run, Pallas kernels for 2% -> 4%
where the time goes in v5:
time: 156 us; the launch traced here: 154 us
  waiting for transfers between devices  51.9 us (33%)
  blocking collectives  38.9 us (25%)
  starting transfers between devices  37.7 us (24%)
  Pallas kernels  20.9 us (13%)
  local copies, waits for them, and re-layouts  3.73 us (2%)
    ppermute x24, waiting for transfers between devices, routed(): return lax.ppermute(block, AXES, pairs)  51.9 us
    ppermute x24, starting transfers between devices, routed(): return lax.ppermute(block, AXES, pairs)  37.7 us
    pallas_call x15, Pallas kernels, call(): pl.pallas_call(kernel, out_shape=[jax.ShapeDtypeStruct(s, t) for s, t in...  20.9 us
    all_to_all x1, blocking collectives, body(): part = lax.all_to_all(part, 'col', 0, 0, tiled=True)  20.6 us
    all_to_all x1, blocking collectives, body(): part = lax.all_to_all(part, 'z', 0, 0, tiled=True)  18.3 us
    unnamed x22, local copies, waits for them, and re-layouts  3.59 us
  transfers between devices with their start and end apart: 24, of which 7 were waited for; matrix products, arithmetic and copies ran while one was open for 0% of the time, Pallas kernels for 4%

profile of v5, /device:TPU:6, one launch (start us, length us, event | category | flops | bytes accessed | tf_op | source)
XLA Modules:
  0.0 154.4 jit_solution(8327309699624815795)
XLA Ops:
  2.2 1.3 collective-permute-start
  3.5 4.5 %collective-permute-start.1 = (bf16[64,512]{1,0:T(8,128)(2,1)S(1)}, bf16[64,512]{1,0:T(8,128)(2,1)S(1)}, u32[]{:S(2)}, u32[]{:S(2)}) collective-permute-start(bf16[64,512]{1,0:T(8,128)(2,1)S(1)} %get-tuple-element.43), channel_id=1, source_target_pairs={{1,0},{2,1},{3,2},{5,4},{6,5},{7,6},{9,8},{10,9},{11,10},{13,12},{... | collective-permute-start | bytes 196616 | tf_op jit(solution)/shard_map/ppermute | solution.py:296
  8.4 1.6 %collective-permute-done.1 = bf16[64,512]{1,0:T(8,128)(2,1)S(1)} collective-permute-done((bf16[64,512]{1,0:T(8,128)(2,1)S(1)}, bf16[64,512]{1,0:T(8,128)(2,1)S(1)}, u32[]{:S(2)}, u32[]{:S(2)}) %collective-permute-start.1) | collective-permute-done | bytes 65568 | tf_op jit(solution)/shard_map/ppermute | solution.py:296
  10.6 3.4 %collective-permute-start.2 = (bf16[256,512]{1,0:T(8,128)(2,1)S(1)}, bf16[256,512]{1,0:T(8,128)(2,1)S(1)}, u32[]{:S(2)}, u32[]{:S(2)}) collective-permute-start(bf16[256,512]{1,0:T(8,128)(2,1)S(1)} %constant_dynamic-update-slice_fusion.12.x_ref), channel_id=1, source_target_pairs={{0,4},{1,5},{2,6},{3,7},{4,0},{5,1},{6,2},{7,3},{8,12},{9,13},{10,... | collective-permute-start | bytes 786440 | tf_op jit(solution)/shard_map/ppermute | solution.py:296
  14.0 1.4 copy-done
  16.3 1.2 shard_map.68
  17.7 3.8 %shard_map.69 = (bf16[768,1024]{1,0:T(8,128)(2,1)S(1)}, bf16[4,256,768]{2,1,0:T(8,128)(2,1)S(1)}, bf16[128,512]{1,0:T(8,128)(2,1)S(1)}, bf16[512,512]{1,0:T(8,12...) custom-call(s32[6]{0:T(128)S(1)} %stack.19.where_ref, ...), custom_call_target="tpu_custom_call" | custom-call | flops 2147483648 | bytes 4194304 | tf_op jit(solution)/shard_map/pallas_call | solution.py:270
  21.5 1.3 collective-permute-start.4
  22.8 4.9 %collective-permute-start.5 = (bf16[64,1152]{1,0:T(8,128)(2,1)S(1)}, bf16[64,1152]{1,0:T(8,128)(2,1)S(1)}, u32[]{:S(2)}, u32[]{:S(2)}) collective-permute-start(bf16[64,1152]{1,0:T(8,128)(2,1)S(1)} %get-tuple-element.48), channel_id=1, source_target_pairs={{1,0},{2,1},{3,2},{5,4},{6,5},{7,6},{9,8},{10,9},{11,10},{13,12},{... | collective-permute-start | bytes 442376 | tf_op jit(solution)/shard_map/ppermute | solution.py:296
  27.8 2.2 %collective-permute-done.4 = bf16[64,1152]{1,0:T(8,128)(2,1)S(1)} collective-permute-done((bf16[64,1152]{1,0:T(8,128)(2,1)S(1)}, bf16[64,1152]{1,0:T(8,128)(2,1)S(1)}, u32[]{:S(2)}, u32[]{:S(2)}) %collective-permute-start.4) | collective-permute-done | bytes 147488 | tf_op jit(solution)/shard_map/ppermute | solution.py:296
  31.9 3.3 %collective-permute-start.6 = (bf16[256,1152]{1,0:T(8,128)(2,1)S(1)}, bf16[256,1152]{1,0:T(8,128)(2,1)S(1)}, u32[]{:S(2)}, u32[]{:S(2)}) collective-permute-start(bf16[256,1152]{1,0:T(8,128)(2,1)S(1)} %constant_dynamic-update-slice_fusion.p0.g0), channel_id=1, source_target_pairs={{0,4},{1,5},{2,6},{3,7},{4,0},{5,1},{6,2},{7,3},{8,12},{9,13},{10,... | collective-permute-start | bytes 1769480 | tf_op jit(solution)/shard_map/ppermute | solution.py:296
  36.9 1.6 %shard_map.71 = (bf16[4,256,768]{2,1,0:T(8,128)(2,1)S(1)}, bf16[512,768]{1,0:T(8,128)(2,1)S(1)}) custom-call(s32[6]{0:T(128)S(1)} %stack.19.where_ref, bf16[256,1152]{1,0:T(8,128)(2,1)S(1)} %constant_dynamic-update-slice_fusion.p0.g0, bf16[256,1152]{1,0:T(8,128)(2,1)S(1)} %collective-permute-done.6.p1.g1.m1, ...), custom_call_target="tpu_custom_call" | custom-call | flops 268435456 | bytes 4194304 | tf_op jit(solution)/shard_map/pallas_call | solution.py:270
  48.7 1.3 collective-permute-start.18
  50.0 1.3 collective-permute-start.19
  51.9 42.2 %collective-permute-done.18.g_ref = bf16[128,512]{1,0:T(8,128)(2,1)S(1)} collective-permute-done((bf16[128,512]{1,0:T(8,128)(2,1)S(1)}, bf16[128,512]{1,0:T(8,128)(2,1)S(1)}, u32[]{:S(2)}, u32[]{:S(2)}) %collective-permute-start.18) | collective-permute-done | bytes 131104 | tf_op jit(solution)/shard_map/ppermute | solution.py:296
  94.1 2.8 %collective-permute-done.19 = bf16[64,512]{1,0:T(8,128)(2,1)S(1)} collective-permute-done((bf16[64,512]{1,0:T(8,128)(2,1)S(1)}, bf16[64,512]{1,0:T(8,128)(2,1)S(1)}, u32[]{:S(2)}, u32[]{:S(2)}) %collective-permute-start.19) | collective-permute-done | bytes 65568 | tf_op jit(solution)/shard_map/ppermute | solution.py:296
  97.6 6.9 %collective-permute-start.21 = (bf16[256,512]{1,0:T(8,128)(2,1)S(1)}, bf16[256,512]{1,0:T(8,128)(2,1)S(1)}, u32[]{:S(2)}, u32[]{:S(2)}) collective-permute-start(bf16[256,512]{1,0:T(8,128)(2,1)S(1)} %constant_dynamic-update-slice_fusion.9.g0), channel_id=1, source_target_pairs={{0,4},{1,5},{2,6},{3,7},{4,0},{5,1},{6,2},{7,3},{8,12},{9,13},{10,... | collective-permute-start | bytes 786440 | tf_op jit(solution)/shard_map/ppermute | solution.py:296
  104.5 2.0 %shard_map.78.dq_ref = bf16[128,512]{1,0:T(8,128)(2,1)S(1)} custom-call(s32[6]{0:T(128)S(1)} %stack.19.where_ref, bf16[128,512]{1,0:T(8,128)(2,1)S(1)} %collective-permute-done.18.g_ref, bf16[512,512]{1,0:T(8,128)(2,1)S(1)} %bitcast.25, bf16[128,1152]{1,0:T(8,128)(2,1)S(1)} %get-tuple-element.46.pack_ref.m0, bf16[768,1024]{1,0:T(8,128)(2,1)S(1)} %get-tuple-element.52.kv_ref, ...), custom_call_target="tpu_custom_call" | custom-call | flops 536870912 | bytes 4194304 | tf_op jit(solution)/shard_map/pallas_call | solution.py:270
  106.5 4.0 %shard_map.79 = (f32[128,512]{1,0:T(8,128)}, bf16[128,1536]{1,0:T(8,128)(2,1)S(1)}, bf16[256,512]{1,0:T(8,128)(2,1)S(1)}) custom-call(s32[6]{0:T(128)S(1)} %stack.19.where_ref, bf16[128,512]{1,0:T(8,128)(2,1)S(1)} %collective-permute-done.18.g_ref, bf16[256,512]{1,0:T(8,128)(2,1)S(1)} %constant_dynamic-update-slice_fusion.9.g0, ...), custom_call_target="tpu_custom_call" | custom-call | flops 1073741824 | bytes 4194304 | tf_op jit(solution)/shard_map/pallas_call | solution.py:270
  110.5 1.6 %collective-permute-done.23.d1 = bf16[128,1536]{1,0:T(8,128)(2,1)S(1)} collective-permute-done((bf16[128,1536]{1,0:T(8,128)(2,1)S(1)}, bf16[128,1536]{1,0:T(8,128)(2,1)S(1)}, u32[]{:S(2)}, u32[]{:S(2)}) %collective-permute-start.23) | collective-permute-done | bytes 393248 | tf_op jit(solution)/shard_map/ppermute | solution.py:296
  112.2 1.9 %shard_map.80 = bf16[4,64,2048]{2,1,0:T(8,128)(2,1)S(1)} custom-call(s32[6]{0:T(128)S(1)} %stack.19.where_ref, bf16[128,512]{1,0:T(8,128)(2,1)S(1)} %get-tuple-element.73.n0, bf16[128,512]{1,0:T(8,128)(2,1)S(1)} %get-tuple-element.74.n1, bf16[128,1536]{1,0:T(8,128)(2,1)S(1)} %get-tuple-element.75.d0, bf16[128,1536]{1,0:T(8,128)(2,1)S(1)} %collective-permute-done.23.d1, ...), custom_call_target="tpu_custom_call" | custom-call | flops 1073741824 | bytes 4194304 | tf_op jit(solution)/shard_map/pallas_call | solution.py:270
  114.1 20.6 %all_to_all.10 = bf16[4,64,2048]{2,1,0:T(8,128)(2,1)S(1)} all-to-all(bf16[4,64,2048]{2,1,0:T(8,128)(2,1)S(1)} %shard_map.80), channel_id=1, replica_groups=mesh['pipe'=4,'z'=8,'core'=2,'col'=4] {'col'}, dimensions={0} | all-to-all | bytes 2097152 | tf_op jit(solution)/shard_map/all_to_all | solution.py:371
  134.9 18.3 %all_to_all.11.part_ref = bf16[8,8,2048]{2,1,0:T(8,128)(2,1)S(1)} all-to-all(bf16[8,8,2048]{2,1,0:T(8,128)(2,1)S(1)} %bitcast.35), channel_id=1, replica_groups=mesh['pipe'=4,'z'=8,'core'=2,'col'=4] {'z'}, dimensions={0} | all-to-all | bytes 524288 | tf_op jit(solution)/shard_map/all_to_all | solution.py:373
  153.2 1.2 shard_map.81
  (71 shorter events, 18.8 us)
Async XLA Ops:
  2.2 6.2 %collective-permute-start = (bf16[64,512]{1,0:T(8,128)(2,1)S(1)}, bf16[64,512]{1,0:T(8,128)(2,1)S(1)}, u32[]{:S(2)}, u32[]{:S(2)}) collective-permute-start(bf16[64,512]{1,0:T(8,128)(2,1)S(1)} %get-tuple-element.42), channel_id=1, source_target_pairs={{0,1},{1,2},{2,3},{4,5},{5,6},{6,7},{8,9},{9,10},{10,11},{12,13},{... | collective-permute-start | bytes 196616 | tf_op jit(solution)/shard_map/ppermute | solution.py:296
  3.5 6.4 %collective-permute-start.1 = (bf16[64,512]{1,0:T(8,128)(2,1)S(1)}, bf16[64,512]{1,0:T(8,128)(2,1)S(1)}, u32[]{:S(2)}, u32[]{:S(2)}) collective-permute-start(bf16[64,512]{1,0:T(8,128)(2,1)S(1)} %get-tuple-element.43), channel_id=1, source_target_pairs={{1,0},{2,1},{3,2},{5,4},{6,5},{7,6},{9,8},{10,9},{11,10},{13,12},{... | collective-permute-start | bytes 196616 | tf_op jit(solution)/shard_map/ppermute | solution.py:296
  10.0 7.6 %collective-permute-start.3 = (bf16[256,512]{1,0:T(8,128)(2,1)S(1)}, bf16[256,512]{1,0:T(8,128)(2,1)S(1)}, u32[]{:S(2)}, u32[]{:S(2)}) collective-permute-start(bf16[256,512]{1,0:T(8,128)(2,1)S(1)} %constant_dynamic-update-slice_fusion.12.x_ref), channel_id=1, source_target_pairs={{4,8},{5,9},{6,10},{7,11},{8,4},{9,5},{10,6},{11,7},{12,16},{13,17... | collective-permute-start | bytes 786440 | tf_op jit(solution)/shard_map/ppermute | solution.py:296
  10.6 6.9 %collective-permute-start.2 = (bf16[256,512]{1,0:T(8,128)(2,1)S(1)}, bf16[256,512]{1,0:T(8,128)(2,1)S(1)}, u32[]{:S(2)}, u32[]{:S(2)}) collective-permute-start(bf16[256,512]{1,0:T(8,128)(2,1)S(1)} %constant_dynamic-update-slice_fusion.12.x_ref), channel_id=1, source_target_pairs={{0,4},{1,5},{2,6},{3,7},{4,0},{5,1},{6,2},{7,3},{8,12},{9,13},{10,... | collective-permute-start | bytes 786440 | tf_op jit(solution)/shard_map/ppermute | solution.py:296
  21.5 8.5 %collective-permute-start.4 = (bf16[64,1152]{1,0:T(8,128)(2,1)S(1)}, bf16[64,1152]{1,0:T(8,128)(2,1)S(1)}, u32[]{:S(2)}, u32[]{:S(2)}) collective-permute-start(bf16[64,1152]{1,0:T(8,128)(2,1)S(1)} %get-tuple-element.47), channel_id=1, source_target_pairs={{0,1},{1,2},{2,3},{4,5},{5,6},{6,7},{8,9},{9,10},{10,11},{12,13},{... | collective-permute-start | bytes 442376 | tf_op jit(solution)/shard_map/ppermute | solution.py:296
  22.8 8.3 %collective-permute-start.5 = (bf16[64,1152]{1,0:T(8,128)(2,1)S(1)}, bf16[64,1152]{1,0:T(8,128)(2,1)S(1)}, u32[]{:S(2)}, u32[]{:S(2)}) collective-permute-start(bf16[64,1152]{1,0:T(8,128)(2,1)S(1)} %get-tuple-element.48), channel_id=1, source_target_pairs={{1,0},{2,1},{3,2},{5,4},{6,5},{7,6},{9,8},{10,9},{11,10},{13,12},{... | collective-permute-start | bytes 442376 | tf_op jit(solution)/shard_map/ppermute | solution.py:296
  31.2 5.7 %collective-permute-start.7 = (bf16[256,1152]{1,0:T(8,128)(2,1)S(1)}, bf16[256,1152]{1,0:T(8,128)(2,1)S(1)}, u32[]{:S(2)}, u32[]{:S(2)}) collective-permute-start(bf16[256,1152]{1,0:T(8,128)(2,1)S(1)} %constant_dynamic-update-slice_fusion.p0.g0), channel_id=1, source_target_pairs={{4,8},{5,9},{6,10},{7,11},{8,4},{9,5},{10,6},{11,7},{12,16},{13,17... | collective-permute-start | bytes 1769480 | tf_op jit(solution)/shard_map/ppermute | solution.py:296
  31.9 5.0 %collective-permute-start.6 = (bf16[256,1152]{1,0:T(8,128)(2,1)S(1)}, bf16[256,1152]{1,0:T(8,128)(2,1)S(1)}, u32[]{:S(2)}, u32[]{:S(2)}) collective-permute-start(bf16[256,1152]{1,0:T(8,128)(2,1)S(1)} %constant_dynamic-update-slice_fusion.p0.g0), channel_id=1, source_target_pairs={{0,4},{1,5},{2,6},{3,7},{4,0},{5,1},{6,2},{7,3},{8,12},{9,13},{10,... | collective-permute-start | bytes 1769480 | tf_op jit(solution)/shard_map/ppermute | solution.py:296
  39.1 2.0 %collective-permute-start.8 = (bf16[128,512]{1,0:T(8,128)(2,1)S(1)}, bf16[128,512]{1,0:T(8,128)(2,1)S(1)}, u32[]{:S(2)}, u32[]{:S(2)}) collective-permute-start(bf16[128,512]{1,0:T(8,128)(2,1)S(1)} %get-tuple-element.54), channel_id=1, source_target_pairs={{192,128},{193,129},{194,130},{195,131},{196,132},{197,133},{198,1... | collective-permute-start | bytes 393224 | tf_op jit(solution)/shard_map/ppermute | solution.py:296
  39.8 1.4 collective-permute-start.9
  40.5 0.7 collective-permute-start.10
  41.2 1.9 %collective-permute-start.12 = (bf16[256,512]{1,0:T(8,128)(2,1)S(1)}, bf16[256,512]{1,0:T(8,128)(2,1)S(1)}, u32[]{:S(2)}, u32[]{:S(2)}) collective-permute-start(bf16[256,512]{1,0:T(8,128)(2,1)S(1)} %constant_dynamic-update-slice_fusion.3.g0), channel_id=1, source_target_pairs={{132,136},{133,137},{134,138},{135,139},{136,132},{137,133},{138,1... | collective-permute-start | bytes 786440 | tf_op jit(solution)/shard_map/ppermute | solution.py:296
  41.9 1.3 collective-permute-start.11
  44.0 2.0 %collective-permute-start.13 = (bf16[128,512]{1,0:T(8,128)(2,1)S(1)}, bf16[128,512]{1,0:T(8,128)(2,1)S(1)}, u32[]{:S(2)}, u32[]{:S(2)}) collective-permute-start(bf16[128,512]{1,0:T(8,128)(2,1)S(1)} %get-tuple-element.60), channel_id=1, source_target_pairs={{128,64},{129,65},{130,66},{131,67},{132,68},{133,69},{134,70},{13... | collective-permute-start | bytes 393224 | tf_op jit(solution)/shard_map/ppermute | solution.py:296
  44.7 1.4 collective-permute-start.14
  45.3 0.7 collective-permute-start.15
  46.1 1.9 %collective-permute-start.17 = (bf16[256,512]{1,0:T(8,128)(2,1)S(1)}, bf16[256,512]{1,0:T(8,128)(2,1)S(1)}, u32[]{:S(2)}, u32[]{:S(2)}) collective-permute-start(bf16[256,512]{1,0:T(8,128)(2,1)S(1)} %constant_dynamic-update-slice_fusion.6.g0), channel_id=1, source_target_pairs={{68,72},{69,73},{70,74},{71,75},{72,68},{73,69},{74,70},{75,71},{7... | collective-permute-start | bytes 786440 | tf_op jit(solution)/shard_map/ppermute | solution.py:296
  46.8 1.3 collective-permute-start.16
  48.7 45.4 %collective-permute-start.18 = (bf16[128,512]{1,0:T(8,128)(2,1)S(1)}, bf16[128,512]{1,0:T(8,128)(2,1)S(1)}, u32[]{:S(2)}, u32[]{:S(2)}) collective-permute-start(bf16[128,512]{1,0:T(8,128)(2,1)S(1)} %get-tuple-element.66), channel_id=1, source_target_pairs={{64,0},{65,1},{66,2},{67,3},{68,4},{69,5},{70,6},{71,7},{72,8},{73... | collective-permute-start | bytes 393224 | tf_op jit(solution)/shard_map/ppermute | solution.py:296
  50.0 46.9 %collective-permute-start.19 = (bf16[64,512]{1,0:T(8,128)(2,1)S(1)}, bf16[64,512]{1,0:T(8,128)(2,1)S(1)}, u32[]{:S(2)}, u32[]{:S(2)}) collective-permute-start(bf16[64,512]{1,0:T(8,128)(2,1)S(1)} %get-tuple-element.67), channel_id=1, source_target_pairs={{64,1},{65,2},{66,3},{68,5},{69,6},{70,7},{72,9},{73,10},{74,11},{... | collective-permute-start | bytes 196616 | tf_op jit(solution)/shard_map/ppermute | solution.py:296
  51.3 45.6 %collective-permute-start.20 = (bf16[64,512]{1,0:T(8,128)(2,1)S(1)}, bf16[64,512]{1,0:T(8,128)(2,1)S(1)}, u32[]{:S(2)}, u32[]{:S(2)}) collective-permute-start(bf16[64,512]{1,0:T(8,128)(2,1)S(1)} %get-tuple-element.68), channel_id=1, source_target_pairs={{65,0},{66,1},{67,2},{69,4},{70,5},{71,6},{73,8},{74,9},{75,10},{7... | collective-permute-start | bytes 196616 | tf_op jit(solution)/shard_map/ppermute | solution.py:296
  96.9 9.6 %collective-permute-start.22 = (bf16[256,512]{1,0:T(8,128)(2,1)S(1)}, bf16[256,512]{1,0:T(8,128)(2,1)S(1)}, u32[]{:S(2)}, u32[]{:S(2)}) collective-permute-start(bf16[256,512]{1,0:T(8,128)(2,1)S(1)} %constant_dynamic-update-slice_fusion.9.g0), channel_id=1, source_target_pairs={{4,8},{5,9},{6,10},{7,11},{8,4},{9,5},{10,6},{11,7},{12,16},{13,17... | collective-permute-start | bytes 786440 | tf_op jit(solution)/shard_map/ppermute | solution.py:296
  97.6 8.9 %collective-permute-start.21 = (bf16[256,512]{1,0:T(8,128)(2,1)S(1)}, bf16[256,512]{1,0:T(8,128)(2,1)S(1)}, u32[]{:S(2)}, u32[]{:S(2)}) collective-permute-start(bf16[256,512]{1,0:T(8,128)(2,1)S(1)} %constant_dynamic-update-slice_fusion.9.g0), channel_id=1, source_target_pairs={{0,4},{1,5},{2,6},{3,7},{4,0},{5,1},{6,2},{7,3},{8,12},{9,13},{10,... | collective-permute-start | bytes 786440 | tf_op jit(solution)/shard_map/ppermute | solution.py:296
  110.5 1.7 %collective-permute-start.23 = (bf16[128,1536]{1,0:T(8,128)(2,1)S(1)}, bf16[128,1536]{1,0:T(8,128)(2,1)S(1)}, u32[]{:S(2)}, u32[]{:S(2)}) collective-permute-start(bf16[128,1536]{1,0:T(8,128)(2,1)S(1)} %get-tuple-element.75.d0), channel_id=1, source_target_pairs={{0,4},{1,5},{2,6},{3,7},{4,0},{5,1},{6,2},{7,3},{8,12},{9,13},{10,... | collective-permute-start | bytes 1179656 | tf_op jit(solution)/shard_map/ppermute | solution.py:296
  (7 other events, 8.5 us)

commit v6 on v5

--- a/solution.py
+++ b/solution.py
@@ -17,6 +17,7 @@
 TOK = 128
 OWN = 256
 REGION = 768
+BLOCK = 32
 VMEM_LIMIT = 40 * 1024 * 1024
 
 
@@ -90,18 +91,26 @@
     return (x * inverse).astype(BF16)
 
 
-def own_kernel(where_ref, x_ref, w_ref, cot_ref, proj_ref, nlow_ref, cot_low_ref):
+def centre_kernel(where_ref, x_ref, w_ref, wo_ref, cot_ref, proj_ref, nlow_ref, cot_low_ref, dm_ref):
     low = normed_low(x_ref)
-    nlow_ref[...] = low[:TOK]
+    nlow_ref[...] = low
     proj_ref[...] = nn(low, w_ref[...]).astype(BF16)
-    cot_low_ref[...] = cot_ref[...].astype(BF16)
+    grad = cot_ref[...].astype(BF16)
+    cot_low_ref[...] = grad
+    dm_ref[...] = nt(grad, wo_ref[...]).astype(BF16)
+
+
+def side_kernel(where_ref, left_ref, right_ref, w_ref, proj_ref):
+    low = jnp.concatenate([normed_low(left_ref), normed_low(right_ref)], axis=0)
+    proj_ref[...] = nn(low, w_ref[...]).astype(BF16)
 
 
 def forward_kernel(
-    where_ref, x1, x2, proj_ref, w_ref, cot_ref,
-    kv_ref, prob_ref, nlow_ref, far_ref, pack_ref, left_ref, right_ref,
+    where_ref, x1, x2, proj_ref, side_ref, w_ref, cot_ref, dm_ref,
+    kv_ref, prob_ref, nlow_ref, far_ref, mixed_ref, pack_ref, left_ref, right_ref,
 ):
-    kv_ref[:OWN] = proj_ref[:, D:]
+    kv_ref[:TOK] = proj_ref[:, D:]
+    kv_ref[TOK:OWN] = side_ref[:, D:]
     for piece, x_ref in enumerate((x1, x2)):
         low = normed_low(x_ref)
         far_ref[piece * OWN : (piece + 1) * OWN] = low
@@ -114,7 +123,7 @@
     stats = jnp.zeros((TOK, 128), F32)
     for pair in range(PAIRS):
         at = slice(128 * pair, 128 * pair + 128)
-        query = two_heads(proj_ref[:TOK, at] * 0.125)
+        query = two_heads(proj_ref[:, at] * 0.125)
         scores = nt(query, kv_ref[:, at])
         scores = jnp.where(ok2, scores, -1e30)
         highest = jnp.max(scores, axis=-1, keepdims=True)
@@ -123,38 +132,69 @@
         probs = (grown * (1.0 / total)).astype(BF16)
         prob_ref[pair] = probs
         value = kv_ref[:, D + 128 * pair : D + 128 * pair + 128]
-        pack_ref[:, at] = one_block(nn(probs, value)).astype(BF16)
+        mixed = one_block(nn(probs, value)).astype(BF16)
+        mixed_ref[:, at] = mixed
         log_total = highest + jnp.log(total)
-        rest = log_total
-        for part in range(3):
-            piece = rest.astype(BF16).astype(F32)
-            rest = rest - piece
-            for head in range(2):
-                chosen = lane == 8 * part + 2 * pair + head
-                stats = jnp.where(chosen, piece[TOK * head : TOK * head + TOK], stats)
-    pack_ref[:, D : D + 128] = stats.astype(BF16)
-    pack_ref[:, D + 128 :] = cot_ref[...]
+        delta = two_sums(dm_ref[:, at], mixed)
+        for first, rest in ((0, log_total), (24, delta)):
+            for part in range(3):
+                piece = rest.astype(BF16).astype(F32)
+                rest = rest - piece
+                for head in range(2):
+                    chosen = lane == first + 8 * part + 2 * pair + head
+                    stats = jnp.where(chosen, piece[TOK * head : TOK * head + TOK], stats)
+    starts = where_ref[5] == 0
+    pack_ref[:, D:] = stats.astype(BF16)
+
+    @pl.when(starts)
+    def _():
+        pack_ref[:, :D] = cot_ref[...]
+
+    @pl.when(jnp.logical_not(starts))
+    def _():
+        pack_ref[:, :D] = mixed_ref[...]
+
     put_sides(pack_ref[...].astype(F32), left_ref, right_ref)
 
 
-def turned_kernel(where_ref, proj_ref, far_ref, w_ref, query_ref):
-    query_ref[:, :OWN] = proj_ref[:, :D].astype(F32).T.astype(BF16)
+def turned_kernel(where_ref, proj_ref, side_ref, far_ref, w_ref, n0, n1, query_ref, nt_ref, full_ref):
+    query_ref[:, :TOK] = proj_ref[:, :D].astype(F32).T.astype(BF16)
+    query_ref[:, TOK:OWN] = side_ref[:, :D].astype(F32).T.astype(BF16)
     far = nn(far_ref[...], w_ref[:, :D]).astype(BF16)
     query_ref[:, OWN:] = far.astype(F32).T.astype(BF16)
-
-
-def key_probs_kernel(where_ref, p0, p1, p2, proj_ref, query_ref, prob_ref, mixed_ref):
+    full_ref[:, :TOK] = n0[...].astype(F32).T
+    full_ref[:, TOK:] = n1[...].astype(F32).T
+    nt_ref[...] = own_half(where_ref, full_ref).astype(BF16)
+
+
+def own_half(where_ref, full_ref):
+    rows = [
+        full_ref[pl.ds(pl.multiple_of((2 * at + where_ref[2]) * BLOCK, BLOCK), BLOCK)]
+        for at in range(full_ref.shape[0] // (2 * BLOCK))
+    ]
+    return jnp.concatenate(rows, axis=0)
+
+
+def key_probs_kernel(
+    where_ref, p0, p1, p2, proj_ref, query_ref, prob_ref, mixed_ref, delta_ref
+):
     head = lax.broadcasted_iota(jnp.int32, (8, 128), 0)
     lane = lax.broadcasted_iota(jnp.int32, (8, 128), 1)
-    chosen = ((lane & 7) == head) & (lane < 24)
-    pick = jnp.where(chosen, 1.0, 0.0).astype(BF16)
-    stats = jnp.concatenate([p[:, D : D + 128] for p in (p0, p1, p2)], axis=0)
-    log_total = nt(pick, stats)
-    for piece, p in enumerate((p0, p1, p2)):
-        mixed_ref[:, piece * OWN : (piece + 1) * OWN] = p[:, :D].astype(F32).T.astype(BF16)
+    stats = jnp.concatenate([p[:, D:] for p in (p0, p1, p2)], axis=0)
+    sums = []
+    for first in (0, 24):
+        chosen = ((lane & 7) == head) & (lane >= first) & (lane < first + 24)
+        sums.append(nt(jnp.where(chosen, 1.0, 0.0).astype(BF16), stats))
+    log_total, delta_ref[...] = sums
+
+    @pl.when(where_ref[5] != 0)
+    def _():
+        for piece, p in enumerate((p0, p1, p2)):
+            mixed_ref[:, piece * OWN : (piece + 1) * OWN] = p[:, :D].astype(F32).T.astype(BF16)
+
     ok = window(where_ref, True)
     for pair in range(PAIRS):
-        key = two_heads(proj_ref[:TOK, D + 128 * pair : D + 128 * pair + 128] * 0.125)
+        key = two_heads(proj_ref[:, D + 128 * pair : D + 128 * pair + 128] * 0.125)
         scores = nn(key, query_ref[128 * pair : 128 * pair + 128])
         for side in range(2):
             at = 2 * pair + side
@@ -163,22 +203,26 @@
             prob_ref[pair, TOK * side : TOK * side + TOK] = probs.astype(BF16)
 
 
-def query_kernel(where_ref, g_ref, w_ref, pack_ref, kv_ref, prob_ref, dq_ref, *, turn):
+def two_sums(grad, mixed):
+    prod = grad.astype(F32) * mixed.astype(F32)
+    lane = lax.broadcasted_iota(jnp.int32, prod.shape, 1)
+    return jnp.concatenate(
+        [
+            jnp.sum(jnp.where(lane < 64, prod, 0.0), axis=-1, keepdims=True),
+            jnp.sum(jnp.where(lane < 64, 0.0, prod), axis=-1, keepdims=True),
+        ],
+        axis=0,
+    )
+
+
+def query_kernel(where_ref, g_ref, w_ref, mixed_ref, kv_ref, prob_ref, dq_ref, *, turn):
     @pl.when(where_ref[5] == turn)
     def _():
-        d_mixed = nt(g_ref[...].astype(BF16), w_ref[...]).astype(BF16)
-        lane = lax.broadcasted_iota(jnp.int32, (TOK, 128), 1)
+        d_mixed = nt(g_ref[...], w_ref[...]).astype(BF16)
         for pair in range(PAIRS):
             at = slice(128 * pair, 128 * pair + 128)
             grad = d_mixed[:, at]
-            prod = grad.astype(F32) * pack_ref[:, at].astype(F32)
-            delta = jnp.concatenate(
-                [
-                    jnp.sum(jnp.where(lane < 64, prod, 0.0), axis=-1, keepdims=True),
-                    jnp.sum(jnp.where(lane < 64, 0.0, prod), axis=-1, keepdims=True),
-                ],
-                axis=0,
-            )
+            delta = two_sums(grad, mixed_ref[:, at])
             value = kv_ref[:, D + 128 * pair : D + 128 * pair + 128]
             pressure = nt(two_heads(grad), value)
             slopes = (prob_ref[pair].astype(F32) * (pressure - delta)).astype(BF16)
@@ -191,70 +235,94 @@
 
 
 def key_kernel(
-    where_ref, g_ref, g0, g1, g2, wo_ref, mixed_ref, proj_ref, query_ref, prob_ref, dq_ref, wq_ref,
-    x_ref, *rest, turn,
+    where_ref, g0, g1, g2, wo_ref, delta_ref, proj_ref, query_ref, prob_ref, dq_ref, mixed_ref,
+    *rest, turn, last,
 ):
-    prev, rest = (rest[:3], rest[3:]) if turn else ((), rest)
-    (in_ref, dp_ref, gl_ref), sends, dm_ref = rest[:3], rest[3:-1], rest[-1]
+    ins, rest = ((), rest) if last else (rest[:3], rest[3:])
+    prev = (3 - last) if turn else 0
+    prev, rest = rest[:prev], rest[prev:]
+    outs, sends, dm_ref = rest[: 3 - last], rest[3 - last : -1], rest[-1]
+    dp_ref, gl_ref = outs[:2]
     active = where_ref[5] == turn
 
     if prev:
 
         @pl.when(jnp.logical_not(active))
         def _():
-            for new, old in zip((in_ref, dp_ref, gl_ref), prev):
+            for new, old in zip(outs, prev):
                 new[...] = old[...]
 
     @pl.when(active)
     def _():
         for piece, g in enumerate((g0, g1, g2)):
-            d_mixed = nt(wo_ref[...], g[:, -D:]).astype(BF16)
+            d_mixed = nt(wo_ref[...], g[:, :D]).astype(BF16)
             dm_ref[:, piece * OWN : (piece + 1) * OWN] = d_mixed
         dp_ref[:, :D] = dq_ref[...]
+        dp_ref[:, 3 * D :] = mixed_ref[...]
+        gl_ref[:TOK] = g0[:TOK, :D]
+        gl_ref[TOK:] = g1[:TOK, :D]
         for pair in range(PAIRS):
             at = slice(128 * pair, 128 * pair + 128)
-            value = two_heads(proj_ref[:TOK, 2 * D + 128 * pair : 2 * D + 128 * pair + 128])
+            value = two_heads(proj_ref[:, 2 * D + 128 * pair : 2 * D + 128 * pair + 128])
             grad = dm_ref[at]
-            prod = grad.astype(F32) * mixed_ref[at].astype(F32)
+            if turn:
+                prod = grad.astype(F32) * delta_ref[at].astype(F32)
+                deltas = [jnp.sum(prod[r : r + 64], axis=0, keepdims=True) for r in (0, 64)]
+            else:
+                deltas = [delta_ref[2 * pair + side : 2 * pair + side + 1] for side in range(2)]
             pressure = nn(value, grad)
             probs = prob_ref[pair]
             d_value = nt(grad, probs)
             slopes = []
             for side in range(2):
-                delta = jnp.sum(prod[64 * side : 64 * side + 64], axis=0, keepdims=True)
                 rows = slice(TOK * side, TOK * side + TOK)
-                slopes.append((probs[rows].astype(F32) * (pressure[rows] - delta)).astype(BF16))
+                slopes.append(
+                    (probs[rows].astype(F32) * (pressure[rows] - deltas[side])).astype(BF16)
+                )
             d_key = nt(query_ref[at], jnp.concatenate(slopes, axis=0))
             low, high = D + 128 * pair, D + 128 * pair + 128
             dp_ref[:, low:high] = (turned_block(d_key) * 0.125).astype(BF16)
             dp_ref[:, D + low : D + high] = turned_block(d_value).astype(BF16)
-        d_normed = nt(dp_ref[...], wq_ref[...])
-        x = x_ref[...].astype(F32)
-        inverse = lax.rsqrt(jnp.mean(x * x, axis=-1, keepdims=True) + 1e-06)
-        normed = x * inverse
-        inner = jnp.mean(d_normed * normed, axis=-1, keepdims=True)
-        gradient = g_ref[...].astype(F32)
-        out = gradient + inverse * (d_normed - normed * inner)
-        in_ref[...] = out
-        gl_ref[:TOK] = g_ref[...].astype(BF16)
-        gl_ref[TOK:] = g1[:TOK, -D:]
-        if sends:
+        if not last:
+            out = input_grad(dp_ref, *ins)
+            outs[2][...] = out
             low_ref, left_ref, right_ref = sends
             low_ref[...] = out.astype(BF16)
             put_sides(out, left_ref, right_ref)
 
 
-def weight_kernel(where_ref, n0, n1, d0, d1, m0, m1, g_ref, out_ref, full_ref):
-    core = where_ref[2]
-    full_ref[:, : 3 * D] = tn(n0[...], d0[...]) + tn(n1[...], d1[...])
-    full_ref[:, 3 * D :] = tn(m0[:, :D], g_ref[:TOK]) + tn(m1[:TOK, :D], g_ref[TOK:])
-    chips, cols = out_ref.shape[1] // 8, out_ref.shape[0]
+def input_grad(dp_ref, g_ref, wq_ref, x_ref):
+    d_normed = nt(dp_ref[:, : 3 * D], wq_ref[...])
+    x = x_ref[...].astype(F32)
+    inverse = lax.rsqrt(jnp.mean(x * x, axis=-1, keepdims=True) + 1e-06)
+    normed = x * inverse
+    inner = jnp.mean(d_normed * normed, axis=-1, keepdims=True)
+    return g_ref[...].astype(F32) + inverse * (d_normed - normed * inner)
+
+
+def input_kernel(where_ref, dp_ref, g_ref, wq_ref, x_ref, prev_ref, in_ref, *, turn):
+    @pl.when(where_ref[5] == turn)
+    def _():
+        in_ref[...] = input_grad(dp_ref, g_ref, wq_ref, x_ref)
+
+    @pl.when(where_ref[5] != turn)
+    def _():
+        in_ref[...] = prev_ref[...]
+
+
+def weight_kernel(where_ref, nt_ref, d0, d1, g_ref, out_ref, full_ref):
+    d_proj = jnp.concatenate([d0[:, : 3 * D], d1[:, : 3 * D]], axis=0)
+    mixed = jnp.concatenate([d0[:, 3 * D :], d1[:, 3 * D :]], axis=0)
+    full_ref[...] = tn(mixed, g_ref[...])
+    left, right = nn(nt_ref[...], d_proj), own_half(where_ref, full_ref)
+    cols = out_ref.shape[0]
     for col in range(cols):
-        rows = [
-            full_ref[pl.ds(pl.multiple_of((2 * chip + core) * (8 * cols) + 8 * col, 8), 8)]
-            for chip in range(chips)
-        ]
-        out_ref[col] = jnp.concatenate(rows, axis=0).astype(BF16)
+        for at, part in ((slice(0, 3 * D), left), (slice(3 * D, 4 * D), right)):
+            rows = [
+                part[BLOCK * chip + 8 * col : BLOCK * chip + 8 * col + 8]
+                for chip in range(out_ref.shape[1] // 8)
+            ]
+            out_ref[col, :, at] = jnp.concatenate(rows, axis=0).astype(BF16)
 
 
 def total_kernel(where_ref, part_ref, qkv_ref, out_ref, *, scale):
@@ -320,29 +388,37 @@
     base, low_side, high_side = call(
         first_kernel, [((OWN, D), BF16), ((64, D), BF16), ((64, D), BF16)], where, x
     )
+    proj, nlow, cot_low, d_mixed = call(
+        centre_kernel, [((TOK, 3 * D), BF16), ((TOK, D), BF16), ((TOK, D), BF16), ((TOK, D), BF16)],
+        where, x, w_qkv, w_out, cot, flops=1 << 28,
+    )
     left, right = col_rims(low_side, high_side)
+    base, proj = lax.optimization_barrier((base, proj))
     own = lax.dynamic_update_slice(base, left, (TOK, 0))
     own, near, far = row_rims([lax.dynamic_update_slice(own, right, (TOK + 64, 0))])
-    proj, nlow, cot_low = call(
-        own_kernel, [((OWN, 3 * D), BF16), ((TOK, D), BF16), ((TOK, D), BF16)],
-        where, own, w_qkv, cot, flops=1 << 29,
-    )
-    wide = 2 * D + 128
-    kv, q_probs, nlow_mate, low_far, pack, low_side, high_side = call(
+    (side_proj,) = call(
+        side_kernel, [((TOK, 3 * D), BF16)], where, left, right, w_qkv, flops=1 << 28
+    )
+    wide = D + 128
+    kv, q_probs, nlow_mate, low_far, mixed, pack, low_side, high_side = call(
         forward_kernel,
         [((REGION, 2 * D), BF16), ((PAIRS, OWN, REGION), BF16), ((TOK, D), BF16),
-         ((2 * OWN, D), BF16), ((TOK, wide), BF16), ((64, wide), BF16), ((64, wide), BF16)],
-        where, near, far, proj, w_qkv, cot_low, flops=2 << 30,
+         ((2 * OWN, D), BF16), ((TOK, D), BF16), ((TOK, wide), BF16), ((64, wide), BF16),
+         ((64, wide), BF16)],
+        where, near, far, proj, side_proj, w_qkv, cot_low, d_mixed, flops=2 << 30,
     )
     packs = row_rims([pack, *col_rims(low_side, high_side)])
-    (queries,) = call(
-        turned_kernel, [((D, REGION), BF16)], where, proj, low_far, w_qkv, flops=1 << 28
-    )
-    k_probs, mixed = call(
-        key_probs_kernel, [((PAIRS, OWN, REGION), BF16), ((D, REGION), BF16)],
+    queries, n_turned = call(
+        turned_kernel, [((D, REGION), BF16), ((OWN, OWN), BF16)],
+        where, proj, side_proj, low_far, w_qkv, nlow, nlow_mate,
+        scratch=[pltpu.VMEM((D, OWN), F32)], flops=1 << 28,
+    )
+    k_probs, mixed_turned, delta = call(
+        key_probs_kernel,
+        [((PAIRS, OWN, REGION), BF16), ((D, REGION), BF16), ((8, REGION), F32)],
         where, *packs, proj, queries, flops=1 << 28,
     )
-    gradient, gs = cot, packs
+    gradient, gs = cot_low, packs
     state = ()
     for turn in range(pipes):
         plane, last = pipes - 1 - turn, turn == pipes - 1
@@ -352,21 +428,29 @@
             gs = row_rims([gradient, *col_rims(low_side, high_side, 1, plane + 1)], plane)
         (d_query,) = call(
             functools.partial(query_kernel, turn=turn), [((TOK, D), BF16)],
-            where, gradient, w_out, pack, kv, q_probs, flops=1 << 29,
+            where, gradient, w_out, mixed, kv, q_probs, flops=1 << 29,
         )
-        halves = [((TOK, D), BF16), ((64, D), BF16), ((64, D), BF16)]
+        outs = [((TOK, 4 * D), BF16), ((OWN, D), BF16)]
+        if not last:
+            outs += [((TOK, D), F32), ((TOK, D), BF16), ((64, D), BF16), ((64, D), BF16)]
+        ins = () if last else (gradient if turn else cot, w_qkv, x)
         outs = call(
-            functools.partial(key_kernel, turn=turn),
-            [((TOK, D), F32), ((TOK, 3 * D), BF16), ((OWN, D), BF16)] + ([] if last else halves),
-            where, gradient, *gs, w_out, mixed, proj, queries, k_probs, d_query, w_qkv, x, *state,
+            functools.partial(key_kernel, turn=turn, last=last), outs,
+            where, *gs, w_out, mixed_turned if turn else delta, proj, queries, k_probs, d_query,
+            mixed, *ins, *state[: 2 if last else 3],
             scratch=[pltpu.VMEM((D, REGION), BF16)], flops=1 << 30,
         )
+        if last:
+            d_proj, g_low = outs
+            (d_in,) = call(
+                functools.partial(input_kernel, turn=turn), [((TOK, D), F32)],
+                where, d_proj, gradient, w_qkv, x, state[2], flops=1 << 28,
+            )
         state, sends = outs[:3], outs[3:]
-    d_in, d_proj, g_low = state
     (part,) = call(
         weight_kernel, [((cols, 8 * chips, 4 * D), BF16)],
-        where, nlow, nlow_mate, d_proj, routed(d_proj, mate), pack, packs[1], g_low,
-        scratch=[pltpu.VMEM((D, 4 * D), F32)], flops=1 << 30,
+        where, n_turned, d_proj, routed(d_proj, mate), g_low,
+        scratch=[pltpu.VMEM((D, D), F32)], flops=1 << 29,
     )
     part = lax.all_to_all(part, "col", 0, 0, tiled=True)
     part = jnp.sum(part.astype(F32), axis=0).astype(BF16).reshape(chips, 8, 4 * D)

time: 156 us -> 155 us (level)
  blocking collectives: 38.9 us -> 20.8 us
  starting transfers between devices: 37.7 us -> 47.9 us
  waiting for transfers between devices: 51.9 us -> 54.7 us
  other arithmetic: 0.2 us -> 2.15 us
    all_to_all x1 -> x0, blocking collectives: 18.3 us -> none  [body(): part = lax.all_to_all(part, 'z', 0, 0, tiled=True)]
    all_to_all x0 -> x1, starting transfers between devices: none -> 8.98 us  [body(): part = lax.all_to_all(part, 'z', 0, 0, tiled=True)]
    all_to_all x0 -> x1, waiting for transfers between devices: none -> 8.74 us  [body(): part = lax.all_to_all(part, 'z', 0, 0, tiled=True)]
    ppermute x24, waiting for transfers between devices: 51.9 us -> 46 us  [routed(): return lax.ppermute(block, AXES, pairs)]
    reduce_sum x1, other arithmetic: 0.2 us -> 2.15 us  [body(): jnp.sum(part.astype(F32), axis=0).astype(BF16).reshape(chips, 8, 4 * D)]
    pallas_call x15 -> x17, Pallas kernels: 20.9 us -> 22.3 us  [call(): pl.pallas_call(kernel, out_shape=[jax.ShapeDtypeStruct(s, t) for s, t in...]
  transfers between devices with their start and end apart: 24 -> 25, of which waited for: 7 -> 7; matrix products, arithmetic and copies ran while one was open for 0% -> 0% of each run, Pallas kernels for 4% -> 6%
where the time goes in v6:
time: 155 us; the launch traced here: 154 us
  waiting for transfers between devices  54.7 us (35%)
  starting transfers between devices  47.9 us (31%)
  Pallas kernels  22.3 us (14%)
  blocking collectives  20.8 us (13%)
  local copies, waits for them, and re-layouts  4.53 us (3%)
  other arithmetic  2.15 us (1%)
    ppermute x24, waiting for transfers between devices, routed(): return lax.ppermute(block, AXES, pairs)  46 us
    ppermute x24, starting transfers between devices, routed(): return lax.ppermute(block, AXES, pairs)  38.9 us
    pallas_call x17, Pallas kernels, call(): pl.pallas_call(kernel, out_shape=[jax.ShapeDtypeStruct(s, t) for s, t in...  22.3 us
    all_to_all x1, blocking collectives, body(): part = lax.all_to_all(part, 'col', 0, 0, tiled=True)  20.8 us
    all_to_all x1, starting transfers between devices, body(): part = lax.all_to_all(part, 'z', 0, 0, tiled=True)  8.98 us
    all_to_all x1, waiting for transfers between devices, body(): part = lax.all_to_all(part, 'z', 0, 0, tiled=True)  8.74 us
    unnamed x22, local copies, waits for them, and re-layouts  4.39 us
  transfers between devices with their start and end apart: 25, of which 7 were waited for; matrix products, arithmetic and copies ran while one was open for 0% of the time, Pallas kernels for 6%

profile of v6, /device:TPU:6, one launch (start us, length us, event | category | flops | bytes accessed | tf_op | source)
XLA Modules:
  0.0 153.6 jit_solution(6427911578870673350)
XLA Ops:
  2.2 1.3 collective-permute-start
  3.5 4.5 %collective-permute-start.1 = (bf16[64,512]{1,0:T(8,128)(2,1)S(1)}, bf16[64,512]{1,0:T(8,128)(2,1)S(1)}, u32[]{:S(2)}, u32[]{:S(2)}) collective-permute-start(bf16[64,512]{1,0:T(8,128)(2,1)S(1)} %get-tuple-element.51), channel_id=1, source_target_pairs={{1,0},{2,1},{3,2},{5,4},{6,5},{7,6},{9,8},{10,9},{11,10},{13,12},{... | collective-permute-start | bytes 196616 | tf_op jit(solution)/shard_map/ppermute | solution.py:364
  8.1 1.4 copy-done
  13.4 3.4 %collective-permute-start.2 = (bf16[256,512]{1,0:T(8,128)(2,1)S(1)}, bf16[256,512]{1,0:T(8,128)(2,1)S(1)}, u32[]{:S(2)}, u32[]{:S(2)}) collective-permute-start(bf16[256,512]{1,0:T(8,128)(2,1)S(1)} %constant_dynamic-update-slice_fusion.12), channel_id=1, source_target_pairs={{0,4},{1,5},{2,6},{3,7},{4,0},{5,1},{6,2},{7,3},{8,12},{9,13},{10,... | collective-permute-start | bytes 786440 | tf_op jit(solution)/shard_map/ppermute | solution.py:364
  17.9 4.0 %shard_map.70 = (bf16[768,1024]{1,0:T(8,128)(2,1)S(1)}, bf16[4,256,768]{2,1,0:T(8,128)(2,1)S(1)}, bf16[128,512]{1,0:T(8,128)(2,1)S(1)}, bf16[512,512]{1,0:T(8,12...) custom-call(s32[6]{0:T(128)S(1)} %stack.19.where_ref, ...), custom_call_target="tpu_custom_call" | custom-call | flops 2147483648 | bytes 4194304 | tf_op jit(solution)/shard_map/pallas_call | solution.py:338
  21.9 1.3 collective-permute-start.4
  23.2 4.6 %collective-permute-start.5 = (bf16[64,640]{1,0:T(8,128)(2,1)S(1)}, bf16[64,640]{1,0:T(8,128)(2,1)S(1)}, u32[]{:S(2)}, u32[]{:S(2)}) collective-permute-start(bf16[64,640]{1,0:T(8,128)(2,1)S(1)} %get-tuple-element.57), channel_id=1, source_target_pairs={{1,0},{2,1},{3,2},{5,4},{6,5},{7,6},{9,8},{10,9},{11,10},{13,12},{... | collective-permute-start | bytes 245768 | tf_op jit(solution)/shard_map/ppermute | solution.py:364
  28.2 1.5 %collective-permute-done.5 = bf16[64,640]{1,0:T(8,128)(2,1)S(1)} collective-permute-done((bf16[64,640]{1,0:T(8,128)(2,1)S(1)}, bf16[64,640]{1,0:T(8,128)(2,1)S(1)}, u32[]{:S(2)}, u32[]{:S(2)}) %collective-permute-start.5) | collective-permute-done | bytes 81952 | tf_op jit(solution)/shard_map/ppermute | solution.py:364
  30.5 5.8 %collective-permute-start.6 = (bf16[256,640]{1,0:T(8,128)(2,1)S(1)}, bf16[256,640]{1,0:T(8,128)(2,1)S(1)}, u32[]{:S(2)}, u32[]{:S(2)}) collective-permute-start(bf16[256,640]{1,0:T(8,128)(2,1)S(1)} %constant_dynamic-update-slice_fusion.p0.g0), channel_id=1, source_target_pairs={{0,4},{1,5},{2,6},{3,7},{4,0},{5,1},{6,2},{7,3},{8,12},{9,13},{10,... | collective-permute-start | bytes 983048 | tf_op jit(solution)/shard_map/ppermute | solution.py:364
  38.0 1.9 %shard_map.72 = (bf16[4,256,768]{2,1,0:T(8,128)(2,1)S(1)}, bf16[512,768]{1,0:T(8,128)(2,1)S(1)}, f32[8,768]{1,0:T(8,128)S(1)}) custom-call(s32[6]{0:T(128)S(1)} %stack.19.where_ref, bf16[256,640]{1,0:T(8,128)(2,1)S(1)} %constant_dynamic-update-slice_fusion.p0.g0, bf16[256,640]{1,0:T(8,128)(2,1)S(1)} %collective-permute-done.6.p1.g1, ...), custom_call_target="tpu_custom_call" | custom-call | flops 268435456 | bytes 4194304 | tf_op jit(solution)/shard_map/pallas_call | solution.py:338
  50.1 1.3 collective-permute-start.18
  51.4 1.3 collective-permute-start.19
  53.4 39.2 %collective-permute-done.18.g_ref = bf16[128,512]{1,0:T(8,128)(2,1)S(1)} collective-permute-done((bf16[128,512]{1,0:T(8,128)(2,1)S(1)}, bf16[128,512]{1,0:T(8,128)(2,1)S(1)}, u32[]{:S(2)}, u32[]{:S(2)}) %collective-permute-start.18) | collective-permute-done | bytes 131104 | tf_op jit(solution)/shard_map/ppermute | solution.py:364
  92.6 2.8 %collective-permute-done.19 = bf16[64,512]{1,0:T(8,128)(2,1)S(1)} collective-permute-done((bf16[64,512]{1,0:T(8,128)(2,1)S(1)}, bf16[64,512]{1,0:T(8,128)(2,1)S(1)}, u32[]{:S(2)}, u32[]{:S(2)}) %collective-permute-start.19) | collective-permute-done | bytes 65568 | tf_op jit(solution)/shard_map/ppermute | solution.py:364
  96.1 5.9 %collective-permute-start.21 = (bf16[256,512]{1,0:T(8,128)(2,1)S(1)}, bf16[256,512]{1,0:T(8,128)(2,1)S(1)}, u32[]{:S(2)}, u32[]{:S(2)}) collective-permute-start(bf16[256,512]{1,0:T(8,128)(2,1)S(1)} %constant_dynamic-update-slice_fusion.9.g0), channel_id=1, source_target_pairs={{0,4},{1,5},{2,6},{3,7},{4,0},{5,1},{6,2},{7,3},{8,12},{9,13},{10,... | collective-permute-start | bytes 786440 | tf_op jit(solution)/shard_map/ppermute | solution.py:364
  102.0 2.0 %shard_map.79.dq_ref = bf16[128,512]{1,0:T(8,128)(2,1)S(1)} custom-call(s32[6]{0:T(128)S(1)} %stack.19.where_ref, bf16[128,512]{1,0:T(8,128)(2,1)S(1)} %collective-permute-done.18.g_ref, bf16[512,512]{1,0:T(8,128)(2,1)S(1)} %bitcast.27, bf16[128,512]{1,0:T(8,128)(2,1)S(1)} %get-tuple-element.64.mixed_ref, bf16[768,1024]{1,0:T(8,128)(2,1)S(1)} %get-tuple-element.65.kv_ref, ...), custom_call_target="tpu_custom_call" | custom-call | flops 536870912 | bytes 4194304 | tf_op jit(solution)/shard_map/pallas_call | solution.py:338
  104.0 2.7 %shard_map.80 = (bf16[128,2048]{1,0:T(8,128)(2,1)S(1)}, bf16[256,512]{1,0:T(8,128)(2,1)S(1)}) custom-call(s32[6]{0:T(128)S(1)} %stack.19.where_ref, bf16[256,512]{1,0:T(8,128)(2,1)S(1)} %constant_dynamic-update-slice_fusion.9.g0, bf16[256,512]{1,0:T(8,128)(2,1)S(1)} %collective-permute-done.21.g1, bf16[256,512]{1,0:T(8,128)(2,1)S(1)} %collective-permute-done.22.g2, ...), custom_call_target="tpu_custom_call" | custom-call | flops 1073741824 | bytes 4194304 | tf_op jit(solution)/shard_map/pallas_call | solution.py:338
  106.9 1.8 %collective-permute-done.23.d1 = bf16[128,2048]{1,0:T(8,128)(2,1)S(1)} collective-permute-done((bf16[128,2048]{1,0:T(8,128)(2,1)S(1)}, bf16[128,2048]{1,0:T(8,128)(2,1)S(1)}, u32[]{:S(2)}, u32[]{:S(2)}) %collective-permute-start.23) | collective-permute-done | bytes 524320 | tf_op jit(solution)/shard_map/ppermute | solution.py:364
  109.8 20.8 %all_to_all.10 = bf16[4,64,2048]{2,1,0:T(8,128)(2,1)} all-to-all(bf16[4,64,2048]{2,1,0:T(8,128)(2,1)S(1)} %shard_map.82), channel_id=1, replica_groups=mesh['pipe'=4,'z'=8,'core'=2,'col'=4] {'col'}, dimensions={0} | all-to-all | bytes 2097152 | tf_op jit(solution)/shard_map/all_to_all | solution.py:455
  130.5 2.2 %reduce_sum.12 = bf16[64,2048]{1,0:T(8,128)(2,1)} reduce(bf16[4,64,2048]{2,1,0:T(8,128)(2,1)} %all_to_all.10, bf16[]{:T(256)} %constant.37.clone.1), dimensions={0}, to_apply=%region_0.0 | reduce | flops 393216 | bytes 1310722 | tf_op jit(solution)/shard_map/reduce_sum | solution.py:456
  132.7 9.0 %all-to-all-start.1 = ((bf16[8,8,2048]{2,1,0:T(8,128)(2,1)}), bf16[8,8,2048]{2,1,0:T(8,128)(2,1)S(1)}, u32[]{:S(2)}, u32[]{:S(2)}) async-start(bf16[8,8,2048]{2,1,0:T(8,128)(2,1)} %bitcast.9), calls=%async_computation.1 | async-start | bytes 524288 | tf_op jit(solution)/shard_map/all_to_all | solution.py:457
  141.7 2.0 %shard_map.81 = f32[128,512]{1,0:T(8,128)} custom-call(s32[6]{0:T(128)S(1)} %stack.19.where_ref, bf16[128,2048]{1,0:T(8,128)(2,1)S(1)} %get-tuple-element.85.dp_ref.d0, bf16[128,512]{1,0:T(8,128)(2,1)S(1)} %collective-permute-done.18.g_ref, bf16[512,1536]{1,0:T(8,128)(2,1)S(1)} %bitcast.19, bf16[128,512]{1,0:T(8,128)(2,1)S(1)} %bitcast.34, ...), custom_call_target="tpu_custom_call" | custom-call | flops 268435456 | bytes 4194304 | tf_op jit(solution)/shard_map/pallas_call | solution.py:338
  143.7 8.7 %all-to-all-done.1.part_ref = bf16[8,8,2048]{2,1,0:T(8,128)(2,1)S(1)} async-done(((bf16[8,8,2048]{2,1,0:T(8,128)(2,1)}), bf16[8,8,2048]{2,1,0:T(8,128)(2,1)S(1)}, u32[]{:S(2)}, u32[]{:S(2)}) %all-to-all-start.1) | async-done | bytes 262176 | tf_op jit(solution)/shard_map/all_to_all | solution.py:457
  152.4 1.2 shard_map.83
  (74 shorter events, 21.9 us)
Async XLA Ops:
  2.2 10.4 %collective-permute-start = (bf16[64,512]{1,0:T(8,128)(2,1)S(1)}, bf16[64,512]{1,0:T(8,128)(2,1)S(1)}, u32[]{:S(2)}, u32[]{:S(2)}) collective-permute-start(bf16[64,512]{1,0:T(8,128)(2,1)S(1)} %get-tuple-element.50), channel_id=1, source_target_pairs={{0,1},{1,2},{2,3},{4,5},{5,6},{6,7},{8,9},{9,10},{10,11},{12,13},{... | collective-permute-start | bytes 196616 | tf_op jit(solution)/shard_map/ppermute | solution.py:364
  3.5 9.1 %collective-permute-start.1 = (bf16[64,512]{1,0:T(8,128)(2,1)S(1)}, bf16[64,512]{1,0:T(8,128)(2,1)S(1)}, u32[]{:S(2)}, u32[]{:S(2)}) collective-permute-start(bf16[64,512]{1,0:T(8,128)(2,1)S(1)} %get-tuple-element.51), channel_id=1, source_target_pairs={{1,0},{2,1},{3,2},{5,4},{6,5},{7,6},{9,8},{10,9},{11,10},{13,12},{... | collective-permute-start | bytes 196616 | tf_op jit(solution)/shard_map/ppermute | solution.py:364
  12.7 5.0 %collective-permute-start.3 = (bf16[256,512]{1,0:T(8,128)(2,1)S(1)}, bf16[256,512]{1,0:T(8,128)(2,1)S(1)}, u32[]{:S(2)}, u32[]{:S(2)}) collective-permute-start(bf16[256,512]{1,0:T(8,128)(2,1)S(1)} %constant_dynamic-update-slice_fusion.12), channel_id=1, source_target_pairs={{4,8},{5,9},{6,10},{7,11},{8,4},{9,5},{10,6},{11,7},{12,16},{13,17... | collective-permute-start | bytes 786440 | tf_op jit(solution)/shard_map/ppermute | solution.py:364
  13.4 4.5 %collective-permute-start.2 = (bf16[256,512]{1,0:T(8,128)(2,1)S(1)}, bf16[256,512]{1,0:T(8,128)(2,1)S(1)}, u32[]{:S(2)}, u32[]{:S(2)}) collective-permute-start(bf16[256,512]{1,0:T(8,128)(2,1)S(1)} %constant_dynamic-update-slice_fusion.12), channel_id=1, source_target_pairs={{0,4},{1,5},{2,6},{3,7},{4,0},{5,1},{6,2},{7,3},{8,12},{9,13},{10,... | collective-permute-start | bytes 786440 | tf_op jit(solution)/shard_map/ppermute | solution.py:364
  21.9 6.3 %collective-permute-start.4 = (bf16[64,640]{1,0:T(8,128)(2,1)S(1)}, bf16[64,640]{1,0:T(8,128)(2,1)S(1)}, u32[]{:S(2)}, u32[]{:S(2)}) collective-permute-start(bf16[64,640]{1,0:T(8,128)(2,1)S(1)} %get-tuple-element.56), channel_id=1, source_target_pairs={{0,1},{1,2},{2,3},{4,5},{5,6},{6,7},{8,9},{9,10},{10,11},{12,13},{... | collective-permute-start | bytes 245768 | tf_op jit(solution)/shard_map/ppermute | solution.py:364
  23.2 6.6 %collective-permute-start.5 = (bf16[64,640]{1,0:T(8,128)(2,1)S(1)}, bf16[64,640]{1,0:T(8,128)(2,1)S(1)}, u32[]{:S(2)}, u32[]{:S(2)}) collective-permute-start(bf16[64,640]{1,0:T(8,128)(2,1)S(1)} %get-tuple-element.57), channel_id=1, source_target_pairs={{1,0},{2,1},{3,2},{5,4},{6,5},{7,6},{9,8},{10,9},{11,10},{13,12},{... | collective-permute-start | bytes 245768 | tf_op jit(solution)/shard_map/ppermute | solution.py:364
  29.8 8.2 %collective-permute-start.7 = (bf16[256,640]{1,0:T(8,128)(2,1)S(1)}, bf16[256,640]{1,0:T(8,128)(2,1)S(1)}, u32[]{:S(2)}, u32[]{:S(2)}) collective-permute-start(bf16[256,640]{1,0:T(8,128)(2,1)S(1)} %constant_dynamic-update-slice_fusion.p0.g0), channel_id=1, source_target_pairs={{4,8},{5,9},{6,10},{7,11},{8,4},{9,5},{10,6},{11,7},{12,16},{13,17... | collective-permute-start | bytes 983048 | tf_op jit(solution)/shard_map/ppermute | solution.py:364
  30.5 7.5 %collective-permute-start.6 = (bf16[256,640]{1,0:T(8,128)(2,1)S(1)}, bf16[256,640]{1,0:T(8,128)(2,1)S(1)}, u32[]{:S(2)}, u32[]{:S(2)}) collective-permute-start(bf16[256,640]{1,0:T(8,128)(2,1)S(1)} %constant_dynamic-update-slice_fusion.p0.g0), channel_id=1, source_target_pairs={{0,4},{1,5},{2,6},{3,7},{4,0},{5,1},{6,2},{7,3},{8,12},{9,13},{10,... | collective-permute-start | bytes 983048 | tf_op jit(solution)/shard_map/ppermute | solution.py:364
  40.5 2.0 %collective-permute-start.8 = (bf16[128,512]{1,0:T(8,128)(2,1)S(1)}, bf16[128,512]{1,0:T(8,128)(2,1)S(1)}, u32[]{:S(2)}, u32[]{:S(2)}) collective-permute-start(bf16[128,512]{1,0:T(8,128)(2,1)S(1)} %get-tuple-element.67), channel_id=1, source_target_pairs={{192,128},{193,129},{194,130},{195,131},{196,132},{197,133},{198,1... | collective-permute-start | bytes 393224 | tf_op jit(solution)/shard_map/ppermute | solution.py:364
  41.2 1.4 collective-permute-start.9
  41.9 0.7 collective-permute-start.10
  42.6 2.1 %collective-permute-start.12 = (bf16[256,512]{1,0:T(8,128)(2,1)S(1)}, bf16[256,512]{1,0:T(8,128)(2,1)S(1)}, u32[]{:S(2)}, u32[]{:S(2)}) collective-permute-start(bf16[256,512]{1,0:T(8,128)(2,1)S(1)} %constant_dynamic-update-slice_fusion.3.g0), channel_id=1, source_target_pairs={{132,136},{133,137},{134,138},{135,139},{136,132},{137,133},{138,1... | collective-permute-start | bytes 786440 | tf_op jit(solution)/shard_map/ppermute | solution.py:364
  43.3 1.4 collective-permute-start.11
  45.4 2.0 %collective-permute-start.13 = (bf16[128,512]{1,0:T(8,128)(2,1)S(1)}, bf16[128,512]{1,0:T(8,128)(2,1)S(1)}, u32[]{:S(2)}, u32[]{:S(2)}) collective-permute-start(bf16[128,512]{1,0:T(8,128)(2,1)S(1)} %get-tuple-element.74), channel_id=1, source_target_pairs={{128,64},{129,65},{130,66},{131,67},{132,68},{133,69},{134,70},{13... | collective-permute-start | bytes 393224 | tf_op jit(solution)/shard_map/ppermute | solution.py:364
  46.1 1.4 collective-permute-start.14
  47.5 1.9 %collective-permute-start.17 = (bf16[256,512]{1,0:T(8,128)(2,1)S(1)}, bf16[256,512]{1,0:T(8,128)(2,1)S(1)}, u32[]{:S(2)}, u32[]{:S(2)}) collective-permute-start(bf16[256,512]{1,0:T(8,128)(2,1)S(1)} %constant_dynamic-update-slice_fusion.6.g0), channel_id=1, source_target_pairs={{68,72},{69,73},{70,74},{71,75},{72,68},{73,69},{74,70},{75,71},{7... | collective-permute-start | bytes 786440 | tf_op jit(solution)/shard_map/ppermute | solution.py:364
  48.2 1.3 collective-permute-start.16
  50.1 42.5 %collective-permute-start.18 = (bf16[128,512]{1,0:T(8,128)(2,1)S(1)}, bf16[128,512]{1,0:T(8,128)(2,1)S(1)}, u32[]{:S(2)}, u32[]{:S(2)}) collective-permute-start(bf16[128,512]{1,0:T(8,128)(2,1)S(1)} %get-tuple-element.80), channel_id=1, source_target_pairs={{64,0},{65,1},{66,2},{67,3},{68,4},{69,5},{70,6},{71,7},{72,8},{73... | collective-permute-start | bytes 393224 | tf_op jit(solution)/shard_map/ppermute | solution.py:364
  51.4 44.0 %collective-permute-start.19 = (bf16[64,512]{1,0:T(8,128)(2,1)S(1)}, bf16[64,512]{1,0:T(8,128)(2,1)S(1)}, u32[]{:S(2)}, u32[]{:S(2)}) collective-permute-start(bf16[64,512]{1,0:T(8,128)(2,1)S(1)} %get-tuple-element.81), channel_id=1, source_target_pairs={{64,1},{65,2},{66,3},{68,5},{69,6},{70,7},{72,9},{73,10},{74,11},{... | collective-permute-start | bytes 196616 | tf_op jit(solution)/shard_map/ppermute | solution.py:364
  52.7 42.7 %collective-permute-start.20 = (bf16[64,512]{1,0:T(8,128)(2,1)S(1)}, bf16[64,512]{1,0:T(8,128)(2,1)S(1)}, u32[]{:S(2)}, u32[]{:S(2)}) collective-permute-start(bf16[64,512]{1,0:T(8,128)(2,1)S(1)} %get-tuple-element.82), channel_id=1, source_target_pairs={{65,0},{66,1},{67,2},{69,4},{70,5},{71,6},{73,8},{74,9},{75,10},{7... | collective-permute-start | bytes 196616 | tf_op jit(solution)/shard_map/ppermute | solution.py:364
  95.4 8.6 %collective-permute-start.22 = (bf16[256,512]{1,0:T(8,128)(2,1)S(1)}, bf16[256,512]{1,0:T(8,128)(2,1)S(1)}, u32[]{:S(2)}, u32[]{:S(2)}) collective-permute-start(bf16[256,512]{1,0:T(8,128)(2,1)S(1)} %constant_dynamic-update-slice_fusion.9.g0), channel_id=1, source_target_pairs={{4,8},{5,9},{6,10},{7,11},{8,4},{9,5},{10,6},{11,7},{12,16},{13,17... | collective-permute-start | bytes 786440 | tf_op jit(solution)/shard_map/ppermute | solution.py:364
  96.1 7.9 %collective-permute-start.21 = (bf16[256,512]{1,0:T(8,128)(2,1)S(1)}, bf16[256,512]{1,0:T(8,128)(2,1)S(1)}, u32[]{:S(2)}, u32[]{:S(2)}) collective-permute-start(bf16[256,512]{1,0:T(8,128)(2,1)S(1)} %constant_dynamic-update-slice_fusion.9.g0), channel_id=1, source_target_pairs={{0,4},{1,5},{2,6},{3,7},{4,0},{5,1},{6,2},{7,3},{8,12},{9,13},{10,... | collective-permute-start | bytes 786440 | tf_op jit(solution)/shard_map/ppermute | solution.py:364
  106.7 2.0 %collective-permute-start.23 = (bf16[128,2048]{1,0:T(8,128)(2,1)S(1)}, bf16[128,2048]{1,0:T(8,128)(2,1)S(1)}, u32[]{:S(2)}, u32[]{:S(2)}) collective-permute-start(bf16[128,2048]{1,0:T(8,128)(2,1)S(1)} %get-tuple-element.85.dp_ref.d0), channel_id=1, source_target_pairs={{0,4},{1,5},{2,6},{3,7},{4,0},{5,1},{6,2},{7,3},{8,12},{9,13},{10,... | collective-permute-start | bytes 1572872 | tf_op jit(solution)/shard_map/ppermute | solution.py:364
  132.7 19.7 %all-to-all-start.1 = ((bf16[8,8,2048]{2,1,0:T(8,128)(2,1)}), bf16[8,8,2048]{2,1,0:T(8,128)(2,1)S(1)}, u32[]{:S(2)}, u32[]{:S(2)}) async-start(bf16[8,8,2048]{2,1,0:T(8,128)(2,1)} %bitcast.9), calls=%async_computation.1 | async-start | bytes 524288 | tf_op jit(solution)/shard_map/all_to_all | solution.py:457
  (8 other events, 43.3 us)

commit v7 on v6

--- a/solution.py
+++ b/solution.py
@@ -91,18 +91,17 @@
     return (x * inverse).astype(BF16)
 
 
-def centre_kernel(where_ref, x_ref, w_ref, wo_ref, cot_ref, proj_ref, nlow_ref, cot_low_ref, dm_ref):
+def centre_kernel(where_ref, x_ref, w_ref, cot_ref, proj_ref, nlow_ref, cot_low_ref):
     low = normed_low(x_ref)
     nlow_ref[...] = low
     proj_ref[...] = nn(low, w_ref[...]).astype(BF16)
-    grad = cot_ref[...].astype(BF16)
-    cot_low_ref[...] = grad
-    dm_ref[...] = nt(grad, wo_ref[...]).astype(BF16)
-
-
-def side_kernel(where_ref, left_ref, right_ref, w_ref, proj_ref):
+    cot_low_ref[...] = cot_ref[...].astype(BF16)
+
+
+def side_kernel(where_ref, left_ref, right_ref, w_ref, wo_ref, cot_ref, proj_ref, dm_ref):
     low = jnp.concatenate([normed_low(left_ref), normed_low(right_ref)], axis=0)
     proj_ref[...] = nn(low, w_ref[...]).astype(BF16)
+    dm_ref[...] = nt(cot_ref[...], wo_ref[...]).astype(BF16)
 
 
 def forward_kernel(
@@ -310,19 +309,30 @@
         in_ref[...] = prev_ref[...]
 
 
-def weight_kernel(where_ref, nt_ref, d0, d1, g_ref, out_ref, full_ref):
+def weight_kernel(where_ref, nt_ref, d0, d1, g_ref, *refs):
+    outs, (left_ref, full_ref) = refs[:-2], refs[-2:]
     d_proj = jnp.concatenate([d0[:, : 3 * D], d1[:, : 3 * D]], axis=0)
     mixed = jnp.concatenate([d0[:, 3 * D :], d1[:, 3 * D :]], axis=0)
     full_ref[...] = tn(mixed, g_ref[...])
-    left, right = nn(nt_ref[...], d_proj), own_half(where_ref, full_ref)
-    cols = out_ref.shape[0]
-    for col in range(cols):
-        for at, part in ((slice(0, 3 * D), left), (slice(3 * D, 4 * D), right)):
+    left_ref[...] = nn(nt_ref[...], d_proj)
+    core, cols = where_ref[2], len(outs)
+    for distance, out_ref in enumerate(outs):
+        col = lax.rem(where_ref[6] + distance, cols)
+        for at, ref, step, first in (
+            (slice(0, 3 * D), left_ref, BLOCK, 0), (slice(3 * D, 4 * D), full_ref, 2 * BLOCK, core)
+        ):
             rows = [
-                part[BLOCK * chip + 8 * col : BLOCK * chip + 8 * col + 8]
-                for chip in range(out_ref.shape[1] // 8)
+                ref[pl.ds(pl.multiple_of(step * chip + first * BLOCK + 8 * col, 8), 8)]
+                for chip in range(out_ref.shape[0] // 8)
             ]
-            out_ref[col, :, at] = jnp.concatenate(rows, axis=0).astype(BF16)
+            out_ref[:, at] = jnp.concatenate(rows, axis=0).astype(BF16)
+
+
+def col_total_kernel(where_ref, *refs):
+    total = refs[0][...].astype(F32)
+    for ref in refs[1:-1]:
+        total = total + ref[...].astype(F32)
+    refs[-1][...] = total.astype(BF16)
 
 
 def total_kernel(where_ref, part_ref, qkv_ref, out_ref, *, scale):
@@ -351,16 +361,12 @@
 
     def routed(block, step, plane=None):
         pairs = []
-        for p in range(pipes):
-            for z in range(chips):
-                for k in range(2):
-                    for c in range(cols):
-                        if plane is not None and p != plane:
-                            continue
-                        p2, r2, c2 = step(p, 2 * z + k, c)
-                        if 0 <= p2 < pipes and 0 <= r2 < 2 * chips and 0 <= c2 < cols:
-                            source = (p * 2 * chips + 2 * z + k) * cols + c
-                            pairs.append((source, (p2 * 2 * chips + r2) * cols + c2))
+        for p in range(pipes) if plane is None else (plane,):
+            for r in range(2 * chips):
+                for c in range(cols):
+                    p2, r2, c2 = step(p, r, c)
+                    target = (p2 * 2 * chips + r2 % (2 * chips)) * cols + c2 % cols
+                    pairs.append(((p * 2 * chips + r) * cols + c, target))
         return lax.ppermute(block, AXES, pairs)
 
     def col_rims(left_half, right_half, down=0, plane=None):
@@ -382,22 +388,23 @@
     cot = cotangent.reshape(TOK, D)
     row_total, col_total = 16 * chips, 16 * cols
     where = jnp.stack(
-        [8 * (2 * z + core), 16 * col, core, row_total, col_total, pipes - 1 - pipe]
+        [8 * (2 * z + core), 16 * col, core, row_total, col_total, pipes - 1 - pipe, col]
     ).astype(jnp.int32)
 
     base, low_side, high_side = call(
         first_kernel, [((OWN, D), BF16), ((64, D), BF16), ((64, D), BF16)], where, x
     )
-    proj, nlow, cot_low, d_mixed = call(
-        centre_kernel, [((TOK, 3 * D), BF16), ((TOK, D), BF16), ((TOK, D), BF16), ((TOK, D), BF16)],
-        where, x, w_qkv, w_out, cot, flops=1 << 28,
+    proj, nlow, cot_low = call(
+        centre_kernel, [((TOK, 3 * D), BF16), ((TOK, D), BF16), ((TOK, D), BF16)],
+        where, x, w_qkv, cot, flops=1 << 28,
     )
     left, right = col_rims(low_side, high_side)
     base, proj = lax.optimization_barrier((base, proj))
     own = lax.dynamic_update_slice(base, left, (TOK, 0))
     own, near, far = row_rims([lax.dynamic_update_slice(own, right, (TOK + 64, 0))])
-    (side_proj,) = call(
-        side_kernel, [((TOK, 3 * D), BF16)], where, left, right, w_qkv, flops=1 << 28
+    side_proj, d_mixed = call(
+        side_kernel, [((TOK, 3 * D), BF16), ((TOK, D), BF16)],
+        where, left, right, w_qkv, w_out, cot_low, flops=1 << 28,
     )
     wide = D + 128
     kv, q_probs, nlow_mate, low_far, mixed, pack, low_side, high_side = call(
@@ -407,12 +414,22 @@
          ((64, wide), BF16)],
         where, near, far, proj, side_proj, w_qkv, cot_low, d_mixed, flops=2 << 30,
     )
-    packs = row_rims([pack, *col_rims(low_side, high_side)])
+    sides = col_rims(low_side, high_side)
     queries, n_turned = call(
         turned_kernel, [((D, REGION), BF16), ((OWN, OWN), BF16)],
         where, proj, side_proj, low_far, w_qkv, nlow, nlow_mate,
         scratch=[pltpu.VMEM((D, OWN), F32)], flops=1 << 28,
     )
+
+    def query_side(turn, gradient):
+        return call(
+            functools.partial(query_kernel, turn=turn), [((TOK, D), BF16)],
+            where, gradient, w_out, mixed, kv, q_probs, flops=1 << 29,
+        )[0]
+
+    d_query = query_side(0, cot_low)
+    pack, queries, d_query = lax.optimization_barrier((pack, queries, d_query))
+    packs = row_rims([pack, *sides])
     k_probs, mixed_turned, delta = call(
         key_probs_kernel,
         [((PAIRS, OWN, REGION), BF16), ((D, REGION), BF16), ((8, REGION), F32)],
@@ -426,10 +443,7 @@
             low, low_side, high_side = sends
             gradient = routed(low, lambda p, r, c: (p - 1, r, c), plane + 1)
             gs = row_rims([gradient, *col_rims(low_side, high_side, 1, plane + 1)], plane)
-        (d_query,) = call(
-            functools.partial(query_kernel, turn=turn), [((TOK, D), BF16)],
-            where, gradient, w_out, mixed, kv, q_probs, flops=1 << 29,
-        )
+            d_query = query_side(turn, gradient)
         outs = [((TOK, 4 * D), BF16), ((OWN, D), BF16)]
         if not last:
             outs += [((TOK, D), F32), ((TOK, D), BF16), ((64, D), BF16), ((64, D), BF16)]
@@ -447,13 +461,16 @@
                 where, d_proj, gradient, w_qkv, x, state[2], flops=1 << 28,
             )
         state, sends = outs[:3], outs[3:]
-    (part,) = call(
-        weight_kernel, [((cols, 8 * chips, 4 * D), BF16)],
+    parts = call(
+        weight_kernel, [((8 * chips, 4 * D), BF16)] * cols,
         where, n_turned, d_proj, routed(d_proj, mate), g_low,
-        scratch=[pltpu.VMEM((D, D), F32)], flops=1 << 29,
-    )
-    part = lax.all_to_all(part, "col", 0, 0, tiled=True)
-    part = jnp.sum(part.astype(F32), axis=0).astype(BF16).reshape(chips, 8, 4 * D)
+        scratch=[pltpu.VMEM((OWN, 3 * D), F32), pltpu.VMEM((D, D), F32)], flops=1 << 29,
+    )
+    parts = list(parts)
+    for distance in sorted(range(1, cols), key=lambda d: -min(d, cols - d)):
+        parts[distance] = routed(parts[distance], lambda p, r, c: (p, r, c + distance))
+    (part,) = call(col_total_kernel, [((8 * chips, 4 * D), BF16)], where, *parts)
+    part = part.reshape(chips, 8, 4 * D)
     part = lax.all_to_all(part, "z", 0, 0, tiled=True)
     qkv_part, out_part = call(
         functools.partial(total_kernel, scale=(row_total * col_total) ** (-0.5)),

time: 155 us -> 144 us (0.929)
  waiting for transfers between devices: 54.7 us -> 80.7 us
  blocking collectives: 20.8 us -> 0 us
  starting transfers between devices: 47.9 us -> 33.6 us
  other arithmetic: 2.15 us -> 0 us
  Pallas kernels: 22.3 us -> 24.1 us
    ppermute x24 -> x27, waiting for transfers between devices: 46 us -> 70.7 us  [routed(): return lax.ppermute(block, AXES, pairs)]
    all_to_all x1 -> x0, blocking collectives: 20.8 us -> none  [body(): part = lax.all_to_all(part, 'col', 0, 0, tiled=True)]
    ppermute x24 -> x27, starting transfers between devices: 38.9 us -> 27.6 us  [routed(): return lax.ppermute(block, AXES, pairs)]
    all_to_all x1, starting transfers between devices: 8.98 us -> 5.93 us  [body(): part = lax.all_to_all(part, 'z', 0, 0, tiled=True)]
    reduce_sum x1 -> x0, other arithmetic: 2.15 us -> none  [body(): jnp.sum(part.astype(F32), axis=0).astype(BF16).reshape(chips, 8, 4 * D)]
    pallas_call x17 -> x18, Pallas kernels: 22.3 us -> 24.1 us  [call(): pl.pallas_call(kernel, out_shape=[jax.ShapeDtypeStruct(s, t) for s, t in...]
  transfers between devices with their start and end apart: 25 -> 28, of which waited for: 7 -> 12; matrix products, arithmetic and copies ran while one was open for 0% -> 0% of each run, Pallas kernels for 6% -> 6%
where the time goes in v7:
time: 144 us; the launch traced here: 143 us
  waiting for transfers between devices  80.7 us (56%)
  starting transfers between devices  33.6 us (23%)
  Pallas kernels  24.1 us (17%)
  local copies, waits for them, and re-layouts  3.5 us (2%)
    ppermute x27, waiting for transfers between devices, routed(): return lax.ppermute(block, AXES, pairs)  70.7 us
    ppermute x27, starting transfers between devices, routed(): return lax.ppermute(block, AXES, pairs)  27.6 us
    pallas_call x18, Pallas kernels, call(): pl.pallas_call(kernel, out_shape=[jax.ShapeDtypeStruct(s, t) for s, t in...  24.1 us
    all_to_all x1, waiting for transfers between devices, body(): part = lax.all_to_all(part, 'z', 0, 0, tiled=True)  10.1 us
    all_to_all x1, starting transfers between devices, body(): part = lax.all_to_all(part, 'z', 0, 0, tiled=True)  5.93 us
    unnamed x22, local copies, waits for them, and re-layouts  3.36 us
  transfers between devices with their start and end apart: 28, of which 12 were waited for; matrix products, arithmetic and copies ran while one was open for 0% of the time, Pallas kernels for 6%

profile of v7, /device:TPU:6, one launch (start us, length us, event | category | flops | bytes accessed | tf_op | source)
XLA Modules:
  0.0 143.1 jit_solution(11936489839607124194)
XLA Ops:
  2.2 2.3 %collective-permute-start = (bf16[64,512]{1,0:T(8,128)(2,1)S(1)}, bf16[64,512]{1,0:T(8,128)(2,1)S(1)}, u32[]{:S(2)}, u32[]{:S(2)}) collective-permute-start(bf16[64,512]{1,0:T(8,128)(2,1)S(1)} %get-tuple-element.58), channel_id=1, source_target_pairs={{0,1},{1,2},{2,3},{3,0},{4,5},{5,6},{6,7},{7,4},{8,9},{9,10},{10,1... | collective-permute-start | bytes 196616 | tf_op jit(solution)/shard_map/ppermute | solution.py:370
  4.5 1.4 copy-done
  7.9 2.1 %collective-permute-done.1.right_ref = bf16[64,512]{1,0:T(8,128)(2,1)S(1)} collective-permute-done((bf16[64,512]{1,0:T(8,128)(2,1)S(1)}, bf16[64,512]{1,0:T(8,128)(2,1)S(1)}, u32[]{:S(2)}, u32[]{:S(2)}) %collective-permute-start.1) | collective-permute-done | bytes 65568 | tf_op jit(solution)/shard_map/ppermute | solution.py:370
  10.0 2.6 %collective-permute-start.3 = (bf16[256,512]{1,0:T(8,128)(2,1)S(1)}, bf16[256,512]{1,0:T(8,128)(2,1)S(1)}, u32[]{:S(2)}, u32[]{:S(2)}) collective-permute-start(bf16[256,512]{1,0:T(8,128)(2,1)S(1)} %constant_dynamic-update-slice_fusion.12), channel_id=1, source_target_pairs={{0,60},{1,61},{2,62},{3,63},{4,8},{5,9},{6,10},{7,11},{8,4},{9,5},... | collective-permute-start | bytes 786440 | tf_op jit(solution)/shard_map/ppermute | solution.py:370
  13.7 3.3 %collective-permute-done.3.x2 = bf16[256,512]{1,0:T(8,128)(2,1)S(1)} collective-permute-done((bf16[256,512]{1,0:T(8,128)(2,1)S(1)}, bf16[256,512]{1,0:T(8,128)(2,1)S(1)}, u32[]{:S(2)}, u32[]{:S(2)}) %collective-permute-start.3) | collective-permute-done | bytes 262176 | tf_op jit(solution)/shard_map/ppermute | solution.py:370
  17.0 4.0 %shard_map.70 = (bf16[768,1024]{1,0:T(8,128)(2,1)S(1)}, bf16[4,256,768]{2,1,0:T(8,128)(2,1)S(1)}, bf16[128,512]{1,0:T(8,128)(2,1)S(1)}, bf16[512,512]{1,0:T(8,12...) custom-call(s32[7]{0:T(128)S(1)} %stack.23.where_ref, ...), custom_call_target="tpu_custom_call" | custom-call | flops 2147483648 | bytes 4194304 | tf_op jit(solution)/shard_map/pallas_call | solution.py:348
  25.5 2.5 %collective-permute-done.5 = bf16[64,640]{1,0:T(8,128)(2,1)S(1)} collective-permute-done((bf16[64,640]{1,0:T(8,128)(2,1)S(1)}, bf16[64,640]{1,0:T(8,128)(2,1)S(1)}, u32[]{:S(2)}, u32[]{:S(2)}) %collective-permute-start.5) | collective-permute-done | bytes 81952 | tf_op jit(solution)/shard_map/ppermute | solution.py:370
  28.0 2.0 %collective-permute-start.7 = (bf16[256,640]{1,0:T(8,128)(2,1)S(1)}, bf16[256,640]{1,0:T(8,128)(2,1)S(1)}, u32[]{:S(2)}, u32[]{:S(2)}) collective-permute-start(bf16[256,640]{1,0:T(8,128)(2,1)S(1)} %constant_dynamic-update-slice_fusion.p0.g0), channel_id=1, source_target_pairs={{0,60},{1,61},{2,62},{3,63},{4,8},{5,9},{6,10},{7,11},{8,4},{9,5},... | collective-permute-start | bytes 983048 | tf_op jit(solution)/shard_map/ppermute | solution.py:370
  30.1 5.8 %collective-permute-done.7.p2.g2 = bf16[256,640]{1,0:T(8,128)(2,1)S(1)} collective-permute-done((bf16[256,640]{1,0:T(8,128)(2,1)S(1)}, bf16[256,640]{1,0:T(8,128)(2,1)S(1)}, u32[]{:S(2)}, u32[]{:S(2)}) %collective-permute-start.7) | collective-permute-done | bytes 327712 | tf_op jit(solution)/shard_map/ppermute | solution.py:370
  35.8 2.1 %shard_map.73 = (bf16[4,256,768]{2,1,0:T(8,128)(2,1)S(1)}, bf16[512,768]{1,0:T(8,128)(2,1)S(1)}, f32[8,768]{1,0:T(8,128)S(1)}) custom-call(s32[7]{0:T(128)S(1)} %stack.23.where_ref, bf16[256,640]{1,0:T(8,128)(2,1)S(1)} %constant_dynamic-update-slice_fusion.p0.g0, bf16[256,640]{1,0:T(8,128)(2,1)S(1)} %collective-permute-done.6.p1.g1, ...), custom_call_target="tpu_custom_call" | custom-call | flops 268435456 | bytes 4194304 | tf_op jit(solution)/shard_map/pallas_call | solution.py:348
  51.8 39.9 %collective-permute-done.18.g_ref = bf16[128,512]{1,0:T(8,128)(2,1)S(1)} collective-permute-done((bf16[128,512]{1,0:T(8,128)(2,1)S(1)}, bf16[128,512]{1,0:T(8,128)(2,1)S(1)}, u32[]{:S(2)}, u32[]{:S(2)}) %collective-permute-start.18) | collective-permute-done | bytes 131104 | tf_op jit(solution)/shard_map/ppermute | solution.py:370
  91.8 3.4 %collective-permute-start.22 = (bf16[256,512]{1,0:T(8,128)(2,1)S(1)}, bf16[256,512]{1,0:T(8,128)(2,1)S(1)}, u32[]{:S(2)}, u32[]{:S(2)}) collective-permute-start(bf16[256,512]{1,0:T(8,128)(2,1)S(1)} %constant_dynamic-update-slice_fusion.9.g0), channel_id=1, source_target_pairs={{0,60},{1,61},{2,62},{3,63},{4,8},{5,9},{6,10},{7,11},{8,4},{9,5},... | collective-permute-start | bytes 786440 | tf_op jit(solution)/shard_map/ppermute | solution.py:370
  95.2 1.9 %collective-permute-start.21 = (bf16[256,512]{1,0:T(8,128)(2,1)S(1)}, bf16[256,512]{1,0:T(8,128)(2,1)S(1)}, u32[]{:S(2)}, u32[]{:S(2)}) collective-permute-start(bf16[256,512]{1,0:T(8,128)(2,1)S(1)} %constant_dynamic-update-slice_fusion.9.g0), channel_id=1, source_target_pairs={{0,4},{1,5},{2,6},{3,7},{4,0},{5,1},{6,2},{7,3},{8,12},{9,13},{10,... | collective-permute-start | bytes 786440 | tf_op jit(solution)/shard_map/ppermute | solution.py:370
  97.1 2.2 %shard_map.79.dq_ref = bf16[128,512]{1,0:T(8,128)(2,1)S(1)} custom-call(s32[7]{0:T(128)S(1)} %stack.23.where_ref, bf16[128,512]{1,0:T(8,128)(2,1)S(1)} %collective-permute-done.18.g_ref, bf16[512,512]{1,0:T(8,128)(2,1)S(1)} %bitcast.28, bf16[128,512]{1,0:T(8,128)(2,1)S(1)} %get-tuple-element.69.mixed_ref, bf16[768,1024]{1,0:T(8,128)(2,1)S(1)} %get-tuple-element.70.kv_ref, ...), custom_call_target="tpu_custom_call" | custom-call | flops 536870912 | bytes 4194304 | tf_op jit(solution)/shard_map/pallas_call | solution.py:348
  100.7 2.7 %shard_map.80 = (bf16[128,2048]{1,0:T(8,128)(2,1)S(1)}, bf16[256,512]{1,0:T(8,128)(2,1)S(1)}) custom-call(s32[7]{0:T(128)S(1)} %stack.23.where_ref, bf16[256,512]{1,0:T(8,128)(2,1)S(1)} %constant_dynamic-update-slice_fusion.9.g0, bf16[256,512]{1,0:T(8,128)(2,1)S(1)} %collective-permute-done.21.g1, bf16[256,512]{1,0:T(8,128)(2,1)S(1)} %collective-permute-done.22.g2, ...), custom_call_target="tpu_custom_call" | custom-call | flops 1073741824 | bytes 4194304 | tf_op jit(solution)/shard_map/pallas_call | solution.py:348
  103.5 1.9 %collective-permute-done.23.d1 = bf16[128,2048]{1,0:T(8,128)(2,1)S(1)} collective-permute-done((bf16[128,2048]{1,0:T(8,128)(2,1)S(1)}, bf16[128,2048]{1,0:T(8,128)(2,1)S(1)}, u32[]{:S(2)}, u32[]{:S(2)}) %collective-permute-start.23) | collective-permute-done | bytes 524320 | tf_op jit(solution)/shard_map/ppermute | solution.py:370
  107.3 2.0 %collective-permute-start.25 = (bf16[64,2048]{1,0:T(8,128)(2,1)S(1)}, bf16[64,2048]{1,0:T(8,128)(2,1)S(1)}, u32[]{:S(2)}, u32[]{:S(2)}) collective-permute-start(bf16[64,2048]{1,0:T(8,128)(2,1)S(1)} %get-tuple-element.103), channel_id=1, source_target_pairs={{0,2},{1,3},{2,0},{3,1},{4,6},{5,7},{6,4},{7,5},{8,10},{9,11},{10,... | collective-permute-start | bytes 786440 | tf_op jit(solution)/shard_map/ppermute | solution.py:370
  109.3 6.6 %collective-permute-done.24.refs_1_ = bf16[64,2048]{1,0:T(8,128)(2,1)S(1)} collective-permute-done((bf16[64,2048]{1,0:T(8,128)(2,1)S(1)}, bf16[64,2048]{1,0:T(8,128)(2,1)S(1)}, u32[]{:S(2)}, u32[]{:S(2)}) %collective-permute-start.24) | collective-permute-done | bytes 262176 | tf_op jit(solution)/shard_map/ppermute | solution.py:370
  115.9 2.2 %collective-permute-done.25.refs_2_ = bf16[64,2048]{1,0:T(8,128)(2,1)S(1)} collective-permute-done((bf16[64,2048]{1,0:T(8,128)(2,1)S(1)}, bf16[64,2048]{1,0:T(8,128)(2,1)S(1)}, u32[]{:S(2)}, u32[]{:S(2)}) %collective-permute-start.25) | collective-permute-done | bytes 262176 | tf_op jit(solution)/shard_map/ppermute | solution.py:370
  118.0 4.4 %collective-permute-done.26.refs_3_ = bf16[64,2048]{1,0:T(8,128)(2,1)S(1)} collective-permute-done((bf16[64,2048]{1,0:T(8,128)(2,1)S(1)}, bf16[64,2048]{1,0:T(8,128)(2,1)S(1)}, u32[]{:S(2)}, u32[]{:S(2)}) %collective-permute-start.26) | collective-permute-done | bytes 262176 | tf_op jit(solution)/shard_map/ppermute | solution.py:370
  122.5 1.4 shard_map.83
  123.9 5.9 %all-to-all-start = ((bf16[8,8,2048]{2,1,0:T(8,128)(2,1)}), bf16[8,8,2048]{2,1,0:T(8,128)(2,1)S(1)}, u32[]{:S(2)}, u32[]{:S(2)}) async-start(bf16[8,8,2048]{2,1,0:T(8,128)(2,1)} %bitcast.10), calls=%async_computation | async-start | bytes 524288 | tf_op jit(solution)/shard_map/all_to_all | solution.py:474
  129.8 2.0 %shard_map.81 = f32[128,512]{1,0:T(8,128)} custom-call(s32[7]{0:T(128)S(1)} %stack.23.where_ref, bf16[128,2048]{1,0:T(8,128)(2,1)S(1)} %get-tuple-element.97.dp_ref.d0, bf16[128,512]{1,0:T(8,128)(2,1)S(1)} %collective-permute-done.18.g_ref, bf16[512,1536]{1,0:T(8,128)(2,1)S(1)} %bitcast.20, bf16[128,512]{1,0:T(8,128)(2,1)S(1)} %bitcast.35, ...), custom_call_target="tpu_custom_call" | custom-call | flops 268435456 | bytes 4194304 | tf_op jit(solution)/shard_map/pallas_call | solution.py:348
  131.8 10.1 %all-to-all-done.part_ref = bf16[8,8,2048]{2,1,0:T(8,128)(2,1)S(1)} async-done(((bf16[8,8,2048]{2,1,0:T(8,128)(2,1)}), bf16[8,8,2048]{2,1,0:T(8,128)(2,1)S(1)}, u32[]{:S(2)}, u32[]{:S(2)}) %all-to-all-start) | async-done | bytes 262176 | tf_op jit(solution)/shard_map/all_to_all | solution.py:474
  (79 shorter events, 27.3 us)
Async XLA Ops:
  2.2 5.7 %collective-permute-start = (bf16[64,512]{1,0:T(8,128)(2,1)S(1)}, bf16[64,512]{1,0:T(8,128)(2,1)S(1)}, u32[]{:S(2)}, u32[]{:S(2)}) collective-permute-start(bf16[64,512]{1,0:T(8,128)(2,1)S(1)} %get-tuple-element.58), channel_id=1, source_target_pairs={{0,1},{1,2},{2,3},{3,0},{4,5},{5,6},{6,7},{7,4},{8,9},{9,10},{10,1... | collective-permute-start | bytes 196616 | tf_op jit(solution)/shard_map/ppermute | solution.py:370
  4.5 5.5 %collective-permute-start.1 = (bf16[64,512]{1,0:T(8,128)(2,1)S(1)}, bf16[64,512]{1,0:T(8,128)(2,1)S(1)}, u32[]{:S(2)}, u32[]{:S(2)}) collective-permute-start(bf16[64,512]{1,0:T(8,128)(2,1)S(1)} %get-tuple-element.59), channel_id=1, source_target_pairs={{0,3},{1,0},{2,1},{3,2},{4,7},{5,4},{6,5},{7,6},{8,11},{9,8},{10,9... | collective-permute-start | bytes 196616 | tf_op jit(solution)/shard_map/ppermute | solution.py:370
  10.0 7.0 %collective-permute-start.3 = (bf16[256,512]{1,0:T(8,128)(2,1)S(1)}, bf16[256,512]{1,0:T(8,128)(2,1)S(1)}, u32[]{:S(2)}, u32[]{:S(2)}) collective-permute-start(bf16[256,512]{1,0:T(8,128)(2,1)S(1)} %constant_dynamic-update-slice_fusion.12), channel_id=1, source_target_pairs={{0,60},{1,61},{2,62},{3,63},{4,8},{5,9},{6,10},{7,11},{8,4},{9,5},... | collective-permute-start | bytes 786440 | tf_op jit(solution)/shard_map/ppermute | solution.py:370
  12.5 4.5 %collective-permute-start.2 = (bf16[256,512]{1,0:T(8,128)(2,1)S(1)}, bf16[256,512]{1,0:T(8,128)(2,1)S(1)}, u32[]{:S(2)}, u32[]{:S(2)}) collective-permute-start(bf16[256,512]{1,0:T(8,128)(2,1)S(1)} %constant_dynamic-update-slice_fusion.12), channel_id=1, source_target_pairs={{0,4},{1,5},{2,6},{3,7},{4,0},{5,1},{6,2},{7,3},{8,12},{9,13},{10,... | collective-permute-start | bytes 786440 | tf_op jit(solution)/shard_map/ppermute | solution.py:370
  21.0 4.5 %collective-permute-start.4 = (bf16[64,640]{1,0:T(8,128)(2,1)S(1)}, bf16[64,640]{1,0:T(8,128)(2,1)S(1)}, u32[]{:S(2)}, u32[]{:S(2)}) collective-permute-start(bf16[64,640]{1,0:T(8,128)(2,1)S(1)} %get-tuple-element.73), channel_id=1, source_target_pairs={{0,1},{1,2},{2,3},{3,0},{4,5},{5,6},{6,7},{7,4},{8,9},{9,10},{10,1... | collective-permute-start | bytes 245768 | tf_op jit(solution)/shard_map/ppermute | solution.py:370
  22.4 5.7 %collective-permute-start.5 = (bf16[64,640]{1,0:T(8,128)(2,1)S(1)}, bf16[64,640]{1,0:T(8,128)(2,1)S(1)}, u32[]{:S(2)}, u32[]{:S(2)}) collective-permute-start(bf16[64,640]{1,0:T(8,128)(2,1)S(1)} %get-tuple-element.74), channel_id=1, source_target_pairs={{0,3},{1,0},{2,1},{3,2},{4,7},{5,4},{6,5},{7,6},{8,11},{9,8},{10,9... | collective-permute-start | bytes 245768 | tf_op jit(solution)/shard_map/ppermute | solution.py:370
  28.0 7.8 %collective-permute-start.7 = (bf16[256,640]{1,0:T(8,128)(2,1)S(1)}, bf16[256,640]{1,0:T(8,128)(2,1)S(1)}, u32[]{:S(2)}, u32[]{:S(2)}) collective-permute-start(bf16[256,640]{1,0:T(8,128)(2,1)S(1)} %constant_dynamic-update-slice_fusion.p0.g0), channel_id=1, source_target_pairs={{0,60},{1,61},{2,62},{3,63},{4,8},{5,9},{6,10},{7,11},{8,4},{9,5},... | collective-permute-start | bytes 983048 | tf_op jit(solution)/shard_map/ppermute | solution.py:370
  30.1 5.8 %collective-permute-start.6 = (bf16[256,640]{1,0:T(8,128)(2,1)S(1)}, bf16[256,640]{1,0:T(8,128)(2,1)S(1)}, u32[]{:S(2)}, u32[]{:S(2)}) collective-permute-start(bf16[256,640]{1,0:T(8,128)(2,1)S(1)} %constant_dynamic-update-slice_fusion.p0.g0), channel_id=1, source_target_pairs={{0,4},{1,5},{2,6},{3,7},{4,0},{5,1},{6,2},{7,3},{8,12},{9,13},{10,... | collective-permute-start | bytes 983048 | tf_op jit(solution)/shard_map/ppermute | solution.py:370
  38.5 2.0 %collective-permute-start.8 = (bf16[128,512]{1,0:T(8,128)(2,1)S(1)}, bf16[128,512]{1,0:T(8,128)(2,1)S(1)}, u32[]{:S(2)}, u32[]{:S(2)}) collective-permute-start(bf16[128,512]{1,0:T(8,128)(2,1)S(1)} %get-tuple-element.79), channel_id=1, source_target_pairs={{192,128},{193,129},{194,130},{195,131},{196,132},{197,133},{198,1... | collective-permute-start | bytes 393224 | tf_op jit(solution)/shard_map/ppermute | solution.py:370
  39.2 1.4 collective-permute-start.9
  40.6 1.9 %collective-permute-start.12 = (bf16[256,512]{1,0:T(8,128)(2,1)S(1)}, bf16[256,512]{1,0:T(8,128)(2,1)S(1)}, u32[]{:S(2)}, u32[]{:S(2)}) collective-permute-start(bf16[256,512]{1,0:T(8,128)(2,1)S(1)} %constant_dynamic-update-slice_fusion.3.g0), channel_id=1, source_target_pairs={{128,188},{129,189},{130,190},{131,191},{132,136},{133,137},{134,1... | collective-permute-start | bytes 786440 | tf_op jit(solution)/shard_map/ppermute | solution.py:370
  43.2 2.0 %collective-permute-start.13 = (bf16[128,512]{1,0:T(8,128)(2,1)S(1)}, bf16[128,512]{1,0:T(8,128)(2,1)S(1)}, u32[]{:S(2)}, u32[]{:S(2)}) collective-permute-start(bf16[128,512]{1,0:T(8,128)(2,1)S(1)} %get-tuple-element.86), channel_id=1, source_target_pairs={{128,64},{129,65},{130,66},{131,67},{132,68},{133,69},{134,70},{13... | collective-permute-start | bytes 393224 | tf_op jit(solution)/shard_map/ppermute | solution.py:370
  43.9 1.4 collective-permute-start.14
  45.3 1.9 %collective-permute-start.17 = (bf16[256,512]{1,0:T(8,128)(2,1)S(1)}, bf16[256,512]{1,0:T(8,128)(2,1)S(1)}, u32[]{:S(2)}, u32[]{:S(2)}) collective-permute-start(bf16[256,512]{1,0:T(8,128)(2,1)S(1)} %constant_dynamic-update-slice_fusion.6.g0), channel_id=1, source_target_pairs={{64,124},{65,125},{66,126},{67,127},{68,72},{69,73},{70,74},{71,75... | collective-permute-start | bytes 786440 | tf_op jit(solution)/shard_map/ppermute | solution.py:370
  47.9 43.8 %collective-permute-start.18 = (bf16[128,512]{1,0:T(8,128)(2,1)S(1)}, bf16[128,512]{1,0:T(8,128)(2,1)S(1)}, u32[]{:S(2)}, u32[]{:S(2)}) collective-permute-start(bf16[128,512]{1,0:T(8,128)(2,1)S(1)} %get-tuple-element.92), channel_id=1, source_target_pairs={{64,0},{65,1},{66,2},{67,3},{68,4},{69,5},{70,6},{71,7},{72,8},{73... | collective-permute-start | bytes 393224 | tf_op jit(solution)/shard_map/ppermute | solution.py:370
  49.2 42.5 %collective-permute-start.19 = (bf16[64,512]{1,0:T(8,128)(2,1)S(1)}, bf16[64,512]{1,0:T(8,128)(2,1)S(1)}, u32[]{:S(2)}, u32[]{:S(2)}) collective-permute-start(bf16[64,512]{1,0:T(8,128)(2,1)S(1)} %get-tuple-element.93), channel_id=1, source_target_pairs={{64,1},{65,2},{66,3},{67,0},{68,5},{69,6},{70,7},{71,4},{72,9},{73... | collective-permute-start | bytes 196616 | tf_op jit(solution)/shard_map/ppermute | solution.py:370
  50.5 41.2 %collective-permute-start.20 = (bf16[64,512]{1,0:T(8,128)(2,1)S(1)}, bf16[64,512]{1,0:T(8,128)(2,1)S(1)}, u32[]{:S(2)}, u32[]{:S(2)}) collective-permute-start(bf16[64,512]{1,0:T(8,128)(2,1)S(1)} %get-tuple-element.94), channel_id=1, source_target_pairs={{64,3},{65,0},{66,1},{67,2},{68,7},{69,4},{70,5},{71,6},{72,11},{7... | collective-permute-start | bytes 196616 | tf_op jit(solution)/shard_map/ppermute | solution.py:370
  91.8 8.9 %collective-permute-start.22 = (bf16[256,512]{1,0:T(8,128)(2,1)S(1)}, bf16[256,512]{1,0:T(8,128)(2,1)S(1)}, u32[]{:S(2)}, u32[]{:S(2)}) collective-permute-start(bf16[256,512]{1,0:T(8,128)(2,1)S(1)} %constant_dynamic-update-slice_fusion.9.g0), channel_id=1, source_target_pairs={{0,60},{1,61},{2,62},{3,63},{4,8},{5,9},{6,10},{7,11},{8,4},{9,5},... | collective-permute-start | bytes 786440 | tf_op jit(solution)/shard_map/ppermute | solution.py:370
  95.2 5.5 %collective-permute-start.21 = (bf16[256,512]{1,0:T(8,128)(2,1)S(1)}, bf16[256,512]{1,0:T(8,128)(2,1)S(1)}, u32[]{:S(2)}, u32[]{:S(2)}) collective-permute-start(bf16[256,512]{1,0:T(8,128)(2,1)S(1)} %constant_dynamic-update-slice_fusion.9.g0), channel_id=1, source_target_pairs={{0,4},{1,5},{2,6},{3,7},{4,0},{5,1},{6,2},{7,3},{8,12},{9,13},{10,... | collective-permute-start | bytes 786440 | tf_op jit(solution)/shard_map/ppermute | solution.py:370
  103.4 2.0 %collective-permute-start.23 = (bf16[128,2048]{1,0:T(8,128)(2,1)S(1)}, bf16[128,2048]{1,0:T(8,128)(2,1)S(1)}, u32[]{:S(2)}, u32[]{:S(2)}) collective-permute-start(bf16[128,2048]{1,0:T(8,128)(2,1)S(1)} %get-tuple-element.97.dp_ref.d0), channel_id=1, source_target_pairs={{0,4},{1,5},{2,6},{3,7},{4,0},{5,1},{6,2},{7,3},{8,12},{9,13},{10,... | collective-permute-start | bytes 1572872 | tf_op jit(solution)/shard_map/ppermute | solution.py:370
  106.6 9.2 %collective-permute-start.24 = (bf16[64,2048]{1,0:T(8,128)(2,1)S(1)}, bf16[64,2048]{1,0:T(8,128)(2,1)S(1)}, u32[]{:S(2)}, u32[]{:S(2)}) collective-permute-start(bf16[64,2048]{1,0:T(8,128)(2,1)S(1)} %get-tuple-element.102), channel_id=1, source_target_pairs={{0,1},{1,2},{2,3},{3,0},{4,5},{5,6},{6,7},{7,4},{8,9},{9,10},{10,1... | collective-permute-start | bytes 786440 | tf_op jit(solution)/shard_map/ppermute | solution.py:370
  107.3 10.7 %collective-permute-start.25 = (bf16[64,2048]{1,0:T(8,128)(2,1)S(1)}, bf16[64,2048]{1,0:T(8,128)(2,1)S(1)}, u32[]{:S(2)}, u32[]{:S(2)}) collective-permute-start(bf16[64,2048]{1,0:T(8,128)(2,1)S(1)} %get-tuple-element.103), channel_id=1, source_target_pairs={{0,2},{1,3},{2,0},{3,1},{4,6},{5,7},{6,4},{7,5},{8,10},{9,11},{10,... | collective-permute-start | bytes 786440 | tf_op jit(solution)/shard_map/ppermute | solution.py:370
  109.3 13.2 %collective-permute-start.26 = (bf16[64,2048]{1,0:T(8,128)(2,1)S(1)}, bf16[64,2048]{1,0:T(8,128)(2,1)S(1)}, u32[]{:S(2)}, u32[]{:S(2)}) collective-permute-start(bf16[64,2048]{1,0:T(8,128)(2,1)S(1)} %get-tuple-element.104), channel_id=1, source_target_pairs={{0,3},{1,0},{2,1},{3,2},{4,7},{5,4},{6,5},{7,6},{8,11},{9,8},{10,9... | collective-permute-start | bytes 786440 | tf_op jit(solution)/shard_map/ppermute | solution.py:370
  123.9 18.0 %all-to-all-start = ((bf16[8,8,2048]{2,1,0:T(8,128)(2,1)}), bf16[8,8,2048]{2,1,0:T(8,128)(2,1)S(1)}, u32[]{:S(2)}, u32[]{:S(2)}) async-start(bf16[8,8,2048]{2,1,0:T(8,128)(2,1)} %bitcast.10), calls=%async_computation | async-start | bytes 524288 | tf_op jit(solution)/shard_map/all_to_all | solution.py:474
  (11 other events, 45.0 us)
